TPU v7x, 256 devices: a whole 4x4x8 slice. The times are simulated.
256 devices in a mesh: sample: 64 (over y, x, z_lo, core), tensor: 4 (over z_hi).
Axes of the slice: x: 4, y: 4, z: 8 (z_hi: 4, z_lo: 2; z = z_hi * 2 + z_lo), core: 2. Of those that a mesh axis runs over, the one named last changes fastest.
Arguments:
- prompt_q: bfloat16 [8192, 4096], P('sample', 'tensor'), may hold values from -70 to 70
- prompt_k: bfloat16 [8192, 512], P('sample', 'tensor'), may hold values from -4 to 4
- prompt_v: bfloat16 [8192, 512], P('sample', 'tensor'), may hold values from -6 to 6
- suffix_q: bfloat16 [8192, 4096], P('sample', 'tensor'), may hold values from -70 to 70
- suffix_k: bfloat16 [8192, 512], P('sample', 'tensor'), may hold values from -4 to 4
- suffix_v: bfloat16 [8192, 512], P('sample', 'tensor'), may hold values from -6 to 6
- prompt_of: int32 [64], P('sample'), may hold values from 0 to 1
- suffix_len: int32 [64], P('sample'), may hold values from 1 to 128, 5120 in all
- out_weight: bfloat16 [4096, 8192], P('sample', 'tensor'), may hold values from -0.375 to 0.375
Outputs:
- prompt_out: bfloat16 [8192, 8192], P('sample', 'tensor')
- suffix_out: bfloat16 [8192, 8192], P('sample', 'tensor')
Inputs may be any that keep to these rules, and one draw needn't show every extreme that they name: `suffix_len`: some suffix is exactly 128 long.
All inputs are finite; a program needn't handle non-finite values. No bound on the sum of `suffix_len` on one device may be relied on, other than what follows from the above.
Results may differ from a plain program's by a relative error of at most 0.0095.
Values may be sent and summed in bfloat16 or wider, within the bound.
No kernel may reach another device: no remote copies, remote signals or barrier semaphores. Data moves between devices by JAX's collectives and lax.ppermute only.
A program may use at most 64 MiB of HBM per device.

v0:
```python
import functools

import jax
import jax.numpy as jnp
from jax import lax
from jax.experimental import pallas as pl
from jax.experimental.pallas import tpu as pltpu
from jax.sharding import PartitionSpec as P

HD = 128
HEADS = 8
GROUP = 4
ROWS = 128
SCALE = HD ** (-0.5) * 1.4426950408889634
ORDERS = (((4, 12, 16, 48), (12, 4, 48, 16)), ((16, 48, 4, 12), (48, 16, 12, 4)))
VMEM = pl.BlockSpec(memory_space=pltpu.VMEM)
SMEM = pl.BlockSpec(memory_space=pltpu.SMEM)


def slot_table(me):
    there = jnp.arange(16, dtype=jnp.int32)
    apart = there ^ (me >> 2)
    low_x, high_x = apart & 1, (apart >> 1) & 1
    low_y, high_y = (apart >> 2) & 1, (apart >> 3) & 1
    used = {4: low_x ^ high_x, 12: high_x, 16: low_y ^ high_y, 48: high_y}
    rows = []
    for rc in range(2):
        for piece in range(2):
            first, second = [
                sum(used[mask] << step for step, mask in enumerate(order))
                for order in ORDERS[piece]]
            rows.append(jnp.where((me & 1) == rc, first, second))
    return jnp.concatenate(rows)


def slot_of(info, rc, piece, there):
    return info[4 + (rc * 2 + piece) * 16 + there]


def take(halves, slot):
    low = slot & 7
    return jnp.where(slot > 7, halves[1][low], halves[0][low])


def swap(x, masks):
    masks = masks if isinstance(masks, tuple) else (masks, masks)
    return lax.ppermute(x, "sample", [(s, s ^ masks[s & 1]) for s in range(64)])


def swap_tensor(x, masks):
    pairs = [(s * 4 + t, s * 4 + (t ^ masks[s & 1])) for s in range(64) for t in range(4)]
    return lax.ppermute(x, ("sample", "tensor"), pairs)


def after(x, *others):
    return lax.optimization_barrier((x, *others))[0]


def step_masks(piece, step):
    return (ORDERS[piece][0][step], ORDERS[piece][1][step])


def gather_step(pieces, step):
    return [swap(piece, step_masks(i, step)) for i, piece in enumerate(pieces)]


def join(pieces, came):
    return [jnp.concatenate([a, b], axis=0) for a, b in zip(pieces, came)]


def score_head(q, h, keys):
    return lax.dot_general(
        q[:, h * HD:(h + 1) * HD], keys, (((1,), (1,)), ((), ())),
        preferred_element_type=jnp.float32)


def add_values(acc, h, exps, shrink, values):
    acc[h] = acc[h] * jnp.concatenate([shrink, shrink], axis=1) + jnp.dot(
        exps, values, preferred_element_type=jnp.float32)


def attend_kernel(is_prompt, first, info, q, own_k, own_v, *refs):
    blocks, (out, top, acc) = refs[:8], refs[8:]
    me = info[0]
    core, low_z = me & 1, (me >> 1) & 1
    row = lax.broadcasted_iota(jnp.int32, (ROWS, ROWS), 0)
    col = lax.broadcasted_iota(jnp.int32, (ROWS, ROWS), 1)
    keys = own_k[...]
    values = jnp.concatenate([own_v[...], jnp.ones((ROWS, HD), jnp.bfloat16)], axis=1)
    scores = [
        jnp.where(row >= col, score_head(q, first + h, keys), -1e30) for h in range(GROUP)]
    best = [
        jnp.broadcast_to(jnp.max(part, axis=1, keepdims=True), (ROWS, HD)) for part in scores]
    exps = [
        jnp.exp2((part - high) * SCALE).astype(jnp.bfloat16) for part, high in zip(scores, best)]
    for h in range(GROUP):
        top[h] = best[h]
        acc[h] = jnp.dot(exps[h], values, preferred_element_type=jnp.float32)

    def absorb(pair, masked):
        begin = 8 * (me >> 5 if is_prompt else info[1]) + 2 * pair
        keys, values, allowed = [], [], []
        for there in (begin, begin + 1):
            for rc in range(2):
                for rz in range(2):
                    slot = slot_of(info, rc, rz, there)
                    both = take(blocks[rc * 4 + rz * 2:rc * 4 + rz * 2 + 2], slot)
                    keys.append(both[:, :HD])
                    values.append(both[:, HD:])
                    allowed.append(there * 4 + ((me ^ (rz * 2 + rc)) & 3) < me)
        keys = jnp.concatenate(keys, axis=0)
        values = jnp.concatenate(values, axis=0)
        values = jnp.concatenate([values, jnp.ones(values.shape, jnp.bfloat16)], axis=1)
        ahead = score_head(q, first, keys)
        behind = None
        for h in range(GROUP):
            scores = ahead
            if h + 1 < GROUP:
                ahead = score_head(q, first + h + 1, keys)
            parts = [scores[:, i * ROWS:(i + 1) * ROWS] for i in range(8)]
            if masked:
                parts = [jnp.where(ok, part, -1e30) for ok, part in zip(allowed, parts)]
            best = functools.reduce(jnp.maximum, parts)
            old = top[h]
            new = jnp.maximum(old, jnp.max(best, axis=1, keepdims=True))
            shrink = jnp.exp2((old - new) * SCALE)
            top[h] = new
            exps = jnp.concatenate(
                [jnp.exp2((part - new) * SCALE).astype(jnp.bfloat16) for part in parts], axis=1)
            if behind is not None:
                add_values(acc, h - 1, *behind, values)
            behind = exps, shrink
        add_values(acc, GROUP - 1, *behind, values)

    whole = (me & 31) >> 3 if is_prompt else 4
    lax.fori_loop(0, whole, lambda i, c: (absorb(i, False), c)[1], 0)
    if is_prompt:
        @pl.when((me & 7) > 0)
        def _():
            absorb(whole, True)
    for h in range(GROUP):
        result = acc[h][:, :HD] / acc[h][:, HD:]
        if not is_prompt:
            result = jnp.where(row < info[2], result, 0.0)
        result = jnp.where(core == 0, result, pltpu.roll(result, HD // 2, 1))
        place = pl.multiple_of((h ^ low_z) * HD, HD)
        out[:, pl.ds(place, HD)] = result.astype(jnp.bfloat16)


def attend(is_prompt, first, info, q, own_k, own_v, blocks):
    return pl.pallas_call(
        functools.partial(attend_kernel, is_prompt, first),
        out_shape=jax.ShapeDtypeStruct((ROWS, GROUP * HD), jnp.bfloat16),
        in_specs=[SMEM] + [VMEM] * (3 + len(blocks)),
        out_specs=VMEM,
        scratch_shapes=[
            pltpu.VMEM((GROUP, ROWS, HD), jnp.float32),
            pltpu.VMEM((GROUP, ROWS, 2 * HD), jnp.float32),
        ],
        compiler_params=pltpu.CompilerParams(vmem_limit_bytes=24 << 20),
        cost_estimate=pl.CostEstimate(
            flops=4 * GROUP * ROWS * 4224 * HD, transcendentals=GROUP * ROWS * 4224,
            bytes_accessed=4 << 20),
        name="attend_%s_%d" % ("prompt" if is_prompt else "suffix", first),
    )(info, q, own_k, own_v, *blocks)


def project_kernel(last, info, *refs):
    if last:
        heads, total_in, weights, (out_p, out_s) = refs[:4], refs[4], refs[5:13], refs[13:]
    else:
        heads, weights, total_out = refs[:8], refs[8:16], refs[16]
    core, tensor = info[0] & 1, info[3]
    near = jnp.where(core == 0, 1, 3)
    if last:
        pieces = [(tensor ^ near ^ 2, [ref[0] for ref in heads]),
                  (tensor ^ 2, [ref[1] for ref in heads])]
    else:
        pieces = [(tensor, [ref[...] for ref in heads[:4]]),
                  (tensor ^ near, [ref[...] for ref in heads[4:]])]
    for piece in range(2):
        lanes = slice(piece * 1024, (piece + 1) * 1024)
        total = total_in[:, lanes] if last else None
        for quarter, rows in pieces:
            rows = jnp.concatenate([
                jnp.concatenate(rows[:2], axis=1), jnp.concatenate(rows[2:], axis=1)], axis=0)
            held = []
            for x in range(4):
                there = quarter * 4 + x
                found = [
                    take(weights[rc * 4 + piece * 2:rc * 4 + piece * 2 + 2],
                         slot_of(info, rc, piece, there)) for rc in range(2)]
                for rz in range(2):
                    held += [found[0][rz], found[1][rz]]
            part = jnp.dot(
                rows, jnp.concatenate(held, axis=0), preferred_element_type=jnp.float32)
            total = part if total is None else total + part
        if last:
            out_p[:, lanes] = total[:ROWS].astype(jnp.bfloat16)
            out_s[:, lanes] = total[ROWS:].astype(jnp.bfloat16)
        else:
            total_out[:, lanes] = total


def project(last, info, heads, weights, total):
    if last:
        out_shape = [jax.ShapeDtypeStruct((ROWS, 2048), jnp.bfloat16)] * 2
    else:
        out_shape = jax.ShapeDtypeStruct((2 * ROWS, 2048), jnp.float32)
    args = [info, *heads] + ([total] if last else []) + list(weights)
    return pl.pallas_call(
        functools.partial(project_kernel, last),
        out_shape=out_shape,
        in_specs=[SMEM] + [VMEM] * (len(args) - 1),
        out_specs=[VMEM] * 2 if last else VMEM,
        compiler_params=pltpu.CompilerParams(vmem_limit_bytes=32 << 20),
        name="project_last" if last else "project_first",
    )(*args)


def per_device(
    prompt_q, prompt_k, prompt_v, suffix_q, suffix_k, suffix_v, prompt_of, suffix_len, out_weight
):
    me = lax.axis_index("sample").astype(jnp.int32)
    info = jnp.concatenate([
        jnp.stack([me, prompt_of[0], suffix_len[0], lax.axis_index("tensor").astype(jnp.int32)]),
        slot_table(me)])

    both = jnp.concatenate([prompt_k, prompt_v], axis=1)
    kv = [both[None], swap(both, 2)[None]]
    others = swap(out_weight, 2)
    kv = join(kv, gather_step(kv, 0))
    others = after(others, *kv)
    w = [jnp.stack([part[:, lanes] for part in (out_weight, others)])[None]
         for lanes in (slice(0, 1024), slice(1024, 2048))]
    w_came = gather_step(w, 0)
    kv = join(kv, gather_step(kv, 1))
    kv = join(kv, gather_step(kv, 2))
    w = join(w, [after(a, *kv) for a in w_came])
    came = gather_step([after(a, *w) for a in kv], 3)
    kv_mate = [swap(a, 1) for a in kv]
    w_came = gather_step([after(a, *came) for a in w], 1)
    came_mate = [swap(a, 1) for a in came]
    blocks = [kv[0], came[0], kv[1], came[1],
              kv_mate[0], came_mate[0], kv_mate[1], came_mate[1]]

    def attend_suffix(first, q):
        return attend(False, first, info, q, suffix_k, suffix_v, blocks)

    def attend_prompt(first, q):
        return attend(True, first, info, q, prompt_k, prompt_v, blocks)

    def to_near(a):
        return swap_tensor(a, (1, 3))

    def to_far(a, near):
        return swap_tensor(jnp.stack([a, near]), (3, 1))

    a0 = attend_suffix(0, suffix_q)
    a0, suffix_q, *w_came = lax.optimization_barrier((a0, suffix_q, *w_came))

    w = join(w, w_came)
    w_came = gather_step(w, 2)
    near0 = to_near(a0)
    a1 = attend_suffix(GROUP, suffix_q)
    a0, a1, near0, prompt_q = lax.optimization_barrier((a0, a1, near0, prompt_q))

    far0 = to_far(a0, near0)
    near1 = to_near(a1)
    a2 = attend_prompt(0, prompt_q)
    a1, a2, near1, far0, prompt_q, *w_came = lax.optimization_barrier(
        (a1, a2, near1, far0, prompt_q, *w_came))

    w = join(w, w_came)
    w_came = gather_step(w, 3)
    far1 = to_far(a1, near1)
    near2 = to_near(a2)
    a3 = attend_prompt(GROUP, prompt_q)
    a2, a3, near2, far1, *w_mate = lax.optimization_barrier((a2, a3, near2, far1, *w))

    far2 = to_far(a2, near2)
    near3 = to_near(a3)
    far3 = to_far(a3, near3)
    w_mate = [swap(after(a, near3), 1) for a in w_mate]
    w_came_mate = [swap(after(a, far2), 1) for a in w_came]
    weights = [w[0], w_came[0], w[1], w_came[1],
               w_mate[0], w_came_mate[0], w_mate[1], w_came_mate[1]]
    total = project(
        False, info, [a2, a3, a0, a1, near2, near3, near0, near1], weights, None)
    return tuple(project(True, info, [far2, far3, far0, far1], weights, total))


def solution(mesh):
    both = P("sample", "tensor")
    return jax.shard_map(
        per_device,
        mesh=mesh,
        in_specs=(both,) * 6 + (P("sample"), P("sample"), both),
        out_specs=(both, both),
        check_vma=False,
    )
```

profile of v0, /device:TPU:37, one launch (start us, length us, event | category | flops | bytes accessed | tf_op | source)
XLA Modules:
  0.0 133.6 jit_solution(13889664099713437836)
XLA Ops:
  2.6 1.4 %collective-permute-start.3 = (bf16[64,2048]{1,0:T(8,128)(2,1)}, bf16[64,2048]{1,0:T(8,128)(2,1)S(1)}, u32[]{:S(2)}, u32[]{:S(2)}) collective-permute-start(bf16[64,2048]{1,0:T(8,128)(2,1)} %param.17), channel_id=1, source_target_pairs={{0,8},{4,12},{8,0},{12,4},{16,24},{20,28},{24,16},{28,20},{32,40},... | collective-permute-start | bytes 786440 | tf_op jit(solution)/shard_map/ppermute | solution.py:47
  4.0 1.4 %collective-permute-done.4 = bf16[128,256]{1,0:T(8,128)(2,1)S(1)} collective-permute-done((bf16[128,256]{1,0:T(8,128)(2,1)S(1)}, bf16[128,256]{1,0:T(8,128)(2,1)S(1)}, u32[]{:S(2)}, u32[]{:S(2)}) %collective-permute-start.4) | collective-permute-done | bytes 65568 | tf_op jit(solution)/shard_map/ppermute | solution.py:47
  5.4 2.7 %collective-permute-start.5 = (bf16[1,128,256]{2,1,0:T(8,128)(2,1)S(1)}, bf16[1,128,256]{2,1,0:T(8,128)(2,1)S(1)}, u32[]{:S(2)}, u32[]{:S(2)}) collective-permute-start(bf16[1,128,256]{2,1,0:T(8,128)(2,1)S(1)} %bitcast.36), channel_id=1, source_target_pairs={{0,64},{4,196},{8,72},{12,204},{16,80},{20,212},{24,88},{28,220},{... | collective-permute-start | bytes 196616 | tf_op jit(solution)/shard_map/ppermute | solution.py:47
  12.1 1.6 %collective-permute-start.2 = (bf16[4,128,256]{2,1,0:T(8,128)(2,1)S(1)}, bf16[4,128,256]{2,1,0:T(8,128)(2,1)S(1)}, u32[]{:S(2)}, u32[]{:S(2)}) collective-permute-start(bf16[4,128,256]{2,1,0:T(8,128)(2,1)S(1)} %pad_maximum_fusion.8), channel_id=1, source_target_pairs={{0,64},{4,196},{8,72},{12,204},{16,80},{20,212},{24,88},{28,220},{... | collective-permute-start | bytes 786440 | tf_op jit(solution)/shard_map/ppermute | solution.py:47
  14.3 1.4 %collective-permute-start.6 = (bf16[1,2,64,1024]{3,2,1,0:T(8,128)(2,1)S(1)}, bf16[1,2,64,1024]{3,2,1,0:T(8,128)(2,1)S(1)}, u32[]{:S(2)}, u32[]{:S(2)}) collective-permute-start(bf16[1,2,64,1024]{3,2,1,0:T(8,128)(2,1)S(1)} %maximum_bitcast_fusion), channel_id=1, source_target_pairs={{0,16},{4,52},{8,24},{12,60},{16,0},{20,36},{24,8},{28,44},{32,48}... | collective-permute-start | bytes 786440 | tf_op jit(solution)/shard_map/ppermute | solution.py:47
  15.8 2.5 %collective-permute-start.9 = (bf16[1,2,64,1024]{3,2,1,0:T(8,128)(2,1)S(1)}, bf16[1,2,64,1024]{3,2,1,0:T(8,128)(2,1)S(1)}, u32[]{:S(2)}, u32[]{:S(2)}) collective-permute-start(bf16[1,2,64,1024]{3,2,1,0:T(8,128)(2,1)S(1)} %maximum_bitcast_fusion.1), channel_id=1, source_target_pairs={{0,64},{4,196},{8,72},{12,204},{16,80},{20,212},{24,88},{28,220},{... | collective-permute-start | bytes 786440 | tf_op jit(solution)/shard_map/ppermute | solution.py:47
  18.3 1.7 %collective-permute-done.2 = bf16[4,128,256]{2,1,0:T(8,128)(2,1)S(1)} collective-permute-done((bf16[4,128,256]{2,1,0:T(8,128)(2,1)S(1)}, bf16[4,128,256]{2,1,0:T(8,128)(2,1)S(1)}, u32[]{:S(2)}, u32[]{:S(2)}) %collective-permute-start.2) | collective-permute-done | bytes 262176 | tf_op jit(solution)/shard_map/ppermute | solution.py:47
  20.1 2.3 %collective-permute-done.6 = bf16[1,2,64,1024]{3,2,1,0:T(8,128)(2,1)S(1)} collective-permute-done((bf16[1,2,64,1024]{3,2,1,0:T(8,128)(2,1)S(1)}, bf16[1,2,64,1024]{3,2,1,0:T(8,128)(2,1)S(1)}, u32[]{:S(2)}, u32[]{:S(2)}) %collective-permute-start.6) | collective-permute-done | bytes 262176 | tf_op jit(solution)/shard_map/ppermute | solution.py:47
  24.0 2.0 %collective-permute-start.11 = (bf16[8,128,256]{2,1,0:T(8,128)(2,1)S(1)}, bf16[8,128,256]{2,1,0:T(8,128)(2,1)S(1)}, u32[]{:S(2)}, u32[]{:S(2)}) collective-permute-start(bf16[8,128,256]{2,1,0:T(8,128)(2,1)S(1)} %pad_maximum_fusion.5.refs_2_), channel_id=1, source_target_pairs={{0,48},{4,20},{8,56},{12,28},{16,32},{20,4},{24,40},{28,12},{32,16... | collective-permute-start | bytes 1572872 | tf_op jit(solution)/shard_map/ppermute | solution.py:47
  26.0 9.1 %collective-permute-start.12 = (bf16[8,128,256]{2,1,0:T(8,128)(2,1)S(1)}, bf16[8,128,256]{2,1,0:T(8,128)(2,1)S(1)}, u32[]{:S(2)}, u32[]{:S(2)}) collective-permute-start(bf16[8,128,256]{2,1,0:T(8,128)(2,1)S(1)} %pad_maximum_fusion.4.refs_0_), channel_id=1, source_target_pairs={{0,4},{4,0},{8,12},{12,8},{16,20},{20,16},{24,28},{28,24},{32,36},... | collective-permute-start | bytes 1572872 | tf_op jit(solution)/shard_map/ppermute | solution.py:47
  35.1 7.0 %collective-permute-start.13 = (bf16[8,128,256]{2,1,0:T(8,128)(2,1)S(1)}, bf16[8,128,256]{2,1,0:T(8,128)(2,1)}, u32[]{:S(2)}, u32[]{:S(2)}) collective-permute-start(bf16[8,128,256]{2,1,0:T(8,128)(2,1)S(1)} %collective-permute-done.10.refs_1_), channel_id=1, source_target_pairs={{0,4},{4,0},{8,12},{12,8},{16,20},{20,16},{24,28},{28,24},{32,36},... | collective-permute-start | bytes 1572872 | tf_op jit(solution)/shard_map/ppermute | solution.py:47
  42.1 1.7 %collective-permute-start.15 = (bf16[8,128,256]{2,1,0:T(8,128)(2,1)S(1)}, bf16[8,128,256]{2,1,0:T(8,128)(2,1)}, u32[]{:S(2)}, u32[]{:S(2)}) collective-permute-start(bf16[8,128,256]{2,1,0:T(8,128)(2,1)S(1)} %collective-permute-done.11.refs_3_), channel_id=1, source_target_pairs={{0,4},{4,0},{8,12},{12,8},{16,20},{20,16},{24,28},{28,24},{32,36},... | collective-permute-start | bytes 1572872 | tf_op jit(solution)/shard_map/ppermute | solution.py:47
  43.8 1.5 %collective-permute-start.16 = (bf16[2,2,64,1024]{3,2,1,0:T(8,128)(2,1)}, bf16[2,2,64,1024]{3,2,1,0:T(8,128)(2,1)}, u32[]{:S(2)}, u32[]{:S(2)}) collective-permute-start(bf16[2,2,64,1024]{3,2,1,0:T(8,128)(2,1)} %get-tuple-element.39), channel_id=1, source_target_pairs={{0,48},{4,20},{8,56},{12,28},{16,32},{20,4},{24,40},{28,12},{32,16... | collective-permute-start | bytes 1572872 | tf_op jit(solution)/shard_map/ppermute | solution.py:47
  46.8 5.5 %attend_suffix_0.1.refs_2_ = bf16[128,512]{1,0:T(8,128)(2,1)S(1)} custom-call(s32[68]{0:T(128)S(1)} %concatenate.50.info, bf16[128,1024]{1,0:T(8,128)(2,1)S(1)} %copy-done, bf16[128,128]{1,0:T(8,128)(2,1)S(1)} %copy-done.4, bf16[128,128]{1,0:T(8,128)(2,1)S(1)} %copy-done.5, bf16[8,128,256]{2,1,0:T(8,128)(2,1)S(1)} %pad_maximum_fusion.4.refs_0_, ...), custom_call_target="tpu_custom_call" | custom-call | flops 1107296256 | bytes 4194304 | tf_op jit(solution)/shard_map/attend_suffix_0/pallas_call | solution.py:151
  52.5 1.5 %collective-permute-done.17 = bf16[2,2,64,1024]{3,2,1,0:T(8,128)(2,1)} collective-permute-done((bf16[2,2,64,1024]{3,2,1,0:T(8,128)(2,1)}, bf16[2,2,64,1024]{3,2,1,0:T(8,128)(2,1)}, u32[]{:S(2)}, u32[]{:S(2)}) %collective-permute-start.17) | collective-permute-done | bytes 524320 | tf_op jit(solution)/shard_map/ppermute | solution.py:47
  56.8 5.7 %collective-permute-start.18 = (bf16[128,512]{1,0:T(8,128)(2,1)S(1)}, bf16[128,512]{1,0:T(8,128)(2,1)S(1)}, u32[]{:S(2)}, u32[]{:S(2)}) collective-permute-start(bf16[128,512]{1,0:T(8,128)(2,1)S(1)} %attend_suffix_0.1.refs_2_), channel_id=1, source_target_pairs={{0,1},{1,0},{2,3},{3,2},{4,7},{5,6},{6,5},{7,4},{8,9},{9,8},{10,11... | collective-permute-start | bytes 393224 | tf_op jit(solution)/shard_map/ppermute | solution.py:52
  62.5 5.4 %attend_suffix_4.1.refs_3_ = bf16[128,512]{1,0:T(8,128)(2,1)S(1)} custom-call(s32[68]{0:T(128)S(1)} %concatenate.50.info, bf16[128,1024]{1,0:T(8,128)(2,1)S(1)} %copy-done, bf16[128,128]{1,0:T(8,128)(2,1)S(1)} %copy-done.4, bf16[128,128]{1,0:T(8,128)(2,1)S(1)} %copy-done.5, bf16[8,128,256]{2,1,0:T(8,128)(2,1)S(1)} %pad_maximum_fusion.4.refs_0_, ...), custom_call_target="tpu_custom_call" | custom-call | flops 1107296256 | bytes 4194304 | tf_op jit(solution)/shard_map/attend_suffix_4/pallas_call | solution.py:151
  69.2 1.8 %collective-permute-start.19 = (bf16[128,512]{1,0:T(8,128)(2,1)S(1)}, bf16[128,512]{1,0:T(8,128)(2,1)S(1)}, u32[]{:S(2)}, u32[]{:S(2)}) collective-permute-start(bf16[128,512]{1,0:T(8,128)(2,1)S(1)} %attend_suffix_4.1.refs_3_), channel_id=1, source_target_pairs={{0,1},{1,0},{2,3},{3,2},{4,7},{5,6},{6,5},{7,4},{8,9},{9,8},{10,11... | collective-permute-start | bytes 393224 | tf_op jit(solution)/shard_map/ppermute | solution.py:52
  71.0 3.7 %attend_prompt_0.1.refs_0_ = bf16[128,512]{1,0:T(8,128)(2,1)S(1)} custom-call(s32[68]{0:T(128)S(1)} %concatenate.50.info, bf16[128,1024]{1,0:T(8,128)(2,1)S(1)} %copy-done.1, bf16[128,128]{1,0:T(8,128)(2,1)S(1)} %copy-done.2, bf16[128,128]{1,0:T(8,128)(2,1)S(1)} %copy-done.3, bf16[8,128,256]{2,1,0:T(8,128)(2,1)S(1)} %pad_maximum_fusion.4.refs_0_, ...), custom_call_target="tpu_custom_call" | custom-call | flops 1107296256 | bytes 4194304 | tf_op jit(solution)/shard_map/attend_prompt_0/pallas_call | solution.py:151
  74.7 6.3 %collective-permute-done.19.refs_7_ = bf16[128,512]{1,0:T(8,128)(2,1)S(1)} collective-permute-done((bf16[128,512]{1,0:T(8,128)(2,1)S(1)}, bf16[128,512]{1,0:T(8,128)(2,1)S(1)}, u32[]{:S(2)}, u32[]{:S(2)}) %collective-permute-start.19) | collective-permute-done | bytes 131104 | tf_op jit(solution)/shard_map/ppermute | solution.py:52
  84.2 1.3 collective-permute-start.24
  85.6 3.7 %attend_prompt_4.1.refs_1_ = bf16[128,512]{1,0:T(8,128)(2,1)S(1)} custom-call(s32[68]{0:T(128)S(1)} %concatenate.50.info, bf16[128,1024]{1,0:T(8,128)(2,1)S(1)} %copy-done.1, bf16[128,128]{1,0:T(8,128)(2,1)S(1)} %copy-done.2, bf16[128,128]{1,0:T(8,128)(2,1)S(1)} %copy-done.3, bf16[8,128,256]{2,1,0:T(8,128)(2,1)S(1)} %pad_maximum_fusion.4.refs_0_, ...), custom_call_target="tpu_custom_call" | custom-call | flops 1107296256 | bytes 4194304 | tf_op jit(solution)/shard_map/attend_prompt_4/pallas_call | solution.py:151
  89.2 3.4 %collective-permute-done.23.refs_4_ = bf16[128,512]{1,0:T(8,128)(2,1)S(1)} collective-permute-done((bf16[128,512]{1,0:T(8,128)(2,1)S(1)}, bf16[128,512]{1,0:T(8,128)(2,1)S(1)}, u32[]{:S(2)}, u32[]{:S(2)}) %collective-permute-start.23) | collective-permute-done | bytes 131104 | tf_op jit(solution)/shard_map/ppermute | solution.py:52
  92.6 2.0 %collective-permute-start.25 = (bf16[2,128,512]{2,1,0:T(8,128)(2,1)S(1)}, bf16[2,128,512]{2,1,0:T(8,128)(2,1)S(1)}, u32[]{:S(2)}, u32[]{:S(2)}) collective-permute-start(bf16[2,128,512]{2,1,0:T(8,128)(2,1)S(1)} %pad_maximum_fusion.12), channel_id=1, source_target_pairs={{0,3},{1,2},{2,1},{3,0},{4,5},{5,4},{6,7},{7,6},{8,11},{9,10},{10,... | collective-permute-start | bytes 786440 | tf_op jit(solution)/shard_map/ppermute | solution.py:52
  94.6 6.6 %collective-permute-done.26.refs_5_ = bf16[128,512]{1,0:T(8,128)(2,1)S(1)} collective-permute-done((bf16[128,512]{1,0:T(8,128)(2,1)S(1)}, bf16[128,512]{1,0:T(8,128)(2,1)S(1)}, u32[]{:S(2)}, u32[]{:S(2)}) %collective-permute-start.26) | collective-permute-done | bytes 131104 | tf_op jit(solution)/shard_map/ppermute | solution.py:52
  101.3 12.8 %collective-permute-start.30 = (bf16[8,2,64,1024]{3,2,1,0:T(8,128)(2,1)S(1)}, bf16[8,2,64,1024]{3,2,1,0:T(8,128)(2,1)S(1)}, u32[]{:S(2)}, u32[]{:S(2)}) collective-permute-start(bf16[8,2,64,1024]{3,2,1,0:T(8,128)(2,1)S(1)} %pad_maximum_fusion.refs_8_.refs_5_), channel_id=1, source_target_pairs={{0,4},{4,0},{8,12},{12,8},{16,20},{20,16},{24,28},{28,24},{32,36},... | collective-permute-start | bytes 6291464 | tf_op jit(solution)/shard_map/ppermute | solution.py:47
  114.8 3.0 %collective-permute-done.30.refs_12_.refs_9_ = bf16[8,2,64,1024]{3,2,1,0:T(8,128)(2,1)S(1)} collective-permute-done((bf16[8,2,64,1024]{3,2,1,0:T(8,128)(2,1)S(1)}, bf16[8,2,64,1024]{3,2,1,0:T(8,128)(2,1)S(1)}, u32[]{:S(2)}, u32[]{:S(2)}) %collective-permute-start.30) | collective-permute-done | bytes 2097184 | tf_op jit(solution)/shard_map/ppermute | solution.py:47
  117.9 3.0 %collective-permute-done.32.refs_14_.refs_11_ = bf16[8,2,64,1024]{3,2,1,0:T(8,128)(2,1)S(1)} collective-permute-done((bf16[8,2,64,1024]{3,2,1,0:T(8,128)(2,1)S(1)}, bf16[8,2,64,1024]{3,2,1,0:T(8,128)(2,1)S(1)}, u32[]{:S(2)}, u32[]{:S(2)}) %collective-permute-start.32) | collective-permute-done | bytes 2097184 | tf_op jit(solution)/shard_map/ppermute | solution.py:47
  120.9 3.0 %collective-permute-done.33.refs_15_.refs_12_ = bf16[8,2,64,1024]{3,2,1,0:T(8,128)(2,1)S(1)} collective-permute-done((bf16[8,2,64,1024]{3,2,1,0:T(8,128)(2,1)S(1)}, bf16[8,2,64,1024]{3,2,1,0:T(8,128)(2,1)S(1)}, u32[]{:S(2)}, u32[]{:S(2)}) %collective-permute-start.33) | collective-permute-done | bytes 2097184 | tf_op jit(solution)/shard_map/ppermute | solution.py:47
  123.9 3.0 %collective-permute-done.31.refs_13_.refs_10_ = bf16[8,2,64,1024]{3,2,1,0:T(8,128)(2,1)S(1)} collective-permute-done((bf16[8,2,64,1024]{3,2,1,0:T(8,128)(2,1)S(1)}, bf16[8,2,64,1024]{3,2,1,0:T(8,128)(2,1)S(1)}, u32[]{:S(2)}, u32[]{:S(2)}) %collective-permute-start.31) | collective-permute-done | bytes 2097184 | tf_op jit(solution)/shard_map/ppermute | solution.py:47
  126.9 2.9 %project_first.1.refs_4_ = f32[256,2048]{1,0:T(8,128)S(1)} custom-call(s32[68]{0:T(128)S(1)} %concatenate.50.info, bf16[128,512]{1,0:T(8,128)(2,1)S(1)} %attend_prompt_0.1.refs_0_, bf16[128,512]{1,0:T(8,128)(2,1)S(1)} %attend_prompt_4.1.refs_1_, bf16[128,512]{1,0:T(8,128)(2,1)S(1)} %attend_suffix_0.1.refs_2_, bf16[128,512]{1,0:T(8,128)(2,1)S(1)} %attend_suffix_4.1.refs_3_, ...), custom_call_target="tpu_custom_call" | custom-call | tf_op jit(solution)/shard_map/project_first/pallas_call | solution.py:211
  129.8 3.9 %project_last.1 = (bf16[128,2048]{1,0:T(8,128)(2,1)}, bf16[128,2048]{1,0:T(8,128)(2,1)}) custom-call(s32[68]{0:T(128)S(1)} %concatenate.50.info, bf16[2,128,512]{2,1,0:T(8,128)(2,1)S(1)} %collective-permute-done.25.refs_0_, bf16[2,128,512]{2,1,0:T(8,128)(2,1)S(1)} %collective-permute-done.27.refs_1_, ...), custom_call_target="tpu_custom_call" | custom-call | tf_op jit(solution)/shard_map/project_last/pallas_call | solution.py:211
  (94 shorter events, 16.7 us)
Async XLA Ops:
  2.3 5.8 %collective-permute-start = (bf16[1,128,256]{2,1,0:T(8,128)(2,1)S(1)}, bf16[1,128,256]{2,1,0:T(8,128)(2,1)S(1)}, u32[]{:S(2)}, u32[]{:S(2)}) collective-permute-start(bf16[1,128,256]{2,1,0:T(8,128)(2,1)S(1)} %bitcast.32), channel_id=1, source_target_pairs={{0,16},{4,52},{8,24},{12,60},{16,0},{20,36},{24,8},{28,44},{32,48}... | collective-permute-start | bytes 196616 | tf_op jit(solution)/shard_map/ppermute | solution.py:47
  2.6 11.6 %collective-permute-start.3 = (bf16[64,2048]{1,0:T(8,128)(2,1)}, bf16[64,2048]{1,0:T(8,128)(2,1)S(1)}, u32[]{:S(2)}, u32[]{:S(2)}) collective-permute-start(bf16[64,2048]{1,0:T(8,128)(2,1)} %param.17), channel_id=1, source_target_pairs={{0,8},{4,12},{8,0},{12,4},{16,24},{20,28},{24,16},{28,20},{32,40},... | collective-permute-start | bytes 786440 | tf_op jit(solution)/shard_map/ppermute | solution.py:47
  5.4 4.4 %collective-permute-start.5 = (bf16[1,128,256]{2,1,0:T(8,128)(2,1)S(1)}, bf16[1,128,256]{2,1,0:T(8,128)(2,1)S(1)}, u32[]{:S(2)}, u32[]{:S(2)}) collective-permute-start(bf16[1,128,256]{2,1,0:T(8,128)(2,1)S(1)} %bitcast.36), channel_id=1, source_target_pairs={{0,64},{4,196},{8,72},{12,204},{16,80},{20,212},{24,88},{28,220},{... | collective-permute-start | bytes 196616 | tf_op jit(solution)/shard_map/ppermute | solution.py:47
  9.8 4.2 %collective-permute-start.7 = (bf16[2,128,256]{2,1,0:T(8,128)(2,1)S(1)}, bf16[2,128,256]{2,1,0:T(8,128)(2,1)S(1)}, u32[]{:S(2)}, u32[]{:S(2)}) collective-permute-start(bf16[2,128,256]{2,1,0:T(8,128)(2,1)S(1)} %pad_maximum_fusion.15), channel_id=1, source_target_pairs={{0,192},{4,68},{8,200},{12,76},{16,208},{20,84},{24,216},{28,92},{... | collective-permute-start | bytes 393224 | tf_op jit(solution)/shard_map/ppermute | solution.py:47
  12.1 7.9 %collective-permute-start.2 = (bf16[4,128,256]{2,1,0:T(8,128)(2,1)S(1)}, bf16[4,128,256]{2,1,0:T(8,128)(2,1)S(1)}, u32[]{:S(2)}, u32[]{:S(2)}) collective-permute-start(bf16[4,128,256]{2,1,0:T(8,128)(2,1)S(1)} %pad_maximum_fusion.8), channel_id=1, source_target_pairs={{0,64},{4,196},{8,72},{12,204},{16,80},{20,212},{24,88},{28,220},{... | collective-permute-start | bytes 786440 | tf_op jit(solution)/shard_map/ppermute | solution.py:47
  14.0 6.0 %collective-permute-start.8 = (bf16[4,128,256]{2,1,0:T(8,128)(2,1)S(1)}, bf16[4,128,256]{2,1,0:T(8,128)(2,1)S(1)}, u32[]{:S(2)}, u32[]{:S(2)}) collective-permute-start(bf16[4,128,256]{2,1,0:T(8,128)(2,1)S(1)} %pad_maximum_fusion.9), channel_id=1, source_target_pairs={{0,16},{4,52},{8,24},{12,60},{16,0},{20,36},{24,8},{28,44},{32,48}... | collective-permute-start | bytes 786440 | tf_op jit(solution)/shard_map/ppermute | solution.py:47
  14.3 8.1 %collective-permute-start.6 = (bf16[1,2,64,1024]{3,2,1,0:T(8,128)(2,1)S(1)}, bf16[1,2,64,1024]{3,2,1,0:T(8,128)(2,1)S(1)}, u32[]{:S(2)}, u32[]{:S(2)}) collective-permute-start(bf16[1,2,64,1024]{3,2,1,0:T(8,128)(2,1)S(1)} %maximum_bitcast_fusion), channel_id=1, source_target_pairs={{0,16},{4,52},{8,24},{12,60},{16,0},{20,36},{24,8},{28,44},{32,48}... | collective-permute-start | bytes 786440 | tf_op jit(solution)/shard_map/ppermute | solution.py:47
  15.8 7.0 %collective-permute-start.9 = (bf16[1,2,64,1024]{3,2,1,0:T(8,128)(2,1)S(1)}, bf16[1,2,64,1024]{3,2,1,0:T(8,128)(2,1)S(1)}, u32[]{:S(2)}, u32[]{:S(2)}) collective-permute-start(bf16[1,2,64,1024]{3,2,1,0:T(8,128)(2,1)S(1)} %maximum_bitcast_fusion.1), channel_id=1, source_target_pairs={{0,64},{4,196},{8,72},{12,204},{16,80},{20,212},{24,88},{28,220},{... | collective-permute-start | bytes 786440 | tf_op jit(solution)/shard_map/ppermute | solution.py:47
  23.9 11.2 %collective-permute-start.10 = (bf16[8,128,256]{2,1,0:T(8,128)(2,1)S(1)}, bf16[8,128,256]{2,1,0:T(8,128)(2,1)S(1)}, u32[]{:S(2)}, u32[]{:S(2)}) collective-permute-start(bf16[8,128,256]{2,1,0:T(8,128)(2,1)S(1)} %pad_maximum_fusion.4.refs_0_), channel_id=1, source_target_pairs={{0,192},{4,68},{8,200},{12,76},{16,208},{20,84},{24,216},{28,92},{... | collective-permute-start | bytes 1572872 | tf_op jit(solution)/shard_map/ppermute | solution.py:47
  24.0 18.1 %collective-permute-start.11 = (bf16[8,128,256]{2,1,0:T(8,128)(2,1)S(1)}, bf16[8,128,256]{2,1,0:T(8,128)(2,1)S(1)}, u32[]{:S(2)}, u32[]{:S(2)}) collective-permute-start(bf16[8,128,256]{2,1,0:T(8,128)(2,1)S(1)} %pad_maximum_fusion.5.refs_2_), channel_id=1, source_target_pairs={{0,48},{4,20},{8,56},{12,28},{16,32},{20,4},{24,40},{28,12},{32,16... | collective-permute-start | bytes 1572872 | tf_op jit(solution)/shard_map/ppermute | solution.py:47
  26.0 19.3 %collective-permute-start.12 = (bf16[8,128,256]{2,1,0:T(8,128)(2,1)S(1)}, bf16[8,128,256]{2,1,0:T(8,128)(2,1)S(1)}, u32[]{:S(2)}, u32[]{:S(2)}) collective-permute-start(bf16[8,128,256]{2,1,0:T(8,128)(2,1)S(1)} %pad_maximum_fusion.4.refs_0_), channel_id=1, source_target_pairs={{0,4},{4,0},{8,12},{12,8},{16,20},{20,16},{24,28},{28,24},{32,36},... | collective-permute-start | bytes 1572872 | tf_op jit(solution)/shard_map/ppermute | solution.py:47
  35.1 11.6 %collective-permute-start.14 = (bf16[8,128,256]{2,1,0:T(8,128)(2,1)S(1)}, bf16[8,128,256]{2,1,0:T(8,128)(2,1)S(1)}, u32[]{:S(2)}, u32[]{:S(2)}) collective-permute-start(bf16[8,128,256]{2,1,0:T(8,128)(2,1)S(1)} %pad_maximum_fusion.5.refs_2_), channel_id=1, source_target_pairs={{0,4},{4,0},{8,12},{12,8},{16,20},{20,16},{24,28},{28,24},{32,36},... | collective-permute-start | bytes 1572872 | tf_op jit(solution)/shard_map/ppermute | solution.py:47
  35.1 11.6 %collective-permute-start.13 = (bf16[8,128,256]{2,1,0:T(8,128)(2,1)S(1)}, bf16[8,128,256]{2,1,0:T(8,128)(2,1)}, u32[]{:S(2)}, u32[]{:S(2)}) collective-permute-start(bf16[8,128,256]{2,1,0:T(8,128)(2,1)S(1)} %collective-permute-done.10.refs_1_), channel_id=1, source_target_pairs={{0,4},{4,0},{8,12},{12,8},{16,20},{20,16},{24,28},{28,24},{32,36},... | collective-permute-start | bytes 1572872 | tf_op jit(solution)/shard_map/ppermute | solution.py:47
  42.1 4.7 %collective-permute-start.15 = (bf16[8,128,256]{2,1,0:T(8,128)(2,1)S(1)}, bf16[8,128,256]{2,1,0:T(8,128)(2,1)}, u32[]{:S(2)}, u32[]{:S(2)}) collective-permute-start(bf16[8,128,256]{2,1,0:T(8,128)(2,1)S(1)} %collective-permute-done.11.refs_3_), channel_id=1, source_target_pairs={{0,4},{4,0},{8,12},{12,8},{16,20},{20,16},{24,28},{28,24},{32,36},... | collective-permute-start | bytes 1572872 | tf_op jit(solution)/shard_map/ppermute | solution.py:47
  43.8 8.7 %collective-permute-start.16 = (bf16[2,2,64,1024]{3,2,1,0:T(8,128)(2,1)}, bf16[2,2,64,1024]{3,2,1,0:T(8,128)(2,1)}, u32[]{:S(2)}, u32[]{:S(2)}) collective-permute-start(bf16[2,2,64,1024]{3,2,1,0:T(8,128)(2,1)} %get-tuple-element.39), channel_id=1, source_target_pairs={{0,48},{4,20},{8,56},{12,28},{16,32},{20,4},{24,40},{28,12},{32,16... | collective-permute-start | bytes 1572872 | tf_op jit(solution)/shard_map/ppermute | solution.py:47
  45.3 8.6 %collective-permute-start.17 = (bf16[2,2,64,1024]{3,2,1,0:T(8,128)(2,1)}, bf16[2,2,64,1024]{3,2,1,0:T(8,128)(2,1)}, u32[]{:S(2)}, u32[]{:S(2)}) collective-permute-start(bf16[2,2,64,1024]{3,2,1,0:T(8,128)(2,1)} %get-tuple-element.40), channel_id=1, source_target_pairs={{0,192},{4,68},{8,200},{12,76},{16,208},{20,84},{24,216},{28,92},{... | collective-permute-start | bytes 1572872 | tf_op jit(solution)/shard_map/ppermute | solution.py:47
  56.3 24.6 %collective-permute-start.22 = (bf16[4,2,64,1024]{3,2,1,0:T(8,128)(2,1)S(1)}, bf16[4,2,64,1024]{3,2,1,0:T(8,128)(2,1)S(1)}, u32[]{:S(2)}, u32[]{:S(2)}) collective-permute-start(bf16[4,2,64,1024]{3,2,1,0:T(8,128)(2,1)S(1)} %pad_maximum_fusion.3), channel_id=1, source_target_pairs={{0,16},{4,52},{8,24},{12,60},{16,0},{20,36},{24,8},{28,44},{32,48}... | collective-permute-start | bytes 3145736 | tf_op jit(solution)/shard_map/ppermute | solution.py:47
  56.6 24.3 %collective-permute-start.21 = (bf16[4,2,64,1024]{3,2,1,0:T(8,128)(2,1)S(1)}, bf16[4,2,64,1024]{3,2,1,0:T(8,128)(2,1)S(1)}, u32[]{:S(2)}, u32[]{:S(2)}) collective-permute-start(bf16[4,2,64,1024]{3,2,1,0:T(8,128)(2,1)S(1)} %pad_maximum_fusion.2), channel_id=1, source_target_pairs={{0,64},{4,196},{8,72},{12,204},{16,80},{20,212},{24,88},{28,220},{... | collective-permute-start | bytes 3145736 | tf_op jit(solution)/shard_map/ppermute | solution.py:47
  56.8 11.1 %collective-permute-start.18 = (bf16[128,512]{1,0:T(8,128)(2,1)S(1)}, bf16[128,512]{1,0:T(8,128)(2,1)S(1)}, u32[]{:S(2)}, u32[]{:S(2)}) collective-permute-start(bf16[128,512]{1,0:T(8,128)(2,1)S(1)} %attend_suffix_0.1.refs_2_), channel_id=1, source_target_pairs={{0,1},{1,0},{2,3},{3,2},{4,7},{5,6},{6,5},{7,4},{8,9},{9,8},{10,11... | collective-permute-start | bytes 393224 | tf_op jit(solution)/shard_map/ppermute | solution.py:52
  68.0 13.0 %collective-permute-start.20 = (bf16[2,128,512]{2,1,0:T(8,128)(2,1)S(1)}, bf16[2,128,512]{2,1,0:T(8,128)(2,1)S(1)}, u32[]{:S(2)}, u32[]{:S(2)}) collective-permute-start(bf16[2,128,512]{2,1,0:T(8,128)(2,1)S(1)} %pad_maximum_fusion.10), channel_id=1, source_target_pairs={{0,3},{1,2},{2,1},{3,0},{4,5},{5,4},{6,7},{7,6},{8,11},{9,10},{10,... | collective-permute-start | bytes 786440 | tf_op jit(solution)/shard_map/ppermute | solution.py:52
  69.2 11.7 %collective-permute-start.19 = (bf16[128,512]{1,0:T(8,128)(2,1)S(1)}, bf16[128,512]{1,0:T(8,128)(2,1)S(1)}, u32[]{:S(2)}, u32[]{:S(2)}) collective-permute-start(bf16[128,512]{1,0:T(8,128)(2,1)S(1)} %attend_suffix_4.1.refs_3_), channel_id=1, source_target_pairs={{0,1},{1,0},{2,3},{3,2},{4,7},{5,6},{6,5},{7,4},{8,9},{9,8},{10,11... | collective-permute-start | bytes 393224 | tf_op jit(solution)/shard_map/ppermute | solution.py:52
  82.2 31.9 %collective-permute-start.29 = (bf16[8,2,64,1024]{3,2,1,0:T(8,128)(2,1)S(1)}, bf16[8,2,64,1024]{3,2,1,0:T(8,128)(2,1)S(1)}, u32[]{:S(2)}, u32[]{:S(2)}) collective-permute-start(bf16[8,2,64,1024]{3,2,1,0:T(8,128)(2,1)S(1)} %pad_maximum_fusion.1.refs_10_.refs_7_), channel_id=1, source_target_pairs={{0,48},{4,20},{8,56},{12,28},{16,32},{20,4},{24,40},{28,12},{32,16... | collective-permute-start | bytes 6291464 | tf_op jit(solution)/shard_map/ppermute | solution.py:47
  84.1 30.5 %collective-permute-start.28 = (bf16[8,2,64,1024]{3,2,1,0:T(8,128)(2,1)S(1)}, bf16[8,2,64,1024]{3,2,1,0:T(8,128)(2,1)S(1)}, u32[]{:S(2)}, u32[]{:S(2)}) collective-permute-start(bf16[8,2,64,1024]{3,2,1,0:T(8,128)(2,1)S(1)} %pad_maximum_fusion.refs_8_.refs_5_), channel_id=1, source_target_pairs={{0,192},{4,68},{8,200},{12,76},{16,208},{20,84},{24,216},{28,92},{... | collective-permute-start | bytes 6291464 | tf_op jit(solution)/shard_map/ppermute | solution.py:47
  84.2 8.4 %collective-permute-start.24 = (bf16[2,128,512]{2,1,0:T(8,128)(2,1)S(1)}, bf16[2,128,512]{2,1,0:T(8,128)(2,1)S(1)}, u32[]{:S(2)}, u32[]{:S(2)}) collective-permute-start(bf16[2,128,512]{2,1,0:T(8,128)(2,1)S(1)} %pad_maximum_fusion.11), channel_id=1, source_target_pairs={{0,3},{1,2},{2,1},{3,0},{4,5},{5,4},{6,7},{7,6},{8,11},{9,10},{10,... | collective-permute-start | bytes 786440 | tf_op jit(solution)/shard_map/ppermute | solution.py:52
  85.6 7.0 %collective-permute-start.23 = (bf16[128,512]{1,0:T(8,128)(2,1)S(1)}, bf16[128,512]{1,0:T(8,128)(2,1)S(1)}, u32[]{:S(2)}, u32[]{:S(2)}) collective-permute-start(bf16[128,512]{1,0:T(8,128)(2,1)S(1)} %attend_prompt_0.1.refs_0_), channel_id=1, source_target_pairs={{0,1},{1,0},{2,3},{3,2},{4,7},{5,6},{6,5},{7,4},{8,9},{9,8},{10,11... | collective-permute-start | bytes 393224 | tf_op jit(solution)/shard_map/ppermute | solution.py:52
  92.6 21.5 %collective-permute-start.25 = (bf16[2,128,512]{2,1,0:T(8,128)(2,1)S(1)}, bf16[2,128,512]{2,1,0:T(8,128)(2,1)S(1)}, u32[]{:S(2)}, u32[]{:S(2)}) collective-permute-start(bf16[2,128,512]{2,1,0:T(8,128)(2,1)S(1)} %pad_maximum_fusion.12), channel_id=1, source_target_pairs={{0,3},{1,2},{2,1},{3,0},{4,5},{5,4},{6,7},{7,6},{8,11},{9,10},{10,... | collective-permute-start | bytes 786440 | tf_op jit(solution)/shard_map/ppermute | solution.py:52
  94.6 6.7 %collective-permute-start.26 = (bf16[128,512]{1,0:T(8,128)(2,1)S(1)}, bf16[128,512]{1,0:T(8,128)(2,1)S(1)}, u32[]{:S(2)}, u32[]{:S(2)}) collective-permute-start(bf16[128,512]{1,0:T(8,128)(2,1)S(1)} %attend_prompt_4.1.refs_1_), channel_id=1, source_target_pairs={{0,1},{1,0},{2,3},{3,2},{4,7},{5,6},{6,5},{7,4},{8,9},{9,8},{10,11... | collective-permute-start | bytes 393224 | tf_op jit(solution)/shard_map/ppermute | solution.py:52
  101.3 16.6 %collective-permute-start.30 = (bf16[8,2,64,1024]{3,2,1,0:T(8,128)(2,1)S(1)}, bf16[8,2,64,1024]{3,2,1,0:T(8,128)(2,1)S(1)}, u32[]{:S(2)}, u32[]{:S(2)}) collective-permute-start(bf16[8,2,64,1024]{3,2,1,0:T(8,128)(2,1)S(1)} %pad_maximum_fusion.refs_8_.refs_5_), channel_id=1, source_target_pairs={{0,4},{4,0},{8,12},{12,8},{16,20},{20,16},{24,28},{28,24},{32,36},... | collective-permute-start | bytes 6291464 | tf_op jit(solution)/shard_map/ppermute | solution.py:47
  114.1 6.8 %collective-permute-start.32 = (bf16[8,2,64,1024]{3,2,1,0:T(8,128)(2,1)S(1)}, bf16[8,2,64,1024]{3,2,1,0:T(8,128)(2,1)S(1)}, u32[]{:S(2)}, u32[]{:S(2)}) collective-permute-start(bf16[8,2,64,1024]{3,2,1,0:T(8,128)(2,1)S(1)} %pad_maximum_fusion.1.refs_10_.refs_7_), channel_id=1, source_target_pairs={{0,4},{4,0},{8,12},{12,8},{16,20},{20,16},{24,28},{28,24},{32,36},... | collective-permute-start | bytes 6291464 | tf_op jit(solution)/shard_map/ppermute | solution.py:47
  114.1 9.8 %collective-permute-start.33 = (bf16[8,2,64,1024]{3,2,1,0:T(8,128)(2,1)S(1)}, bf16[8,2,64,1024]{3,2,1,0:T(8,128)(2,1)S(1)}, u32[]{:S(2)}, u32[]{:S(2)}) collective-permute-start(bf16[8,2,64,1024]{3,2,1,0:T(8,128)(2,1)S(1)} %collective-permute-done.29.refs_11_.refs_8_), channel_id=1, source_target_pairs={{0,4},{4,0},{8,12},{12,8},{16,20},{20,16},{24,28},{28,24},{32,36},... | collective-permute-start | bytes 6291464 | tf_op jit(solution)/shard_map/ppermute | solution.py:47
  114.6 12.3 %collective-permute-start.31 = (bf16[8,2,64,1024]{3,2,1,0:T(8,128)(2,1)S(1)}, bf16[8,2,64,1024]{3,2,1,0:T(8,128)(2,1)S(1)}, u32[]{:S(2)}, u32[]{:S(2)}) collective-permute-start(bf16[8,2,64,1024]{3,2,1,0:T(8,128)(2,1)S(1)} %collective-permute-done.28.refs_9_.refs_6_), channel_id=1, source_target_pairs={{0,4},{4,0},{8,12},{12,8},{16,20},{20,16},{24,28},{28,24},{32,36},... | collective-permute-start | bytes 6291464 | tf_op jit(solution)/shard_map/ppermute | solution.py:47
  114.7 15.0 %collective-permute-start.27 = (bf16[2,128,512]{2,1,0:T(8,128)(2,1)S(1)}, bf16[2,128,512]{2,1,0:T(8,128)(2,1)S(1)}, u32[]{:S(2)}, u32[]{:S(2)}) collective-permute-start(bf16[2,128,512]{2,1,0:T(8,128)(2,1)S(1)} %pad_maximum_fusion.13), channel_id=1, source_target_pairs={{0,3},{1,2},{2,1},{3,0},{4,5},{5,4},{6,7},{7,6},{8,11},{9,10},{10,... | collective-permute-start | bytes 786440 | tf_op jit(solution)/shard_map/ppermute | solution.py:52
  (16 other events, 184.7 us)
where the time goes:
time: 134 us
  starting transfers between devices  59.8 us (45%)
  waiting for transfers between devices  37.6 us (28%)
  Pallas kernels  25 us (19%)
  other arithmetic  6.25 us (5%)
  local copies, waits for them, and re-layouts  2.69 us (2%)
  between operations  2.33 us (2%)
    ppermute x26, starting transfers between devices, swap(): return lax.ppermute(x, 'sample', [(s, s ^ masks[s & 1]) for s in range(64)])  47.8 us
    ppermute x26, waiting for transfers between devices, swap(): return lax.ppermute(x, 'sample', [(s, s ^ masks[s & 1]) for s in range(64)])  21.3 us
    pallas_call x4, Pallas kernels, attend(): pl.pallas_call(functools.partial(attend_kernel, is_prompt, first), out_sh...  18.2 us
    ppermute x8, waiting for transfers between devices, swap_tensor(): return lax.ppermute(x, ('sample', 'tensor'), pairs)  16.3 us
    ppermute x8, starting transfers between devices, swap_tensor(): return lax.ppermute(x, ('sample', 'tensor'), pairs)  12.1 us
    pallas_call x2, Pallas kernels, project(): pl.pallas_call(functools.partial(project_kernel, last), out_shape=out_sha...  6.74 us
    concatenate x11, other arithmetic, join(): return [jnp.concatenate([a, b], axis=0) for a, b in zip(pieces, came)]  6.06 us
  transfers between devices with their start and end apart: 34, of which 16 were waited for; matrix products, arithmetic and copies ran while one was open for 2% of the time, Pallas kernels for 16%

commit v1 on v0

v1 whole, which is shorter than its diff:
```python
import functools

import jax
import jax.numpy as jnp
from jax import lax
from jax.experimental import pallas as pl
from jax.experimental.pallas import tpu as pltpu
from jax.sharding import PartitionSpec as P

HD = 128
HEADS = 8
ROWS = 128
SCALE = HD ** (-0.5) * 1.4426950408889634
ORDERS = (((4, 12, 16, 48), (12, 4, 48, 16)), ((16, 48, 4, 12), (48, 16, 12, 4)))
VMEM = pl.BlockSpec(memory_space=pltpu.VMEM)
SMEM = pl.BlockSpec(memory_space=pltpu.SMEM)


def slot_table(me):
    there = jnp.arange(16, dtype=jnp.int32)
    apart = there ^ (me >> 2)
    low_x, high_x = apart & 1, (apart >> 1) & 1
    low_y, high_y = (apart >> 2) & 1, (apart >> 3) & 1
    used = {4: low_x ^ high_x, 12: high_x, 16: low_y ^ high_y, 48: high_y}
    rows = []
    for rc in range(2):
        for piece in range(2):
            first, second = [
                sum(used[mask] << step for step, mask in enumerate(order))
                for order in ORDERS[piece]]
            rows.append(jnp.where((me & 1) == rc, first, second))
    return jnp.concatenate(rows)


def slot_of(info, rc, piece, there):
    return info[4 + (rc * 2 + piece) * 16 + there]


def take(halves, slot):
    low = slot & 7
    return jnp.where(slot > 7, halves[1][low], halves[0][low])


def swap(x, masks):
    masks = masks if isinstance(masks, tuple) else (masks, masks)
    return lax.ppermute(x, "sample", [(s, s ^ masks[s & 1]) for s in range(64)])


def swap_tensor(x, masks):
    pairs = [(s * 4 + t, s * 4 + (t ^ masks[s & 1])) for s in range(64) for t in range(4)]
    return lax.ppermute(x, ("sample", "tensor"), pairs)


def after(x, *others):
    return lax.optimization_barrier((x, *others))[0]


def step_masks(piece, step):
    return (ORDERS[piece][0][step], ORDERS[piece][1][step])


def gather_step(pieces, step):
    return [swap(piece, step_masks(i, step)) for i, piece in enumerate(pieces)]


def join(pieces, came):
    return [jnp.concatenate([a, b], axis=0) for a, b in zip(pieces, came)]


def score_head(q, h, keys):
    return lax.dot_general(
        q[:, h * HD:(h + 1) * HD], keys, (((1,), (1,)), ((), ())),
        preferred_element_type=jnp.float32)


def add_values(acc, h, exps, shrink, values):
    acc[h] = acc[h] * jnp.concatenate([shrink, shrink], axis=1) + jnp.dot(
        exps, values, preferred_element_type=jnp.float32)


def attend_kernel(is_prompt, first, count, info, q, own_k, own_v, *refs):
    blocks, (out, top, acc) = refs[:4], refs[4:]
    me = info[0]
    core, low_z = me & 1, (me >> 1) & 1
    row = lax.broadcasted_iota(jnp.int32, (ROWS, ROWS), 0)
    col = lax.broadcasted_iota(jnp.int32, (ROWS, ROWS), 1)
    keys = own_k[...]
    values = jnp.concatenate([own_v[...], jnp.ones((ROWS, HD), jnp.bfloat16)], axis=1)
    scores = [
        jnp.where(row >= col, score_head(q, first + h, keys), -1e30) for h in range(count)]
    best = [
        jnp.broadcast_to(jnp.max(part, axis=1, keepdims=True), (ROWS, HD)) for part in scores]
    exps = [
        jnp.exp2((part - high) * SCALE).astype(jnp.bfloat16) for part, high in zip(scores, best)]
    for h in range(count):
        top[h] = best[h]
        acc[h] = jnp.dot(exps[h], values, preferred_element_type=jnp.float32)

    def absorb(pair, masked):
        begin = 8 * (me >> 5 if is_prompt else info[1]) + 2 * pair
        keys, values, allowed = [], [], []
        for there in (begin, begin + 1):
            for rc in range(2):
                for rz in range(2):
                    slot = slot_of(info, rc, rz, there)
                    both = blocks[rc * 2 + rz][slot]
                    keys.append(both[:, :HD])
                    values.append(both[:, HD:])
                    allowed.append(there * 4 + ((me ^ (rz * 2 + rc)) & 3) < me)
        keys = jnp.concatenate(keys, axis=0)
        values = jnp.concatenate(values, axis=0)
        values = jnp.concatenate([values, jnp.ones(values.shape, jnp.bfloat16)], axis=1)
        ahead = score_head(q, first, keys)
        behind = None
        for h in range(count):
            scores = ahead
            if h + 1 < count:
                ahead = score_head(q, first + h + 1, keys)
            parts = [scores[:, i * ROWS:(i + 1) * ROWS] for i in range(8)]
            if masked:
                parts = [jnp.where(ok, part, -1e30) for ok, part in zip(allowed, parts)]
            best = functools.reduce(jnp.maximum, parts)
            old = top[h]
            new = jnp.maximum(old, jnp.max(best, axis=1, keepdims=True))
            shrink = jnp.exp2((old - new) * SCALE)
            top[h] = new
            exps = jnp.concatenate(
                [jnp.exp2((part - new) * SCALE).astype(jnp.bfloat16) for part in parts], axis=1)
            if behind is not None:
                add_values(acc, h - 1, *behind, values)
            behind = exps, shrink
        add_values(acc, count - 1, *behind, values)

    whole = (me & 31) >> 3 if is_prompt else 4
    lax.fori_loop(0, whole, lambda i, c: (absorb(i, False), c)[1], 0)
    if is_prompt:
        @pl.when((me & 7) > 0)
        def _():
            absorb(whole, True)
    for h in range(count):
        result = acc[h][:, :HD] / acc[h][:, HD:]
        if not is_prompt:
            result = jnp.where(row < info[2], result, 0.0)
        result = jnp.where(core == 0, result, pltpu.roll(result, HD // 2, 1))
        place = pl.multiple_of((h ^ low_z) * HD, HD)
        out[:, pl.ds(place, HD)] = result.astype(jnp.bfloat16)


def attend(is_prompt, first, count, info, q, own_k, own_v, blocks):
    return pl.pallas_call(
        functools.partial(attend_kernel, is_prompt, first, count),
        out_shape=jax.ShapeDtypeStruct((ROWS, count * HD), jnp.bfloat16),
        in_specs=[SMEM] + [VMEM] * (3 + len(blocks)),
        out_specs=VMEM,
        scratch_shapes=[
            pltpu.VMEM((count, ROWS, HD), jnp.float32),
            pltpu.VMEM((count, ROWS, 2 * HD), jnp.float32),
        ],
        compiler_params=pltpu.CompilerParams(vmem_limit_bytes=12 << 20),
        name="attend_%s_%d" % ("prompt" if is_prompt else "suffix", first),
    )(info, q, own_k, own_v, *blocks)


def project_kernel(kind, info, *refs):
    if kind == "first":
        heads, weights, (out,) = refs[:4], refs[4:12], refs[12:]
    else:
        heads, total, weights, (out,) = refs[0], refs[1], refs[2:10], refs[10:]
    core, tensor = info[0] & 1, info[3]
    near = jnp.where(core == 0, 1, 3)
    if kind == "first":
        pieces = [(tensor, jnp.concatenate([heads[0][...], heads[1][...]], axis=0)),
                  (tensor ^ near, jnp.concatenate([heads[2][...], heads[3][...]], axis=0))]
    else:
        pieces = [(tensor ^ near ^ 2, heads[0]), (tensor ^ 2, heads[1])]
    for piece in range(2):
        lanes = slice(piece * 1024, (piece + 1) * 1024)
        sums = None if kind == "first" else total[:, lanes]
        for quarter, rows in pieces:
            held = []
            for x in range(4):
                there = quarter * 4 + x
                found = [
                    take(weights[rc * 4 + piece * 2:rc * 4 + piece * 2 + 2],
                         slot_of(info, rc, piece, there)) for rc in range(2)]
                for rz in range(2):
                    held += [found[0][rz], found[1][rz]]
            part = jnp.dot(
                rows, jnp.concatenate(held, axis=0), preferred_element_type=jnp.float32)
            sums = part if sums is None else sums + part
        out[:, lanes] = sums.astype(out.dtype)


def project(kind, info, heads, weights, total=None):
    if kind == "first":
        out_shape = jax.ShapeDtypeStruct((2 * ROWS, 2048), jnp.float32)
    else:
        out_shape = jax.ShapeDtypeStruct((ROWS, 2048), jnp.bfloat16)
    args = [info, *heads] + ([] if kind == "first" else [total]) + list(weights)
    return pl.pallas_call(
        functools.partial(project_kernel, kind),
        out_shape=out_shape,
        in_specs=[SMEM] + [VMEM] * (len(args) - 1),
        out_specs=VMEM,
        compiler_params=pltpu.CompilerParams(vmem_limit_bytes=24 << 20),
        name="project_" + kind,
    )(*args)


def per_device(
    prompt_q, prompt_k, prompt_v, suffix_q, suffix_k, suffix_v, prompt_of, suffix_len, out_weight
):
    me = lax.axis_index("sample").astype(jnp.int32)
    info = jnp.concatenate([
        jnp.stack([me, prompt_of[0], suffix_len[0], lax.axis_index("tensor").astype(jnp.int32)]),
        slot_table(me)])

    other_k, other_v = swap(prompt_k, 2), swap(prompt_v, 2)
    kv = [jnp.concatenate([prompt_k, prompt_v], axis=1)[None],
          jnp.concatenate([other_k, other_v], axis=1)[None]]
    others = swap(after(out_weight, other_k), 2)
    kv = join(kv, gather_step(kv, 0))
    kv = join(kv, gather_step(kv, 1))
    others, info = lax.optimization_barrier((others, info))
    w = [jnp.stack([part[:, lanes] for part in (out_weight, others)])[None]
         for lanes in (slice(0, 1024), slice(1024, 2048))]
    w_came = gather_step(w, 0)
    kv = join(kv, gather_step([after(a, *w) for a in kv], 2))
    w = join(w, w_came)
    w_came = gather_step(w, 1)
    came = gather_step([after(a, *w) for a in kv], 3)
    kv_mate = [swap(a, 1) for a in kv]
    came_mate = [swap(a, 1) for a in came]
    blocks = [*join(kv, came), *join(kv_mate, came_mate)]
    w = join(w, [after(a, *came) for a in w_came])

    def to_near(a):
        return swap_tensor(a, (1, 3))

    def to_far(a):
        return swap_tensor(a, (3, 1))

    w_came = gather_step(w, 2)
    a_s = attend(False, 0, 8, info, after(suffix_q, *w), suffix_k, suffix_v, blocks)
    a_s, prompt_q, *w_came = lax.optimization_barrier((a_s, prompt_q, *w_came))

    w = join(w, w_came)
    w_came = gather_step(w, 3)
    near_s = to_near(a_s)
    a_p = attend(True, 0, 8, info, after(prompt_q, *w), prompt_k, prompt_v, blocks)
    a_s, near_s, a_p = lax.optimization_barrier((a_s, near_s, a_p))

    far_s = to_far(jnp.stack([a_s, near_s]))
    near_p = to_near(a_p)
    far_p = to_far(jnp.stack([a_p, near_p]))
    w_mate = [swap(after(a, a_p), 1) for a in w]
    w_came_mate = [swap(after(a, near_p), 1) for a in w_came]
    weights = [w[0], w_came[0], w[1], w_came[1],
               w_mate[0], w_came_mate[0], w_mate[1], w_came_mate[1]]
    total = project("first", info, [a_p, a_s, near_p, near_s], weights)
    out_s = project("rest", info, [far_s], weights, total[ROWS:])
    out_p = project("rest", info, [after(far_p, out_s)], weights, total[:ROWS])
    return out_p, out_s


def solution(mesh):
    both = P("sample", "tensor")
    return jax.shard_map(
        per_device,
        mesh=mesh,
        in_specs=(both,) * 6 + (P("sample"), P("sample"), both),
        out_specs=(both, both),
        check_vma=False,
    )
```

time: 134 us -> 125 us (0.933)
  the two profiles are of different devices: /device:TPU:37 before, /device:TPU:1 now
where the time goes in v1:
time: 125 us; the launch traced here: 123 us
  starting transfers between devices  56.6 us (45%)
  waiting for transfers between devices  40.4 us (32%)
  Pallas kernels  19.6 us (16%)
  between operations  2.35 us (2%)
  other arithmetic  1.93 us (2%)
  local copies, waits for them, and re-layouts  1.62 us (1%)
    ppermute x27, starting transfers between devices, swap(): return lax.ppermute(x, 'sample', [(s, s ^ masks[s & 1]) for s in range(64)])  44 us
    ppermute x4, waiting for transfers between devices, swap_tensor(): return lax.ppermute(x, ('sample', 'tensor'), pairs)  22.2 us
    ppermute x27, waiting for transfers between devices, swap(): return lax.ppermute(x, 'sample', [(s, s ^ masks[s & 1]) for s in range(64)])  18.3 us
    ppermute x4, starting transfers between devices, swap_tensor(): return lax.ppermute(x, ('sample', 'tensor'), pairs)  12.6 us
    pallas_call x2, Pallas kernels, attend(): pl.pallas_call(functools.partial(attend_kernel, is_prompt, first, count),...  11.1 us
    pallas_call x3, Pallas kernels, project(): pl.pallas_call(functools.partial(project_kernel, kind), out_shape=out_sha...  8.49 us
  transfers between devices with their start and end apart: 31, of which 18 were waited for; matrix products, arithmetic and copies ran while one was open for 3% of the time, Pallas kernels for 14%

profile of v1, /device:TPU:1, one launch (start us, length us, event | category | flops | bytes accessed | tf_op | source)
XLA Modules:
  0.0 122.6 jit_solution(16565279248332153718)
XLA Ops:
  0.6 2.6 %collective-permute-start = (bf16[128,128]{1,0:T(8,128)(2,1)}, bf16[128,128]{1,0:T(8,128)(2,1)S(1)}, u32[]{:S(2)}, u32[]{:S(2)}) collective-permute-start(bf16[128,128]{1,0:T(8,128)(2,1)} %own_k.3), channel_id=1, source_target_pairs={{0,8},{4,12},{8,0},{12,4},{16,24},{20,28},{24,16},{28,20},{32,40},... | collective-permute-start | bytes 98312 | tf_op jit(solution)/shard_map/ppermute | solution.py:46
  4.1 2.6 %collective-permute-start.4 = (bf16[1,128,256]{2,1,0:T(8,128)(2,1)S(1)}, bf16[1,128,256]{2,1,0:T(8,128)(2,1)S(1)}, u32[]{:S(2)}, u32[]{:S(2)}) collective-permute-start(bf16[1,128,256]{2,1,0:T(8,128)(2,1)S(1)} %maximum_bitcast_fusion.2), channel_id=1, source_target_pairs={{0,16},{4,52},{8,24},{12,60},{16,0},{20,36},{24,8},{28,44},{32,48}... | collective-permute-start | bytes 196616 | tf_op jit(solution)/shard_map/ppermute | solution.py:46
  9.1 1.5 %collective-permute-start.1 = (bf16[64,2048]{1,0:T(8,128)(2,1)}, bf16[64,2048]{1,0:T(8,128)(2,1)S(1)}, u32[]{:S(2)}, u32[]{:S(2)}) collective-permute-start(bf16[64,2048]{1,0:T(8,128)(2,1)} %param.17), channel_id=1, source_target_pairs={{0,8},{4,12},{8,0},{12,4},{16,24},{20,28},{24,16},{28,20},{32,40},... | collective-permute-start | bytes 786440 | tf_op jit(solution)/shard_map/ppermute | solution.py:46
  10.5 2.8 %collective-permute-start.10 = (bf16[1,128,256]{2,1,0:T(8,128)(2,1)S(1)}, bf16[1,128,256]{2,1,0:T(8,128)(2,1)S(1)}, u32[]{:S(2)}, u32[]{:S(2)}) collective-permute-start(bf16[1,128,256]{2,1,0:T(8,128)(2,1)S(1)} %maximum_bitcast_fusion.3), channel_id=1, source_target_pairs={{0,64},{4,196},{8,72},{12,204},{16,80},{20,212},{24,88},{28,220},{... | collective-permute-start | bytes 196616 | tf_op jit(solution)/shard_map/ppermute | solution.py:46
  13.5 1.5 %collective-permute-done.10 = bf16[1,128,256]{2,1,0:T(8,128)(2,1)S(1)} collective-permute-done((bf16[1,128,256]{2,1,0:T(8,128)(2,1)S(1)}, bf16[1,128,256]{2,1,0:T(8,128)(2,1)S(1)}, u32[]{:S(2)}, u32[]{:S(2)}) %collective-permute-start.10) | collective-permute-done | bytes 65568 | tf_op jit(solution)/shard_map/ppermute | solution.py:46
  15.4 1.6 %collective-permute-done.1 = bf16[64,2048]{1,0:T(8,128)(2,1)S(1)} collective-permute-done((bf16[64,2048]{1,0:T(8,128)(2,1)}, bf16[64,2048]{1,0:T(8,128)(2,1)S(1)}, u32[]{:S(2)}, u32[]{:S(2)}) %collective-permute-start.1) | collective-permute-done | bytes 262176 | tf_op jit(solution)/shard_map/ppermute | solution.py:46
  17.2 1.7 %collective-permute-done.11 = bf16[2,128,256]{2,1,0:T(8,128)(2,1)S(1)} collective-permute-done((bf16[2,128,256]{2,1,0:T(8,128)(2,1)S(1)}, bf16[2,128,256]{2,1,0:T(8,128)(2,1)S(1)}, u32[]{:S(2)}, u32[]{:S(2)}) %collective-permute-start.11) | collective-permute-done | bytes 131104 | tf_op jit(solution)/shard_map/ppermute | solution.py:46
  20.0 3.0 %collective-permute-start.7 = (bf16[1,2,64,1024]{3,2,1,0:T(8,128)(2,1)S(1)}, bf16[1,2,64,1024]{3,2,1,0:T(8,128)(2,1)S(1)}, u32[]{:S(2)}, u32[]{:S(2)}) collective-permute-start(bf16[1,2,64,1024]{3,2,1,0:T(8,128)(2,1)S(1)} %maximum_bitcast_fusion.1), channel_id=1, source_target_pairs={{0,64},{4,196},{8,72},{12,204},{16,80},{20,212},{24,88},{28,220},{... | collective-permute-start | bytes 786440 | tf_op jit(solution)/shard_map/ppermute | solution.py:46
  23.8 2.7 %collective-permute-done.12 = bf16[4,128,256]{2,1,0:T(8,128)(2,1)S(1)} collective-permute-done((bf16[4,128,256]{2,1,0:T(8,128)(2,1)S(1)}, bf16[4,128,256]{2,1,0:T(8,128)(2,1)S(1)}, u32[]{:S(2)}, u32[]{:S(2)}) %collective-permute-start.12) | collective-permute-done | bytes 262176 | tf_op jit(solution)/shard_map/ppermute | solution.py:46
  26.9 3.1 %collective-permute-done.6 = bf16[4,128,256]{2,1,0:T(8,128)(2,1)S(1)} collective-permute-done((bf16[4,128,256]{2,1,0:T(8,128)(2,1)S(1)}, bf16[4,128,256]{2,1,0:T(8,128)(2,1)S(1)}, u32[]{:S(2)}, u32[]{:S(2)}) %collective-permute-start.6) | collective-permute-done | bytes 262176 | tf_op jit(solution)/shard_map/ppermute | solution.py:46
  31.7 6.3 %collective-permute-start.15 = (bf16[8,128,256]{2,1,0:T(8,128)(2,1)S(1)}, bf16[8,128,256]{2,1,0:T(8,128)(2,1)S(1)}, u32[]{:S(2)}, u32[]{:S(2)}) collective-permute-start(bf16[8,128,256]{2,1,0:T(8,128)(2,1)S(1)} %pad_maximum_fusion.5), channel_id=1, source_target_pairs={{0,4},{4,0},{8,12},{12,8},{16,20},{20,16},{24,28},{28,24},{32,36},... | collective-permute-start | bytes 1572872 | tf_op jit(solution)/shard_map/ppermute | solution.py:46
  38.4 3.7 %collective-permute-start.17 = (bf16[8,128,256]{2,1,0:T(8,128)(2,1)S(1)}, bf16[8,128,256]{2,1,0:T(8,128)(2,1)S(1)}, u32[]{:S(2)}, u32[]{:S(2)}) collective-permute-start(bf16[8,128,256]{2,1,0:T(8,128)(2,1)S(1)} %pad_maximum_fusion.7), channel_id=1, source_target_pairs={{0,4},{4,0},{8,12},{12,8},{16,20},{20,16},{24,28},{28,24},{32,36},... | collective-permute-start | bytes 1572872 | tf_op jit(solution)/shard_map/ppermute | solution.py:46
  42.2 1.8 %collective-permute-done.14 = bf16[2,2,64,1024]{3,2,1,0:T(8,128)(2,1)S(1)} collective-permute-done((bf16[2,2,64,1024]{3,2,1,0:T(8,128)(2,1)S(1)}, bf16[2,2,64,1024]{3,2,1,0:T(8,128)(2,1)S(1)}, u32[]{:S(2)}, u32[]{:S(2)}) %collective-permute-start.14) | collective-permute-done | bytes 524320 | tf_op jit(solution)/shard_map/ppermute | solution.py:46
  44.0 2.7 %collective-permute-start.19 = (bf16[4,2,64,1024]{3,2,1,0:T(8,128)(2,1)S(1)}, bf16[4,2,64,1024]{3,2,1,0:T(8,128)(2,1)S(1)}, u32[]{:S(2)}, u32[]{:S(2)}) collective-permute-start(bf16[4,2,64,1024]{3,2,1,0:T(8,128)(2,1)S(1)} %pad_maximum_fusion.2), channel_id=1, source_target_pairs={{0,64},{4,196},{8,72},{12,204},{16,80},{20,212},{24,88},{28,220},{... | collective-permute-start | bytes 3145736 | tf_op jit(solution)/shard_map/ppermute | solution.py:46
  48.0 3.1 %collective-permute-start.16 = (bf16[8,128,256]{2,1,0:T(8,128)(2,1)S(1)}, bf16[8,128,256]{2,1,0:T(8,128)(2,1)S(1)}, u32[]{:S(2)}, u32[]{:S(2)}) collective-permute-start(bf16[8,128,256]{2,1,0:T(8,128)(2,1)S(1)} %collective-permute-done.8), channel_id=1, source_target_pairs={{0,4},{4,0},{8,12},{12,8},{16,20},{20,16},{24,28},{28,24},{32,36},... | collective-permute-start | bytes 1572872 | tf_op jit(solution)/shard_map/ppermute | solution.py:46
  53.4 8.2 %attend_suffix_0.1.refs_1_ = bf16[128,1024]{1,0:T(8,128)(2,1)S(1)} custom-call(s32[68]{0:T(128)S(1)} %concatenate.67.info, bf16[128,1024]{1,0:T(8,128)(2,1)S(1)} %copy-done.2, bf16[128,128]{1,0:T(8,128)(2,1)S(1)} %copy-done.4, bf16[128,128]{1,0:T(8,128)(2,1)S(1)} %copy-done.5, bf16[16,128,256]{2,1,0:T(8,128)(2,1)S(1)} %constant_dynamic-update-slice_fusion.refs_0_, ...), custom_call_target="tpu_custom_call" | custom-call | tf_op jit(solution)/shard_map/attend_suffix_0/pallas_call | solution.py:150
  62.3 1.7 %collective-permute-start.25 = (bf16[8,2,64,1024]{3,2,1,0:T(8,128)(2,1)S(1)}, bf16[8,2,64,1024]{3,2,1,0:T(8,128)(2,1)S(1)}, u32[]{:S(2)}, u32[]{:S(2)}) collective-permute-start(bf16[8,2,64,1024]{3,2,1,0:T(8,128)(2,1)S(1)} %pad_maximum_fusion.refs_4_.refs_2_), channel_id=1, source_target_pairs={{0,192},{4,68},{8,200},{12,76},{16,208},{20,84},{24,216},{28,92},{... | collective-permute-start | bytes 6291464 | tf_op jit(solution)/shard_map/ppermute | solution.py:46
  64.0 5.1 %collective-permute-start.21 = (bf16[128,1024]{1,0:T(8,128)(2,1)S(1)}, bf16[128,1024]{1,0:T(8,128)(2,1)S(1)}, u32[]{:S(2)}, u32[]{:S(2)}) collective-permute-start(bf16[128,1024]{1,0:T(8,128)(2,1)S(1)} %attend_suffix_0.1.refs_1_), channel_id=1, source_target_pairs={{0,1},{1,0},{2,3},{3,2},{4,7},{5,6},{6,5},{7,4},{8,9},{9,8},{10,11... | collective-permute-start | bytes 786440 | tf_op jit(solution)/shard_map/ppermute | solution.py:51
  69.1 2.9 %attend_prompt_0.1.refs_0_ = bf16[128,1024]{1,0:T(8,128)(2,1)S(1)} custom-call(s32[68]{0:T(128)S(1)} %concatenate.67.info, bf16[128,1024]{1,0:T(8,128)(2,1)S(1)} %copy-done.3, bf16[128,128]{1,0:T(8,128)(2,1)S(1)} %copy-done, bf16[128,128]{1,0:T(8,128)(2,1)S(1)} %copy-done.1, bf16[16,128,256]{2,1,0:T(8,128)(2,1)S(1)} %constant_dynamic-update-slice_fusion.refs_0_, ...), custom_call_target="tpu_custom_call" | custom-call | tf_op jit(solution)/shard_map/attend_prompt_0/pallas_call | solution.py:150
  72.1 3.2 %collective-permute-done.21.refs_3_ = bf16[128,1024]{1,0:T(8,128)(2,1)S(1)} collective-permute-done((bf16[128,1024]{1,0:T(8,128)(2,1)S(1)}, bf16[128,1024]{1,0:T(8,128)(2,1)S(1)}, u32[]{:S(2)}, u32[]{:S(2)}) %collective-permute-start.21) | collective-permute-done | bytes 262176 | tf_op jit(solution)/shard_map/ppermute | solution.py:51
  75.2 4.1 %collective-permute-start.22 = (bf16[128,1024]{1,0:T(8,128)(2,1)S(1)}, bf16[128,1024]{1,0:T(8,128)(2,1)S(1)}, u32[]{:S(2)}, u32[]{:S(2)}) collective-permute-start(bf16[128,1024]{1,0:T(8,128)(2,1)S(1)} %attend_prompt_0.1.refs_0_), channel_id=1, source_target_pairs={{0,1},{1,0},{2,3},{3,2},{4,7},{5,6},{6,5},{7,4},{8,9},{9,8},{10,11... | collective-permute-start | bytes 786440 | tf_op jit(solution)/shard_map/ppermute | solution.py:51
  79.4 1.8 %collective-permute-start.27 = (bf16[8,2,64,1024]{3,2,1,0:T(8,128)(2,1)S(1)}, bf16[8,2,64,1024]{3,2,1,0:T(8,128)(2,1)S(1)}, u32[]{:S(2)}, u32[]{:S(2)}) collective-permute-start(bf16[8,2,64,1024]{3,2,1,0:T(8,128)(2,1)S(1)} %pad_maximum_fusion.refs_4_.refs_2_), channel_id=1, source_target_pairs={{0,4},{4,0},{8,12},{12,8},{16,20},{20,16},{24,28},{28,24},{32,36},... | collective-permute-start | bytes 6291464 | tf_op jit(solution)/shard_map/ppermute | solution.py:46
  81.2 3.4 %collective-permute-done.22.refs_2_ = bf16[128,1024]{1,0:T(8,128)(2,1)S(1)} collective-permute-done((bf16[128,1024]{1,0:T(8,128)(2,1)S(1)}, bf16[128,1024]{1,0:T(8,128)(2,1)S(1)}, u32[]{:S(2)}, u32[]{:S(2)}) %collective-permute-start.22) | collective-permute-done | bytes 262176 | tf_op jit(solution)/shard_map/ppermute | solution.py:51
  84.6 2.6 %collective-permute-done.26.refs_7_.refs_5_ = bf16[8,2,64,1024]{3,2,1,0:T(8,128)(2,1)S(1)} collective-permute-done((bf16[8,2,64,1024]{3,2,1,0:T(8,128)(2,1)S(1)}, bf16[8,2,64,1024]{3,2,1,0:T(8,128)(2,1)S(1)}, u32[]{:S(2)}, u32[]{:S(2)}) %collective-permute-start.26) | collective-permute-done | bytes 2097184 | tf_op jit(solution)/shard_map/ppermute | solution.py:46
  87.2 4.0 %collective-permute-start.30 = (bf16[8,2,64,1024]{3,2,1,0:T(8,128)(2,1)S(1)}, bf16[8,2,64,1024]{3,2,1,0:T(8,128)(2,1)S(1)}, u32[]{:S(2)}, u32[]{:S(2)}) collective-permute-start(bf16[8,2,64,1024]{3,2,1,0:T(8,128)(2,1)S(1)} %collective-permute-done.26.refs_7_.refs_5_), channel_id=1, source_target_pairs={{0,4},{4,0},{8,12},{12,8},{16,20},{20,16},{24,28},{28,24},{32,36},... | collective-permute-start | bytes 6291464 | tf_op jit(solution)/shard_map/ppermute | solution.py:46
  91.3 3.2 %collective-permute-start.28 = (bf16[8,2,64,1024]{3,2,1,0:T(8,128)(2,1)S(1)}, bf16[8,2,64,1024]{3,2,1,0:T(8,128)(2,1)S(1)}, u32[]{:S(2)}, u32[]{:S(2)}) collective-permute-start(bf16[8,2,64,1024]{3,2,1,0:T(8,128)(2,1)S(1)} %collective-permute-done.25.refs_5_.refs_3_), channel_id=1, source_target_pairs={{0,4},{4,0},{8,12},{12,8},{16,20},{20,16},{24,28},{28,24},{32,36},... | collective-permute-start | bytes 6291464 | tf_op jit(solution)/shard_map/ppermute | solution.py:46
  94.5 3.1 %collective-permute-start.24 = (bf16[2,128,1024]{2,1,0:T(8,128)(2,1)S(1)}, bf16[2,128,1024]{2,1,0:T(8,128)(2,1)S(1)}, u32[]{:S(2)}, u32[]{:S(2)}) collective-permute-start(bf16[2,128,1024]{2,1,0:T(8,128)(2,1)S(1)} %pad_maximum_fusion.9), channel_id=1, source_target_pairs={{0,3},{1,2},{2,1},{3,0},{4,5},{5,4},{6,7},{7,6},{8,11},{9,10},{10,... | collective-permute-start | bytes 1572872 | tf_op jit(solution)/shard_map/ppermute | solution.py:51
  98.3 3.0 %project_first.1 = f32[256,2048]{1,0:T(8,128)S(1)} custom-call(s32[68]{0:T(128)S(1)} %concatenate.67.info, bf16[128,1024]{1,0:T(8,128)(2,1)S(1)} %attend_prompt_0.1.refs_0_, bf16[128,1024]{1,0:T(8,128)(2,1)S(1)} %attend_suffix_0.1.refs_1_, bf16[128,1024]{1,0:T(8,128)(2,1)S(1)} %collective-permute-done.22.refs_2_, ...), custom_call_target="tpu_custom_call" | custom-call | tf_op jit(solution)/shard_map/project_first/pallas_call | solution.py:200
  101.5 12.9 %collective-permute-done.24.refs_0_ = bf16[2,128,1024]{2,1,0:T(8,128)(2,1)S(1)} collective-permute-done((bf16[2,128,1024]{2,1,0:T(8,128)(2,1)S(1)}, bf16[2,128,1024]{2,1,0:T(8,128)(2,1)S(1)}, u32[]{:S(2)}, u32[]{:S(2)}) %collective-permute-start.24) | collective-permute-done | bytes 524320 | tf_op jit(solution)/shard_map/ppermute | solution.py:51
  114.4 2.8 %project_rest.2 = bf16[128,2048]{1,0:T(8,128)(2,1)} custom-call(s32[68]{0:T(128)S(1)} %concatenate.67.info, bf16[2,128,1024]{2,1,0:T(8,128)(2,1)S(1)} %collective-permute-done.24.refs_0_, f32[128,2048]{1,0:T(8,128)S(1)} %get-tuple-element.49.refs_1_, bf16[8,2,64,1024]{3,2,1,0:T(8,128)(2,1)S(1)} %pad_maximum_fusion.refs_4_.refs_2_, ...), custom_call_target="tpu_custom_call" | custom-call | tf_op jit(solution)/shard_map/project_rest/pallas_call | solution.py:200
  117.2 2.6 %collective-permute-done.23.refs_0_ = bf16[2,128,1024]{2,1,0:T(8,128)(2,1)S(1)} collective-permute-done((bf16[2,128,1024]{2,1,0:T(8,128)(2,1)S(1)}, bf16[2,128,1024]{2,1,0:T(8,128)(2,1)S(1)}, u32[]{:S(2)}, u32[]{:S(2)}) %collective-permute-start.23) | collective-permute-done | bytes 524320 | tf_op jit(solution)/shard_map/ppermute | solution.py:51
  119.8 2.8 %project_rest.3 = bf16[128,2048]{1,0:T(8,128)(2,1)} custom-call(s32[68]{0:T(128)S(1)} %concatenate.67.info, bf16[2,128,1024]{2,1,0:T(8,128)(2,1)S(1)} %collective-permute-done.23.refs_0_, f32[128,2048]{1,0:T(8,128)S(1)} %get-tuple-element.48.refs_1_, bf16[8,2,64,1024]{3,2,1,0:T(8,128)(2,1)S(1)} %pad_maximum_fusion.refs_4_.refs_2_, ...), custom_call_target="tpu_custom_call" | custom-call | tf_op jit(solution)/shard_map/project_rest/pallas_call | solution.py:200
  (85 shorter events, 12.2 us)
Async XLA Ops:
  0.6 8.4 %collective-permute-start = (bf16[128,128]{1,0:T(8,128)(2,1)}, bf16[128,128]{1,0:T(8,128)(2,1)S(1)}, u32[]{:S(2)}, u32[]{:S(2)}) collective-permute-start(bf16[128,128]{1,0:T(8,128)(2,1)} %own_k.3), channel_id=1, source_target_pairs={{0,8},{4,12},{8,0},{12,4},{16,24},{20,28},{24,16},{28,20},{32,40},... | collective-permute-start | bytes 98312 | tf_op jit(solution)/shard_map/ppermute | solution.py:46
  3.2 7.3 %collective-permute-start.9 = (bf16[128,128]{1,0:T(8,128)(2,1)}, bf16[128,128]{1,0:T(8,128)(2,1)S(1)}, u32[]{:S(2)}, u32[]{:S(2)}) collective-permute-start(bf16[128,128]{1,0:T(8,128)(2,1)} %own_v.3), channel_id=1, source_target_pairs={{0,8},{4,12},{8,0},{12,4},{16,24},{20,28},{24,16},{28,20},{32,40},... | collective-permute-start | bytes 98312 | tf_op jit(solution)/shard_map/ppermute | solution.py:46
  4.1 9.3 %collective-permute-start.4 = (bf16[1,128,256]{2,1,0:T(8,128)(2,1)S(1)}, bf16[1,128,256]{2,1,0:T(8,128)(2,1)S(1)}, u32[]{:S(2)}, u32[]{:S(2)}) collective-permute-start(bf16[1,128,256]{2,1,0:T(8,128)(2,1)S(1)} %maximum_bitcast_fusion.2), channel_id=1, source_target_pairs={{0,16},{4,52},{8,24},{12,60},{16,0},{20,36},{24,8},{28,44},{32,48}... | collective-permute-start | bytes 196616 | tf_op jit(solution)/shard_map/ppermute | solution.py:46
  9.1 8.0 %collective-permute-start.1 = (bf16[64,2048]{1,0:T(8,128)(2,1)}, bf16[64,2048]{1,0:T(8,128)(2,1)S(1)}, u32[]{:S(2)}, u32[]{:S(2)}) collective-permute-start(bf16[64,2048]{1,0:T(8,128)(2,1)} %param.17), channel_id=1, source_target_pairs={{0,8},{4,12},{8,0},{12,4},{16,24},{20,28},{24,16},{28,20},{32,40},... | collective-permute-start | bytes 786440 | tf_op jit(solution)/shard_map/ppermute | solution.py:46
  10.5 4.5 %collective-permute-start.10 = (bf16[1,128,256]{2,1,0:T(8,128)(2,1)S(1)}, bf16[1,128,256]{2,1,0:T(8,128)(2,1)S(1)}, u32[]{:S(2)}, u32[]{:S(2)}) collective-permute-start(bf16[1,128,256]{2,1,0:T(8,128)(2,1)S(1)} %maximum_bitcast_fusion.3), channel_id=1, source_target_pairs={{0,64},{4,196},{8,72},{12,204},{16,80},{20,212},{24,88},{28,220},{... | collective-permute-start | bytes 196616 | tf_op jit(solution)/shard_map/ppermute | solution.py:46
  13.4 9.7 %collective-permute-start.5 = (bf16[2,128,256]{2,1,0:T(8,128)(2,1)S(1)}, bf16[2,128,256]{2,1,0:T(8,128)(2,1)S(1)}, u32[]{:S(2)}, u32[]{:S(2)}) collective-permute-start(bf16[2,128,256]{2,1,0:T(8,128)(2,1)S(1)} %pad_maximum_fusion.12), channel_id=1, source_target_pairs={{0,48},{4,20},{8,56},{12,28},{16,32},{20,4},{24,40},{28,12},{32,16... | collective-permute-start | bytes 393224 | tf_op jit(solution)/shard_map/ppermute | solution.py:46
  15.0 3.9 %collective-permute-start.11 = (bf16[2,128,256]{2,1,0:T(8,128)(2,1)S(1)}, bf16[2,128,256]{2,1,0:T(8,128)(2,1)S(1)}, u32[]{:S(2)}, u32[]{:S(2)}) collective-permute-start(bf16[2,128,256]{2,1,0:T(8,128)(2,1)S(1)} %pad_maximum_fusion.13), channel_id=1, source_target_pairs={{0,192},{4,68},{8,200},{12,76},{16,208},{20,84},{24,216},{28,92},{... | collective-permute-start | bytes 393224 | tf_op jit(solution)/shard_map/ppermute | solution.py:46
  17.1 6.5 %collective-permute-start.2 = (bf16[1,2,64,1024]{3,2,1,0:T(8,128)(2,1)S(1)}, bf16[1,2,64,1024]{3,2,1,0:T(8,128)(2,1)S(1)}, u32[]{:S(2)}, u32[]{:S(2)}) collective-permute-start(bf16[1,2,64,1024]{3,2,1,0:T(8,128)(2,1)S(1)} %maximum_bitcast_fusion), channel_id=1, source_target_pairs={{0,16},{4,52},{8,24},{12,60},{16,0},{20,36},{24,8},{28,44},{32,48}... | collective-permute-start | bytes 786440 | tf_op jit(solution)/shard_map/ppermute | solution.py:46
  19.0 7.4 %collective-permute-start.12 = (bf16[4,128,256]{2,1,0:T(8,128)(2,1)S(1)}, bf16[4,128,256]{2,1,0:T(8,128)(2,1)S(1)}, u32[]{:S(2)}, u32[]{:S(2)}) collective-permute-start(bf16[4,128,256]{2,1,0:T(8,128)(2,1)S(1)} %pad_maximum_fusion.11), channel_id=1, source_target_pairs={{0,16},{4,52},{8,24},{12,60},{16,0},{20,36},{24,8},{28,44},{32,48}... | collective-permute-start | bytes 786440 | tf_op jit(solution)/shard_map/ppermute | solution.py:46
  20.0 6.8 %collective-permute-start.7 = (bf16[1,2,64,1024]{3,2,1,0:T(8,128)(2,1)S(1)}, bf16[1,2,64,1024]{3,2,1,0:T(8,128)(2,1)S(1)}, u32[]{:S(2)}, u32[]{:S(2)}) collective-permute-start(bf16[1,2,64,1024]{3,2,1,0:T(8,128)(2,1)S(1)} %maximum_bitcast_fusion.1), channel_id=1, source_target_pairs={{0,64},{4,196},{8,72},{12,204},{16,80},{20,212},{24,88},{28,220},{... | collective-permute-start | bytes 786440 | tf_op jit(solution)/shard_map/ppermute | solution.py:46
  23.1 6.8 %collective-permute-start.6 = (bf16[4,128,256]{2,1,0:T(8,128)(2,1)S(1)}, bf16[4,128,256]{2,1,0:T(8,128)(2,1)S(1)}, u32[]{:S(2)}, u32[]{:S(2)}) collective-permute-start(bf16[4,128,256]{2,1,0:T(8,128)(2,1)S(1)} %pad_maximum_fusion.10), channel_id=1, source_target_pairs={{0,64},{4,196},{8,72},{12,204},{16,80},{20,212},{24,88},{28,220},{... | collective-permute-start | bytes 786440 | tf_op jit(solution)/shard_map/ppermute | solution.py:46
  23.7 18.5 %collective-permute-start.3 = (bf16[2,2,64,1024]{3,2,1,0:T(8,128)(2,1)S(1)}, bf16[2,2,64,1024]{3,2,1,0:T(8,128)(2,1)S(1)}, u32[]{:S(2)}, u32[]{:S(2)}) collective-permute-start(bf16[2,2,64,1024]{3,2,1,0:T(8,128)(2,1)S(1)} %pad_maximum_fusion.4), channel_id=1, source_target_pairs={{0,48},{4,20},{8,56},{12,28},{16,32},{20,4},{24,40},{28,12},{32,16... | collective-permute-start | bytes 1572872 | tf_op jit(solution)/shard_map/ppermute | solution.py:46
  30.0 8.4 %collective-permute-start.8 = (bf16[8,128,256]{2,1,0:T(8,128)(2,1)S(1)}, bf16[8,128,256]{2,1,0:T(8,128)(2,1)S(1)}, u32[]{:S(2)}, u32[]{:S(2)}) collective-permute-start(bf16[8,128,256]{2,1,0:T(8,128)(2,1)S(1)} %pad_maximum_fusion.5), channel_id=1, source_target_pairs={{0,192},{4,68},{8,200},{12,76},{16,208},{20,84},{24,216},{28,92},{... | collective-permute-start | bytes 1572872 | tf_op jit(solution)/shard_map/ppermute | solution.py:46
  30.1 12.0 %collective-permute-start.13 = (bf16[8,128,256]{2,1,0:T(8,128)(2,1)S(1)}, bf16[8,128,256]{2,1,0:T(8,128)(2,1)S(1)}, u32[]{:S(2)}, u32[]{:S(2)}) collective-permute-start(bf16[8,128,256]{2,1,0:T(8,128)(2,1)S(1)} %pad_maximum_fusion.7), channel_id=1, source_target_pairs={{0,48},{4,20},{8,56},{12,28},{16,32},{20,4},{24,40},{28,12},{32,16... | collective-permute-start | bytes 1572872 | tf_op jit(solution)/shard_map/ppermute | solution.py:46
  30.2 13.8 %collective-permute-start.14 = (bf16[2,2,64,1024]{3,2,1,0:T(8,128)(2,1)S(1)}, bf16[2,2,64,1024]{3,2,1,0:T(8,128)(2,1)S(1)}, u32[]{:S(2)}, u32[]{:S(2)}) collective-permute-start(bf16[2,2,64,1024]{3,2,1,0:T(8,128)(2,1)S(1)} %pad_maximum_fusion.6), channel_id=1, source_target_pairs={{0,192},{4,68},{8,200},{12,76},{16,208},{20,84},{24,216},{28,92},{... | collective-permute-start | bytes 1572872 | tf_op jit(solution)/shard_map/ppermute | solution.py:46
  31.7 19.4 %collective-permute-start.15 = (bf16[8,128,256]{2,1,0:T(8,128)(2,1)S(1)}, bf16[8,128,256]{2,1,0:T(8,128)(2,1)S(1)}, u32[]{:S(2)}, u32[]{:S(2)}) collective-permute-start(bf16[8,128,256]{2,1,0:T(8,128)(2,1)S(1)} %pad_maximum_fusion.5), channel_id=1, source_target_pairs={{0,4},{4,0},{8,12},{12,8},{16,20},{20,16},{24,28},{28,24},{32,36},... | collective-permute-start | bytes 1572872 | tf_op jit(solution)/shard_map/ppermute | solution.py:46
  38.4 13.0 %collective-permute-start.17 = (bf16[8,128,256]{2,1,0:T(8,128)(2,1)S(1)}, bf16[8,128,256]{2,1,0:T(8,128)(2,1)S(1)}, u32[]{:S(2)}, u32[]{:S(2)}) collective-permute-start(bf16[8,128,256]{2,1,0:T(8,128)(2,1)S(1)} %pad_maximum_fusion.7), channel_id=1, source_target_pairs={{0,4},{4,0},{8,12},{12,8},{16,20},{20,16},{24,28},{28,24},{32,36},... | collective-permute-start | bytes 1572872 | tf_op jit(solution)/shard_map/ppermute | solution.py:46
  44.0 17.6 %collective-permute-start.19 = (bf16[4,2,64,1024]{3,2,1,0:T(8,128)(2,1)S(1)}, bf16[4,2,64,1024]{3,2,1,0:T(8,128)(2,1)S(1)}, u32[]{:S(2)}, u32[]{:S(2)}) collective-permute-start(bf16[4,2,64,1024]{3,2,1,0:T(8,128)(2,1)S(1)} %pad_maximum_fusion.2), channel_id=1, source_target_pairs={{0,64},{4,196},{8,72},{12,204},{16,80},{20,212},{24,88},{28,220},{... | collective-permute-start | bytes 3145736 | tf_op jit(solution)/shard_map/ppermute | solution.py:46
  46.8 14.9 %collective-permute-start.20 = (bf16[4,2,64,1024]{3,2,1,0:T(8,128)(2,1)S(1)}, bf16[4,2,64,1024]{3,2,1,0:T(8,128)(2,1)S(1)}, u32[]{:S(2)}, u32[]{:S(2)}) collective-permute-start(bf16[4,2,64,1024]{3,2,1,0:T(8,128)(2,1)S(1)} %pad_maximum_fusion.3), channel_id=1, source_target_pairs={{0,16},{4,52},{8,24},{12,60},{16,0},{20,36},{24,8},{28,44},{32,48}... | collective-permute-start | bytes 3145736 | tf_op jit(solution)/shard_map/ppermute | solution.py:46
  48.0 4.6 %collective-permute-start.16 = (bf16[8,128,256]{2,1,0:T(8,128)(2,1)S(1)}, bf16[8,128,256]{2,1,0:T(8,128)(2,1)S(1)}, u32[]{:S(2)}, u32[]{:S(2)}) collective-permute-start(bf16[8,128,256]{2,1,0:T(8,128)(2,1)S(1)} %collective-permute-done.8), channel_id=1, source_target_pairs={{0,4},{4,0},{8,12},{12,8},{16,20},{20,16},{24,28},{28,24},{32,36},... | collective-permute-start | bytes 1572872 | tf_op jit(solution)/shard_map/ppermute | solution.py:46
  51.1 2.3 %collective-permute-start.18 = (bf16[8,128,256]{2,1,0:T(8,128)(2,1)S(1)}, bf16[8,128,256]{2,1,0:T(8,128)(2,1)S(1)}, u32[]{:S(2)}, u32[]{:S(2)}) collective-permute-start(bf16[8,128,256]{2,1,0:T(8,128)(2,1)S(1)} %collective-permute-done.13), channel_id=1, source_target_pairs={{0,4},{4,0},{8,12},{12,8},{16,20},{20,16},{24,28},{28,24},{32,36},... | collective-permute-start | bytes 1572872 | tf_op jit(solution)/shard_map/ppermute | solution.py:46
  61.9 7.2 %copy-start.3 = (bf16[128,1024]{1,0:T(8,128)(2,1)S(1)}, bf16[128,1024]{1,0:T(8,128)(2,1)}, u32[]{:S(2)}) copy-start(bf16[128,1024]{1,0:T(8,128)(2,1)} %q.1) | copy-start | bytes 786436
  62.0 25.3 %collective-permute-start.26 = (bf16[8,2,64,1024]{3,2,1,0:T(8,128)(2,1)S(1)}, bf16[8,2,64,1024]{3,2,1,0:T(8,128)(2,1)S(1)}, u32[]{:S(2)}, u32[]{:S(2)}) collective-permute-start(bf16[8,2,64,1024]{3,2,1,0:T(8,128)(2,1)S(1)} %pad_maximum_fusion.1.refs_6_.refs_4_), channel_id=1, source_target_pairs={{0,48},{4,20},{8,56},{12,28},{16,32},{20,4},{24,40},{28,12},{32,16... | collective-permute-start | bytes 6291464 | tf_op jit(solution)/shard_map/ppermute | solution.py:46
  62.3 29.0 %collective-permute-start.25 = (bf16[8,2,64,1024]{3,2,1,0:T(8,128)(2,1)S(1)}, bf16[8,2,64,1024]{3,2,1,0:T(8,128)(2,1)S(1)}, u32[]{:S(2)}, u32[]{:S(2)}) collective-permute-start(bf16[8,2,64,1024]{3,2,1,0:T(8,128)(2,1)S(1)} %pad_maximum_fusion.refs_4_.refs_2_), channel_id=1, source_target_pairs={{0,192},{4,68},{8,200},{12,76},{16,208},{20,84},{24,216},{28,92},{... | collective-permute-start | bytes 6291464 | tf_op jit(solution)/shard_map/ppermute | solution.py:46
  64.0 11.2 %collective-permute-start.21 = (bf16[128,1024]{1,0:T(8,128)(2,1)S(1)}, bf16[128,1024]{1,0:T(8,128)(2,1)S(1)}, u32[]{:S(2)}, u32[]{:S(2)}) collective-permute-start(bf16[128,1024]{1,0:T(8,128)(2,1)S(1)} %attend_suffix_0.1.refs_1_), channel_id=1, source_target_pairs={{0,1},{1,0},{2,3},{3,2},{4,7},{5,6},{6,5},{7,4},{8,9},{9,8},{10,11... | collective-permute-start | bytes 786440 | tf_op jit(solution)/shard_map/ppermute | solution.py:51
  75.2 9.4 %collective-permute-start.22 = (bf16[128,1024]{1,0:T(8,128)(2,1)S(1)}, bf16[128,1024]{1,0:T(8,128)(2,1)S(1)}, u32[]{:S(2)}, u32[]{:S(2)}) collective-permute-start(bf16[128,1024]{1,0:T(8,128)(2,1)S(1)} %attend_prompt_0.1.refs_0_), channel_id=1, source_target_pairs={{0,1},{1,0},{2,3},{3,2},{4,7},{5,6},{6,5},{7,4},{8,9},{9,8},{10,11... | collective-permute-start | bytes 786440 | tf_op jit(solution)/shard_map/ppermute | solution.py:51
  79.4 18.3 %collective-permute-start.27 = (bf16[8,2,64,1024]{3,2,1,0:T(8,128)(2,1)S(1)}, bf16[8,2,64,1024]{3,2,1,0:T(8,128)(2,1)S(1)}, u32[]{:S(2)}, u32[]{:S(2)}) collective-permute-start(bf16[8,2,64,1024]{3,2,1,0:T(8,128)(2,1)S(1)} %pad_maximum_fusion.refs_4_.refs_2_), channel_id=1, source_target_pairs={{0,4},{4,0},{8,12},{12,8},{16,20},{20,16},{24,28},{28,24},{32,36},... | collective-permute-start | bytes 6291464 | tf_op jit(solution)/shard_map/ppermute | solution.py:46
  81.2 16.8 %collective-permute-start.29 = (bf16[8,2,64,1024]{3,2,1,0:T(8,128)(2,1)S(1)}, bf16[8,2,64,1024]{3,2,1,0:T(8,128)(2,1)S(1)}, u32[]{:S(2)}, u32[]{:S(2)}) collective-permute-start(bf16[8,2,64,1024]{3,2,1,0:T(8,128)(2,1)S(1)} %pad_maximum_fusion.1.refs_6_.refs_4_), channel_id=1, source_target_pairs={{0,4},{4,0},{8,12},{12,8},{16,20},{20,16},{24,28},{28,24},{32,36},... | collective-permute-start | bytes 6291464 | tf_op jit(solution)/shard_map/ppermute | solution.py:46
  87.2 10.8 %collective-permute-start.30 = (bf16[8,2,64,1024]{3,2,1,0:T(8,128)(2,1)S(1)}, bf16[8,2,64,1024]{3,2,1,0:T(8,128)(2,1)S(1)}, u32[]{:S(2)}, u32[]{:S(2)}) collective-permute-start(bf16[8,2,64,1024]{3,2,1,0:T(8,128)(2,1)S(1)} %collective-permute-done.26.refs_7_.refs_5_), channel_id=1, source_target_pairs={{0,4},{4,0},{8,12},{12,8},{16,20},{20,16},{24,28},{28,24},{32,36},... | collective-permute-start | bytes 6291464 | tf_op jit(solution)/shard_map/ppermute | solution.py:46
  91.3 7.0 %collective-permute-start.28 = (bf16[8,2,64,1024]{3,2,1,0:T(8,128)(2,1)S(1)}, bf16[8,2,64,1024]{3,2,1,0:T(8,128)(2,1)S(1)}, u32[]{:S(2)}, u32[]{:S(2)}) collective-permute-start(bf16[8,2,64,1024]{3,2,1,0:T(8,128)(2,1)S(1)} %collective-permute-done.25.refs_5_.refs_3_), channel_id=1, source_target_pairs={{0,4},{4,0},{8,12},{12,8},{16,20},{20,16},{24,28},{28,24},{32,36},... | collective-permute-start | bytes 6291464 | tf_op jit(solution)/shard_map/ppermute | solution.py:46
  94.5 19.9 %collective-permute-start.24 = (bf16[2,128,1024]{2,1,0:T(8,128)(2,1)S(1)}, bf16[2,128,1024]{2,1,0:T(8,128)(2,1)S(1)}, u32[]{:S(2)}, u32[]{:S(2)}) collective-permute-start(bf16[2,128,1024]{2,1,0:T(8,128)(2,1)S(1)} %pad_maximum_fusion.9), channel_id=1, source_target_pairs={{0,3},{1,2},{2,1},{3,0},{4,5},{5,4},{6,7},{7,6},{8,11},{9,10},{10,... | collective-permute-start | bytes 1572872 | tf_op jit(solution)/shard_map/ppermute | solution.py:51
  97.7 22.1 %collective-permute-start.23 = (bf16[2,128,1024]{2,1,0:T(8,128)(2,1)S(1)}, bf16[2,128,1024]{2,1,0:T(8,128)(2,1)S(1)}, u32[]{:S(2)}, u32[]{:S(2)}) collective-permute-start(bf16[2,128,1024]{2,1,0:T(8,128)(2,1)S(1)} %pad_maximum_fusion.8), channel_id=1, source_target_pairs={{0,3},{1,2},{2,1},{3,0},{4,5},{5,4},{6,7},{7,6},{8,11},{9,10},{10,... | collective-permute-start | bytes 1572872 | tf_op jit(solution)/shard_map/ppermute | solution.py:51
  (5 other events, 19.9 us)

commit v2 on v1

--- a/solution.py
+++ b/solution.py
@@ -161,21 +161,19 @@
     )(info, q, own_k, own_v, *blocks)
 
 
-def project_kernel(kind, info, *refs):
-    if kind == "first":
-        heads, weights, (out,) = refs[:4], refs[4:12], refs[12:]
-    else:
-        heads, total, weights, (out,) = refs[0], refs[1], refs[2:10], refs[10:]
+def project_kernel(info, a_p, a_s, near_s, mixed, far_p, *refs):
+    weights, (out_p, out_s) = refs[:8], refs[8:]
     core, tensor = info[0] & 1, info[3]
     near = jnp.where(core == 0, 1, 3)
-    if kind == "first":
-        pieces = [(tensor, jnp.concatenate([heads[0][...], heads[1][...]], axis=0)),
-                  (tensor ^ near, jnp.concatenate([heads[2][...], heads[3][...]], axis=0))]
-    else:
-        pieces = [(tensor ^ near ^ 2, heads[0]), (tensor ^ 2, heads[1])]
+    pieces = [
+        (quarter, jnp.concatenate(rows, axis=0)) for quarter, rows in (
+            (tensor, (a_p[...], a_s[...])),
+            (tensor ^ near, (far_p[0], near_s[...])),
+            (tensor ^ near ^ 2, (mixed[2], mixed[0])),
+            (tensor ^ 2, (far_p[1], mixed[1])))]
     for piece in range(2):
         lanes = slice(piece * 1024, (piece + 1) * 1024)
-        sums = None if kind == "first" else total[:, lanes]
+        sums = None
         for quarter, rows in pieces:
             held = []
             for x in range(4):
@@ -188,22 +186,19 @@
             part = jnp.dot(
                 rows, jnp.concatenate(held, axis=0), preferred_element_type=jnp.float32)
             sums = part if sums is None else sums + part
-        out[:, lanes] = sums.astype(out.dtype)
-
-
-def project(kind, info, heads, weights, total=None):
-    if kind == "first":
-        out_shape = jax.ShapeDtypeStruct((2 * ROWS, 2048), jnp.float32)
-    else:
-        out_shape = jax.ShapeDtypeStruct((ROWS, 2048), jnp.bfloat16)
-    args = [info, *heads] + ([] if kind == "first" else [total]) + list(weights)
+        out_p[:, lanes] = sums[:ROWS].astype(jnp.bfloat16)
+        out_s[:, lanes] = sums[ROWS:].astype(jnp.bfloat16)
+
+
+def project(info, heads, weights):
+    args = [info, *heads, *weights]
     return pl.pallas_call(
-        functools.partial(project_kernel, kind),
-        out_shape=out_shape,
+        project_kernel,
+        out_shape=[jax.ShapeDtypeStruct((ROWS, 2048), jnp.bfloat16)] * 2,
         in_specs=[SMEM] + [VMEM] * (len(args) - 1),
-        out_specs=VMEM,
+        out_specs=[VMEM] * 2,
         compiler_params=pltpu.CompilerParams(vmem_limit_bytes=24 << 20),
-        name="project_" + kind,
+        name="project",
     )(*args)
 
 
@@ -216,12 +211,12 @@
         slot_table(me)])
 
     other_k, other_v = swap(prompt_k, 2), swap(prompt_v, 2)
-    kv = [jnp.concatenate([prompt_k, prompt_v], axis=1)[None],
-          jnp.concatenate([other_k, other_v], axis=1)[None]]
+    own = lax.optimization_barrier(jnp.concatenate([prompt_k, prompt_v], axis=1))
+    kv = [own[None], jnp.concatenate([other_k, other_v], axis=1)[None]]
     others = swap(after(out_weight, other_k), 2)
     kv = join(kv, gather_step(kv, 0))
     kv = join(kv, gather_step(kv, 1))
-    others, info = lax.optimization_barrier((others, info))
+    others, info, out_weight, _ = lax.optimization_barrier((others, info, out_weight, kv[0]))
     w = [jnp.stack([part[:, lanes] for part in (out_weight, others)])[None]
          for lanes in (slice(0, 1024), slice(1024, 2048))]
     w_came = gather_step(w, 0)
@@ -232,35 +227,35 @@
     kv_mate = [swap(a, 1) for a in kv]
     came_mate = [swap(a, 1) for a in came]
     blocks = [*join(kv, came), *join(kv_mate, came_mate)]
-    w = join(w, [after(a, *came) for a in w_came])
-
-    def to_near(a):
-        return swap_tensor(a, (1, 3))
-
-    def to_far(a):
-        return swap_tensor(a, (3, 1))
-
-    w_came = gather_step(w, 2)
-    a_s = attend(False, 0, 8, info, after(suffix_q, *w), suffix_k, suffix_v, blocks)
+
+    a_s = attend(False, 0, 8, info, suffix_q, suffix_k, suffix_v, blocks)
     a_s, prompt_q, *w_came = lax.optimization_barrier((a_s, prompt_q, *w_came))
 
     w = join(w, w_came)
-    w_came = gather_step(w, 3)
-    near_s = to_near(a_s)
+    w_3 = gather_step(w, 2)
+    near_s = swap_tensor(a_s, (1, 3))
     a_p = attend(True, 0, 8, info, after(prompt_q, *w), prompt_k, prompt_v, blocks)
-    a_s, near_s, a_p = lax.optimization_barrier((a_s, near_s, a_p))
-
-    far_s = to_far(jnp.stack([a_s, near_s]))
-    near_p = to_near(a_p)
-    far_p = to_far(jnp.stack([a_p, near_p]))
-    w_mate = [swap(after(a, a_p), 1) for a in w]
-    w_came_mate = [swap(after(a, near_p), 1) for a in w_came]
+    a_s, near_s, a_p, *w = lax.optimization_barrier((a_s, near_s, a_p, *w))
+
+    mixed = swap_tensor(jnp.stack([a_s, near_s, a_p]), (3, 1))
+    w_4 = gather_step(w, 3)
+    mixed, *w = lax.optimization_barrier((mixed, *w, *w_3, *w_4))
+    w, w_3, w_4 = w[:2], w[2:4], w[4:]
+
+    far_p = swap_tensor(jnp.stack([a_p, mixed[2]]), (1, 3))
+    w_5 = gather_step(w_3, 3)
+    w = join(w, w_3)
+    w_mate = [swap(a, 1) for a in w]
+    far_p, *w_mate = lax.optimization_barrier((far_p, *w_mate))
+
+    *w_5, _ = lax.optimization_barrier((*w_5, far_p))
+    w_5_mate = [swap(a, 1) for a in w_5]
+    w_4_mate = [swap(after(a, *w_5), 1) for a in w_4]
+    w_came = join(w_4, w_5)
+    w_came_mate = join(w_4_mate, w_5_mate)
     weights = [w[0], w_came[0], w[1], w_came[1],
                w_mate[0], w_came_mate[0], w_mate[1], w_came_mate[1]]
-    total = project("first", info, [a_p, a_s, near_p, near_s], weights)
-    out_s = project("rest", info, [far_s], weights, total[ROWS:])
-    out_p = project("rest", info, [after(far_p, out_s)], weights, total[:ROWS])
-    return out_p, out_s
+    return tuple(project(info, [a_p, a_s, near_s, mixed, far_p], weights))
 
 
 def solution(mesh):

time: 125 us -> 121 us (0.968); the launches traced: 123 us -> 121 us
  waiting for transfers between devices: 40.4 us -> 48.7 us
  starting transfers between devices: 56.6 us -> 48.8 us
  Pallas kernels: 19.6 us -> 17.2 us
    ppermute x27 -> x31, starting transfers between devices: 44 us -> 38 us  [swap(): return lax.ppermute(x, 'sample', [(s, s ^ masks[s & 1]) for s in range(64)])]
    ppermute x4 -> x3, waiting for transfers between devices: 22.2 us -> 27.6 us  [swap_tensor(): return lax.ppermute(x, ('sample', 'tensor'), pairs)]
    ppermute x27 -> x31, waiting for transfers between devices: 18.3 us -> 21.1 us  [swap(): return lax.ppermute(x, 'sample', [(s, s ^ masks[s & 1]) for s in range(64)])]
    pallas_call x3 -> x1, Pallas kernels: 8.49 us -> 6.19 us  [project(): pl.pallas_call(project_kernel, out_shape=[jax.ShapeDtypeStruct((ROWS, 204...]
    ppermute x4 -> x3, starting transfers between devices: 12.6 us -> 10.8 us  [swap_tensor(): return lax.ppermute(x, ('sample', 'tensor'), pairs)]
  transfers between devices with their start and end apart: 31 -> 34, of which waited for: 18 -> 15; matrix products, arithmetic and copies ran while one was open for 3% -> 3% of each run, Pallas kernels for 14% -> 9%
where the time goes in v2:
time: 121 us
  starting transfers between devices  48.8 us (40%)
  waiting for transfers between devices  48.7 us (40%)
  Pallas kernels  17.2 us (14%)
  between operations  2.44 us (2%)
  other arithmetic  2.27 us (2%)
  local copies, waits for them, and re-layouts  1.71 us (1%)
    ppermute x31, starting transfers between devices, swap(): return lax.ppermute(x, 'sample', [(s, s ^ masks[s & 1]) for s in range(64)])  38 us
    ppermute x3, waiting for transfers between devices, swap_tensor(): return lax.ppermute(x, ('sample', 'tensor'), pairs)  27.6 us
    ppermute x31, waiting for transfers between devices, swap(): return lax.ppermute(x, 'sample', [(s, s ^ masks[s & 1]) for s in range(64)])  21.1 us
    pallas_call x2, Pallas kernels, attend(): pl.pallas_call(functools.partial(attend_kernel, is_prompt, first, count),...  11 us
    ppermute x3, starting transfers between devices, swap_tensor(): return lax.ppermute(x, ('sample', 'tensor'), pairs)  10.8 us
    pallas_call x1, Pallas kernels, project(): pl.pallas_call(project_kernel, out_shape=[jax.ShapeDtypeStruct((ROWS, 204...  6.19 us
  transfers between devices with their start and end apart: 34, of which 15 were waited for; matrix products, arithmetic and copies ran while one was open for 3% of the time, Pallas kernels for 9%

profile of v2, /device:TPU:1, one launch (start us, length us, event | category | flops | bytes accessed | tf_op | source)
XLA Modules:
  0.0 121.1 jit_solution(6988642300416906836)
XLA Ops:
  0.6 2.6 %collective-permute-start = (bf16[128,128]{1,0:T(8,128)(2,1)}, bf16[128,128]{1,0:T(8,128)(2,1)S(1)}, u32[]{:S(2)}, u32[]{:S(2)}) collective-permute-start(bf16[128,128]{1,0:T(8,128)(2,1)} %own_k.3), channel_id=1, source_target_pairs={{0,8},{4,12},{8,0},{12,4},{16,24},{20,28},{24,16},{28,20},{32,40},... | collective-permute-start | bytes 98312 | tf_op jit(solution)/shard_map/ppermute | solution.py:46
  4.1 2.6 %collective-permute-start.2 = (bf16[1,128,256]{2,1,0:T(8,128)(2,1)S(1)}, bf16[1,128,256]{2,1,0:T(8,128)(2,1)S(1)}, u32[]{:S(2)}, u32[]{:S(2)}) collective-permute-start(bf16[1,128,256]{2,1,0:T(8,128)(2,1)S(1)} %bitcast.27), channel_id=1, source_target_pairs={{0,16},{4,52},{8,24},{12,60},{16,0},{20,36},{24,8},{28,44},{32,48}... | collective-permute-start | bytes 196616 | tf_op jit(solution)/shard_map/ppermute | solution.py:46
  6.7 2.8 %collective-permute-start.9 = (bf16[1,128,256]{2,1,0:T(8,128)(2,1)S(1)}, bf16[1,128,256]{2,1,0:T(8,128)(2,1)S(1)}, u32[]{:S(2)}, u32[]{:S(2)}) collective-permute-start(bf16[1,128,256]{2,1,0:T(8,128)(2,1)S(1)} %maximum_bitcast_fusion.2), channel_id=1, source_target_pairs={{0,64},{4,196},{8,72},{12,204},{16,80},{20,212},{24,88},{28,220},{... | collective-permute-start | bytes 196616 | tf_op jit(solution)/shard_map/ppermute | solution.py:46
  9.5 1.4 %collective-permute-start.1 = (bf16[64,2048]{1,0:T(8,128)(2,1)}, bf16[64,2048]{1,0:T(8,128)(2,1)S(1)}, u32[]{:S(2)}, u32[]{:S(2)}) collective-permute-start(bf16[64,2048]{1,0:T(8,128)(2,1)} %param.17), channel_id=1, source_target_pairs={{0,8},{4,12},{8,0},{12,4},{16,24},{20,28},{24,16},{28,20},{32,40},... | collective-permute-start | bytes 786440 | tf_op jit(solution)/shard_map/ppermute | solution.py:46
  12.6 2.6 %collective-permute-done.3 = bf16[2,128,256]{2,1,0:T(8,128)(2,1)S(1)} collective-permute-done((bf16[2,128,256]{2,1,0:T(8,128)(2,1)S(1)}, bf16[2,128,256]{2,1,0:T(8,128)(2,1)S(1)}, u32[]{:S(2)}, u32[]{:S(2)}) %collective-permute-start.3) | collective-permute-done | bytes 131104 | tf_op jit(solution)/shard_map/ppermute | solution.py:46
  15.2 2.1 %collective-permute-done.1 = bf16[64,2048]{1,0:T(8,128)(2,1)S(1)} collective-permute-done((bf16[64,2048]{1,0:T(8,128)(2,1)}, bf16[64,2048]{1,0:T(8,128)(2,1)S(1)}, u32[]{:S(2)}, u32[]{:S(2)}) %collective-permute-start.1) | collective-permute-done | bytes 262176 | tf_op jit(solution)/shard_map/ppermute | solution.py:46
  18.4 2.7 %collective-permute-start.6 = (bf16[1,2,64,1024]{3,2,1,0:T(8,128)(2,1)S(1)}, bf16[1,2,64,1024]{3,2,1,0:T(8,128)(2,1)S(1)}, u32[]{:S(2)}, u32[]{:S(2)}) collective-permute-start(bf16[1,2,64,1024]{3,2,1,0:T(8,128)(2,1)S(1)} %maximum_bitcast_fusion.1), channel_id=1, source_target_pairs={{0,64},{4,196},{8,72},{12,204},{16,80},{20,212},{24,88},{28,220},{... | collective-permute-start | bytes 786440 | tf_op jit(solution)/shard_map/ppermute | solution.py:46
  21.2 1.3 %collective-permute-start.5 = (bf16[1,2,64,1024]{3,2,1,0:T(8,128)(2,1)S(1)}, bf16[1,2,64,1024]{3,2,1,0:T(8,128)(2,1)S(1)}, u32[]{:S(2)}, u32[]{:S(2)}) collective-permute-start(bf16[1,2,64,1024]{3,2,1,0:T(8,128)(2,1)S(1)} %maximum_bitcast_fusion), channel_id=1, source_target_pairs={{0,16},{4,52},{8,24},{12,60},{16,0},{20,36},{24,8},{28,44},{32,48}... | collective-permute-start | bytes 786440 | tf_op jit(solution)/shard_map/ppermute | solution.py:46
  22.5 1.4 %collective-permute-start.11 = (bf16[4,128,256]{2,1,0:T(8,128)(2,1)S(1)}, bf16[4,128,256]{2,1,0:T(8,128)(2,1)S(1)}, u32[]{:S(2)}, u32[]{:S(2)}) collective-permute-start(bf16[4,128,256]{2,1,0:T(8,128)(2,1)S(1)} %pad_maximum_fusion.13), channel_id=1, source_target_pairs={{0,16},{4,52},{8,24},{12,60},{16,0},{20,36},{24,8},{28,44},{32,48}... | collective-permute-start | bytes 786440 | tf_op jit(solution)/shard_map/ppermute | solution.py:46
  26.2 1.5 %collective-permute-done.6 = bf16[1,2,64,1024]{3,2,1,0:T(8,128)(2,1)S(1)} collective-permute-done((bf16[1,2,64,1024]{3,2,1,0:T(8,128)(2,1)S(1)}, bf16[1,2,64,1024]{3,2,1,0:T(8,128)(2,1)S(1)}, u32[]{:S(2)}, u32[]{:S(2)}) %collective-permute-start.6) | collective-permute-done | bytes 262176 | tf_op jit(solution)/shard_map/ppermute | solution.py:46
  27.9 2.6 %collective-permute-done.11 = bf16[4,128,256]{2,1,0:T(8,128)(2,1)S(1)} collective-permute-done((bf16[4,128,256]{2,1,0:T(8,128)(2,1)S(1)}, bf16[4,128,256]{2,1,0:T(8,128)(2,1)S(1)}, u32[]{:S(2)}, u32[]{:S(2)}) %collective-permute-start.11) | collective-permute-done | bytes 262176 | tf_op jit(solution)/shard_map/ppermute | solution.py:46
  30.6 2.7 %collective-permute-start.15 = (bf16[8,128,256]{2,1,0:T(8,128)(2,1)S(1)}, bf16[8,128,256]{2,1,0:T(8,128)(2,1)S(1)}, u32[]{:S(2)}, u32[]{:S(2)}) collective-permute-start(bf16[8,128,256]{2,1,0:T(8,128)(2,1)S(1)} %pad_maximum_fusion.10), channel_id=1, source_target_pairs={{0,4},{4,0},{8,12},{12,8},{16,20},{20,16},{24,28},{28,24},{32,36},... | collective-permute-start | bytes 1572872 | tf_op jit(solution)/shard_map/ppermute | solution.py:46
  33.5 2.7 %collective-permute-done.7 = bf16[8,128,256]{2,1,0:T(8,128)(2,1)S(1)} collective-permute-done((bf16[8,128,256]{2,1,0:T(8,128)(2,1)S(1)}, bf16[8,128,256]{2,1,0:T(8,128)(2,1)S(1)}, u32[]{:S(2)}, u32[]{:S(2)}) %collective-permute-start.7) | collective-permute-done | bytes 524320 | tf_op jit(solution)/shard_map/ppermute | solution.py:46
  36.2 3.2 %collective-permute-start.14 = (bf16[8,128,256]{2,1,0:T(8,128)(2,1)S(1)}, bf16[8,128,256]{2,1,0:T(8,128)(2,1)S(1)}, u32[]{:S(2)}, u32[]{:S(2)}) collective-permute-start(bf16[8,128,256]{2,1,0:T(8,128)(2,1)S(1)} %collective-permute-done.7), channel_id=1, source_target_pairs={{0,4},{4,0},{8,12},{12,8},{16,20},{20,16},{24,28},{28,24},{32,36},... | collective-permute-start | bytes 1572872 | tf_op jit(solution)/shard_map/ppermute | solution.py:46
  39.6 1.9 %collective-permute-start.16 = (bf16[8,128,256]{2,1,0:T(8,128)(2,1)S(1)}, bf16[8,128,256]{2,1,0:T(8,128)(2,1)S(1)}, u32[]{:S(2)}, u32[]{:S(2)}) collective-permute-start(bf16[8,128,256]{2,1,0:T(8,128)(2,1)S(1)} %collective-permute-done.12), channel_id=1, source_target_pairs={{0,4},{4,0},{8,12},{12,8},{16,20},{20,16},{24,28},{28,24},{32,36},... | collective-permute-start | bytes 1572872 | tf_op jit(solution)/shard_map/ppermute | solution.py:46
  43.1 8.0 %attend_suffix_0.1.a_s = bf16[128,1024]{1,0:T(8,128)(2,1)S(1)} custom-call(s32[68]{0:T(128)S(1)} %concatenate.77.info, bf16[128,1024]{1,0:T(8,128)(2,1)S(1)} %copy-done, bf16[128,128]{1,0:T(8,128)(2,1)S(1)} %copy-done.4, bf16[128,128]{1,0:T(8,128)(2,1)S(1)} %copy-done.5, bf16[16,128,256]{2,1,0:T(8,128)(2,1)S(1)} %constant_dynamic-update-slice_fusion.refs_0_, ...), custom_call_target="tpu_custom_call" | custom-call | tf_op jit(solution)/shard_map/attend_suffix_0/pallas_call | solution.py:150
  51.2 5.8 %collective-permute-start.19 = (bf16[128,1024]{1,0:T(8,128)(2,1)S(1)}, bf16[128,1024]{1,0:T(8,128)(2,1)S(1)}, u32[]{:S(2)}, u32[]{:S(2)}) collective-permute-start(bf16[128,1024]{1,0:T(8,128)(2,1)S(1)} %attend_suffix_0.1.a_s), channel_id=1, source_target_pairs={{0,1},{1,0},{2,3},{3,2},{4,7},{5,6},{6,5},{7,4},{8,9},{9,8},{10,11... | collective-permute-start | bytes 786440 | tf_op jit(solution)/shard_map/ppermute | solution.py:51
  57.1 1.4 %collective-permute-start.22 = (bf16[4,2,64,1024]{3,2,1,0:T(8,128)(2,1)S(1)}, bf16[4,2,64,1024]{3,2,1,0:T(8,128)(2,1)S(1)}, u32[]{:S(2)}, u32[]{:S(2)}) collective-permute-start(bf16[4,2,64,1024]{3,2,1,0:T(8,128)(2,1)S(1)} %pad_maximum_fusion.5), channel_id=1, source_target_pairs={{0,16},{4,52},{8,24},{12,60},{16,0},{20,36},{24,8},{28,44},{32,48}... | collective-permute-start | bytes 3145736 | tf_op jit(solution)/shard_map/ppermute | solution.py:46
  58.6 1.5 %collective-permute-start.21 = (bf16[4,2,64,1024]{3,2,1,0:T(8,128)(2,1)S(1)}, bf16[4,2,64,1024]{3,2,1,0:T(8,128)(2,1)S(1)}, u32[]{:S(2)}, u32[]{:S(2)}) collective-permute-start(bf16[4,2,64,1024]{3,2,1,0:T(8,128)(2,1)S(1)} %pad_maximum_fusion.4), channel_id=1, source_target_pairs={{0,64},{4,196},{8,72},{12,204},{16,80},{20,212},{24,88},{28,220},{... | collective-permute-start | bytes 3145736 | tf_op jit(solution)/shard_map/ppermute | solution.py:46
  60.2 2.9 %attend_prompt_0.1.a_p = bf16[128,1024]{1,0:T(8,128)(2,1)S(1)} custom-call(s32[68]{0:T(128)S(1)} %concatenate.77.info, bf16[128,1024]{1,0:T(8,128)(2,1)S(1)} %copy-done.1, bf16[128,128]{1,0:T(8,128)(2,1)S(1)} %copy-done.2, bf16[128,128]{1,0:T(8,128)(2,1)S(1)} %copy-done.3, bf16[16,128,256]{2,1,0:T(8,128)(2,1)S(1)} %constant_dynamic-update-slice_fusion.refs_0_, ...), custom_call_target="tpu_custom_call" | custom-call | tf_op jit(solution)/shard_map/attend_prompt_0/pallas_call | solution.py:150
  63.1 4.3 %collective-permute-start.23 = (bf16[4,2,64,1024]{3,2,1,0:T(8,128)(2,1)S(1)}, bf16[4,2,64,1024]{3,2,1,0:T(8,128)(2,1)S(1)}, u32[]{:S(2)}, u32[]{:S(2)}) collective-permute-start(bf16[4,2,64,1024]{3,2,1,0:T(8,128)(2,1)S(1)} %pad_maximum_fusion.4), channel_id=1, source_target_pairs={{0,192},{4,68},{8,200},{12,76},{16,208},{20,84},{24,216},{28,92},{... | collective-permute-start | bytes 3145736 | tf_op jit(solution)/shard_map/ppermute | solution.py:46
  68.8 19.3 %collective-permute-done.20.mixed = bf16[3,128,1024]{2,1,0:T(8,128)(2,1)S(1)} collective-permute-done((bf16[3,128,1024]{2,1,0:T(8,128)(2,1)S(1)}, bf16[3,128,1024]{2,1,0:T(8,128)(2,1)S(1)}, u32[]{:S(2)}, u32[]{:S(2)}) %collective-permute-start.20) | collective-permute-done | bytes 786464 | tf_op jit(solution)/shard_map/ppermute | solution.py:51
  88.4 2.8 %collective-permute-start.27 = (bf16[8,2,64,1024]{3,2,1,0:T(8,128)(2,1)S(1)}, bf16[8,2,64,1024]{3,2,1,0:T(8,128)(2,1)S(1)}, u32[]{:S(2)}, u32[]{:S(2)}) collective-permute-start(bf16[8,2,64,1024]{3,2,1,0:T(8,128)(2,1)S(1)} %constant_dynamic-update-slice_fusion.16.refs_2_), channel_id=1, source_target_pairs={{0,4},{4,0},{8,12},{12,8},{16,20},{20,16},{24,28},{28,24},{32,36},... | collective-permute-start | bytes 6291464 | tf_op jit(solution)/shard_map/ppermute | solution.py:46
  91.7 3.7 %collective-permute-start.25 = (bf16[2,128,1024]{2,1,0:T(8,128)(2,1)S(1)}, bf16[2,128,1024]{2,1,0:T(8,128)(2,1)S(1)}, u32[]{:S(2)}, u32[]{:S(2)}) collective-permute-start(bf16[2,128,1024]{2,1,0:T(8,128)(2,1)S(1)} %pad_maximum_fusion.11), channel_id=1, source_target_pairs={{0,1},{1,0},{2,3},{3,2},{4,7},{5,6},{6,5},{7,4},{8,9},{9,8},{10,11... | collective-permute-start | bytes 1572872 | tf_op jit(solution)/shard_map/ppermute | solution.py:51
  95.4 8.2 %collective-permute-done.25.far_p = bf16[2,128,1024]{2,1,0:T(8,128)(2,1)S(1)} collective-permute-done((bf16[2,128,1024]{2,1,0:T(8,128)(2,1)S(1)}, bf16[2,128,1024]{2,1,0:T(8,128)(2,1)S(1)}, u32[]{:S(2)}, u32[]{:S(2)}) %collective-permute-start.25) | collective-permute-done | bytes 524320 | tf_op jit(solution)/shard_map/ppermute | solution.py:51
  103.6 1.8 %collective-permute-done.28 = bf16[4,2,64,1024]{3,2,1,0:T(8,128)(2,1)S(1)} collective-permute-done((bf16[4,2,64,1024]{3,2,1,0:T(8,128)(2,1)S(1)}, bf16[4,2,64,1024]{3,2,1,0:T(8,128)(2,1)S(1)}, u32[]{:S(2)}, u32[]{:S(2)}) %collective-permute-start.28) | collective-permute-done | bytes 1048608 | tf_op jit(solution)/shard_map/ppermute | solution.py:46
  105.5 2.4 %collective-permute-start.30 = (bf16[4,2,64,1024]{3,2,1,0:T(8,128)(2,1)S(1)}, bf16[4,2,64,1024]{3,2,1,0:T(8,128)(2,1)S(1)}, u32[]{:S(2)}, u32[]{:S(2)}) collective-permute-start(bf16[4,2,64,1024]{3,2,1,0:T(8,128)(2,1)S(1)} %collective-permute-done.23), channel_id=1, source_target_pairs={{0,4},{4,0},{8,12},{12,8},{16,20},{20,16},{24,28},{28,24},{32,36},... | collective-permute-start | bytes 3145736 | tf_op jit(solution)/shard_map/ppermute | solution.py:46
  108.9 1.3 %collective-permute-done.30 = bf16[4,2,64,1024]{3,2,1,0:T(8,128)(2,1)S(1)} collective-permute-done((bf16[4,2,64,1024]{3,2,1,0:T(8,128)(2,1)S(1)}, bf16[4,2,64,1024]{3,2,1,0:T(8,128)(2,1)S(1)}, u32[]{:S(2)}, u32[]{:S(2)}) %collective-permute-start.30) | collective-permute-done | bytes 1048608 | tf_op jit(solution)/shard_map/ppermute | solution.py:46
  110.2 1.5 %collective-permute-done.31 = bf16[4,2,64,1024]{3,2,1,0:T(8,128)(2,1)S(1)} collective-permute-done((bf16[4,2,64,1024]{3,2,1,0:T(8,128)(2,1)S(1)}, bf16[4,2,64,1024]{3,2,1,0:T(8,128)(2,1)S(1)}, u32[]{:S(2)}, u32[]{:S(2)}) %collective-permute-start.31) | collective-permute-done | bytes 1048608 | tf_op jit(solution)/shard_map/ppermute | solution.py:46
  111.9 1.3 %collective-permute-done.32 = bf16[4,2,64,1024]{3,2,1,0:T(8,128)(2,1)S(1)} collective-permute-done((bf16[4,2,64,1024]{3,2,1,0:T(8,128)(2,1)S(1)}, bf16[4,2,64,1024]{3,2,1,0:T(8,128)(2,1)S(1)}, u32[]{:S(2)}, u32[]{:S(2)}) %collective-permute-start.32) | collective-permute-done | bytes 1048608 | tf_op jit(solution)/shard_map/ppermute | solution.py:46
  113.2 1.5 %collective-permute-done.33 = bf16[4,2,64,1024]{3,2,1,0:T(8,128)(2,1)S(1)} collective-permute-done((bf16[4,2,64,1024]{3,2,1,0:T(8,128)(2,1)S(1)}, bf16[4,2,64,1024]{3,2,1,0:T(8,128)(2,1)S(1)}, u32[]{:S(2)}, u32[]{:S(2)}) %collective-permute-start.33) | collective-permute-done | bytes 1048608 | tf_op jit(solution)/shard_map/ppermute | solution.py:46
  114.9 6.2 %project.1 = (bf16[128,2048]{1,0:T(8,128)(2,1)}, bf16[128,2048]{1,0:T(8,128)(2,1)}) custom-call(s32[68]{0:T(128)S(1)} %concatenate.77.info, bf16[128,1024]{1,0:T(8,128)(2,1)S(1)} %attend_prompt_0.1.a_p, bf16[128,1024]{1,0:T(8,128)(2,1)S(1)} %attend_suffix_0.1.a_s, bf16[128,1024]{1,0:T(8,128)(2,1)S(1)} %collective-permute-done.19.near_s, ...), custom_call_target="tpu_custom_call" | custom-call | tf_op jit(solution)/shard_map/project/pallas_call | solution.py:195
  (95 shorter events, 10.4 us)
Async XLA Ops:
  0.6 6.0 %collective-permute-start = (bf16[128,128]{1,0:T(8,128)(2,1)}, bf16[128,128]{1,0:T(8,128)(2,1)S(1)}, u32[]{:S(2)}, u32[]{:S(2)}) collective-permute-start(bf16[128,128]{1,0:T(8,128)(2,1)} %own_k.3), channel_id=1, source_target_pairs={{0,8},{4,12},{8,0},{12,4},{16,24},{20,28},{24,16},{28,20},{32,40},... | collective-permute-start | bytes 98312 | tf_op jit(solution)/shard_map/ppermute | solution.py:46
  4.1 6.8 %collective-permute-start.2 = (bf16[1,128,256]{2,1,0:T(8,128)(2,1)S(1)}, bf16[1,128,256]{2,1,0:T(8,128)(2,1)S(1)}, u32[]{:S(2)}, u32[]{:S(2)}) collective-permute-start(bf16[1,128,256]{2,1,0:T(8,128)(2,1)S(1)} %bitcast.27), channel_id=1, source_target_pairs={{0,16},{4,52},{8,24},{12,60},{16,0},{20,36},{24,8},{28,44},{32,48}... | collective-permute-start | bytes 196616 | tf_op jit(solution)/shard_map/ppermute | solution.py:46
  6.7 5.7 %collective-permute-start.9 = (bf16[1,128,256]{2,1,0:T(8,128)(2,1)S(1)}, bf16[1,128,256]{2,1,0:T(8,128)(2,1)S(1)}, u32[]{:S(2)}, u32[]{:S(2)}) collective-permute-start(bf16[1,128,256]{2,1,0:T(8,128)(2,1)S(1)} %maximum_bitcast_fusion.2), channel_id=1, source_target_pairs={{0,64},{4,196},{8,72},{12,204},{16,80},{20,212},{24,88},{28,220},{... | collective-permute-start | bytes 196616 | tf_op jit(solution)/shard_map/ppermute | solution.py:46
  9.5 7.7 %collective-permute-start.1 = (bf16[64,2048]{1,0:T(8,128)(2,1)}, bf16[64,2048]{1,0:T(8,128)(2,1)S(1)}, u32[]{:S(2)}, u32[]{:S(2)}) collective-permute-start(bf16[64,2048]{1,0:T(8,128)(2,1)} %param.17), channel_id=1, source_target_pairs={{0,8},{4,12},{8,0},{12,4},{16,24},{20,28},{24,16},{28,20},{32,40},... | collective-permute-start | bytes 786440 | tf_op jit(solution)/shard_map/ppermute | solution.py:46
  10.9 4.2 %collective-permute-start.3 = (bf16[2,128,256]{2,1,0:T(8,128)(2,1)S(1)}, bf16[2,128,256]{2,1,0:T(8,128)(2,1)S(1)}, u32[]{:S(2)}, u32[]{:S(2)}) collective-permute-start(bf16[2,128,256]{2,1,0:T(8,128)(2,1)S(1)} %pad_maximum_fusion.14), channel_id=1, source_target_pairs={{0,48},{4,20},{8,56},{12,28},{16,32},{20,4},{24,40},{28,12},{32,16... | collective-permute-start | bytes 393224 | tf_op jit(solution)/shard_map/ppermute | solution.py:46
  12.5 10.0 %collective-permute-start.10 = (bf16[2,128,256]{2,1,0:T(8,128)(2,1)S(1)}, bf16[2,128,256]{2,1,0:T(8,128)(2,1)S(1)}, u32[]{:S(2)}, u32[]{:S(2)}) collective-permute-start(bf16[2,128,256]{2,1,0:T(8,128)(2,1)S(1)} %pad_maximum_fusion.15), channel_id=1, source_target_pairs={{0,192},{4,68},{8,200},{12,76},{16,208},{20,84},{24,216},{28,92},{... | collective-permute-start | bytes 393224 | tf_op jit(solution)/shard_map/ppermute | solution.py:46
  18.3 6.5 %collective-permute-start.4 = (bf16[4,128,256]{2,1,0:T(8,128)(2,1)S(1)}, bf16[4,128,256]{2,1,0:T(8,128)(2,1)S(1)}, u32[]{:S(2)}, u32[]{:S(2)}) collective-permute-start(bf16[4,128,256]{2,1,0:T(8,128)(2,1)S(1)} %pad_maximum_fusion.12), channel_id=1, source_target_pairs={{0,64},{4,196},{8,72},{12,204},{16,80},{20,212},{24,88},{28,220},{... | collective-permute-start | bytes 786440 | tf_op jit(solution)/shard_map/ppermute | solution.py:46
  18.4 9.2 %collective-permute-start.6 = (bf16[1,2,64,1024]{3,2,1,0:T(8,128)(2,1)S(1)}, bf16[1,2,64,1024]{3,2,1,0:T(8,128)(2,1)S(1)}, u32[]{:S(2)}, u32[]{:S(2)}) collective-permute-start(bf16[1,2,64,1024]{3,2,1,0:T(8,128)(2,1)S(1)} %maximum_bitcast_fusion.1), channel_id=1, source_target_pairs={{0,64},{4,196},{8,72},{12,204},{16,80},{20,212},{24,88},{28,220},{... | collective-permute-start | bytes 786440 | tf_op jit(solution)/shard_map/ppermute | solution.py:46
  21.2 6.5 %collective-permute-start.5 = (bf16[1,2,64,1024]{3,2,1,0:T(8,128)(2,1)S(1)}, bf16[1,2,64,1024]{3,2,1,0:T(8,128)(2,1)S(1)}, u32[]{:S(2)}, u32[]{:S(2)}) collective-permute-start(bf16[1,2,64,1024]{3,2,1,0:T(8,128)(2,1)S(1)} %maximum_bitcast_fusion), channel_id=1, source_target_pairs={{0,16},{4,52},{8,24},{12,60},{16,0},{20,36},{24,8},{28,44},{32,48}... | collective-permute-start | bytes 786440 | tf_op jit(solution)/shard_map/ppermute | solution.py:46
  22.5 7.9 %collective-permute-start.11 = (bf16[4,128,256]{2,1,0:T(8,128)(2,1)S(1)}, bf16[4,128,256]{2,1,0:T(8,128)(2,1)S(1)}, u32[]{:S(2)}, u32[]{:S(2)}) collective-permute-start(bf16[4,128,256]{2,1,0:T(8,128)(2,1)S(1)} %pad_maximum_fusion.13), channel_id=1, source_target_pairs={{0,16},{4,52},{8,24},{12,60},{16,0},{20,36},{24,8},{28,44},{32,48}... | collective-permute-start | bytes 786440 | tf_op jit(solution)/shard_map/ppermute | solution.py:46
  24.9 14.6 %collective-permute-start.13 = (bf16[8,128,256]{2,1,0:T(8,128)(2,1)S(1)}, bf16[8,128,256]{2,1,0:T(8,128)(2,1)S(1)}, u32[]{:S(2)}, u32[]{:S(2)}) collective-permute-start(bf16[8,128,256]{2,1,0:T(8,128)(2,1)S(1)} %pad_maximum_fusion.7), channel_id=1, source_target_pairs={{0,4},{4,0},{8,12},{12,8},{16,20},{20,16},{24,28},{28,24},{32,36},... | collective-permute-start | bytes 1572872 | tf_op jit(solution)/shard_map/ppermute | solution.py:46
  27.8 8.4 %collective-permute-start.7 = (bf16[8,128,256]{2,1,0:T(8,128)(2,1)S(1)}, bf16[8,128,256]{2,1,0:T(8,128)(2,1)S(1)}, u32[]{:S(2)}, u32[]{:S(2)}) collective-permute-start(bf16[8,128,256]{2,1,0:T(8,128)(2,1)S(1)} %pad_maximum_fusion.7), channel_id=1, source_target_pairs={{0,192},{4,68},{8,200},{12,76},{16,208},{20,84},{24,216},{28,92},{... | collective-permute-start | bytes 1572872 | tf_op jit(solution)/shard_map/ppermute | solution.py:46
  30.5 9.1 %collective-permute-start.12 = (bf16[8,128,256]{2,1,0:T(8,128)(2,1)S(1)}, bf16[8,128,256]{2,1,0:T(8,128)(2,1)S(1)}, u32[]{:S(2)}, u32[]{:S(2)}) collective-permute-start(bf16[8,128,256]{2,1,0:T(8,128)(2,1)S(1)} %pad_maximum_fusion.10), channel_id=1, source_target_pairs={{0,48},{4,20},{8,56},{12,28},{16,32},{20,4},{24,40},{28,12},{32,16... | collective-permute-start | bytes 1572872 | tf_op jit(solution)/shard_map/ppermute | solution.py:46
  30.6 10.9 %collective-permute-start.15 = (bf16[8,128,256]{2,1,0:T(8,128)(2,1)S(1)}, bf16[8,128,256]{2,1,0:T(8,128)(2,1)S(1)}, u32[]{:S(2)}, u32[]{:S(2)}) collective-permute-start(bf16[8,128,256]{2,1,0:T(8,128)(2,1)S(1)} %pad_maximum_fusion.10), channel_id=1, source_target_pairs={{0,4},{4,0},{8,12},{12,8},{16,20},{20,16},{24,28},{28,24},{32,36},... | collective-permute-start | bytes 1572872 | tf_op jit(solution)/shard_map/ppermute | solution.py:46
  33.4 17.8 %collective-permute-start.17 = (bf16[2,2,64,1024]{3,2,1,0:T(8,128)(2,1)S(1)}, bf16[2,2,64,1024]{3,2,1,0:T(8,128)(2,1)S(1)}, u32[]{:S(2)}, u32[]{:S(2)}) collective-permute-start(bf16[2,2,64,1024]{3,2,1,0:T(8,128)(2,1)S(1)} %pad_maximum_fusion.8), channel_id=1, source_target_pairs={{0,48},{4,20},{8,56},{12,28},{16,32},{20,4},{24,40},{28,12},{32,16... | collective-permute-start | bytes 1572872 | tf_op jit(solution)/shard_map/ppermute | solution.py:46
  36.2 5.5 %collective-permute-start.14 = (bf16[8,128,256]{2,1,0:T(8,128)(2,1)S(1)}, bf16[8,128,256]{2,1,0:T(8,128)(2,1)S(1)}, u32[]{:S(2)}, u32[]{:S(2)}) collective-permute-start(bf16[8,128,256]{2,1,0:T(8,128)(2,1)S(1)} %collective-permute-done.7), channel_id=1, source_target_pairs={{0,4},{4,0},{8,12},{12,8},{16,20},{20,16},{24,28},{28,24},{32,36},... | collective-permute-start | bytes 1572872 | tf_op jit(solution)/shard_map/ppermute | solution.py:46
  39.5 11.7 %collective-permute-start.18 = (bf16[2,2,64,1024]{3,2,1,0:T(8,128)(2,1)S(1)}, bf16[2,2,64,1024]{3,2,1,0:T(8,128)(2,1)S(1)}, u32[]{:S(2)}, u32[]{:S(2)}) collective-permute-start(bf16[2,2,64,1024]{3,2,1,0:T(8,128)(2,1)S(1)} %pad_maximum_fusion.9), channel_id=1, source_target_pairs={{0,192},{4,68},{8,200},{12,76},{16,208},{20,84},{24,216},{28,92},{... | collective-permute-start | bytes 1572872 | tf_op jit(solution)/shard_map/ppermute | solution.py:46
  51.2 11.9 %collective-permute-start.19 = (bf16[128,1024]{1,0:T(8,128)(2,1)S(1)}, bf16[128,1024]{1,0:T(8,128)(2,1)S(1)}, u32[]{:S(2)}, u32[]{:S(2)}) collective-permute-start(bf16[128,1024]{1,0:T(8,128)(2,1)S(1)} %attend_suffix_0.1.a_s), channel_id=1, source_target_pairs={{0,1},{1,0},{2,3},{3,2},{4,7},{5,6},{6,5},{7,4},{8,9},{9,8},{10,11... | collective-permute-start | bytes 786440 | tf_op jit(solution)/shard_map/ppermute | solution.py:51
  57.1 31.0 %collective-permute-start.22 = (bf16[4,2,64,1024]{3,2,1,0:T(8,128)(2,1)S(1)}, bf16[4,2,64,1024]{3,2,1,0:T(8,128)(2,1)S(1)}, u32[]{:S(2)}, u32[]{:S(2)}) collective-permute-start(bf16[4,2,64,1024]{3,2,1,0:T(8,128)(2,1)S(1)} %pad_maximum_fusion.5), channel_id=1, source_target_pairs={{0,16},{4,52},{8,24},{12,60},{16,0},{20,36},{24,8},{28,44},{32,48}... | collective-permute-start | bytes 3145736 | tf_op jit(solution)/shard_map/ppermute | solution.py:46
  58.6 29.5 %collective-permute-start.21 = (bf16[4,2,64,1024]{3,2,1,0:T(8,128)(2,1)S(1)}, bf16[4,2,64,1024]{3,2,1,0:T(8,128)(2,1)S(1)}, u32[]{:S(2)}, u32[]{:S(2)}) collective-permute-start(bf16[4,2,64,1024]{3,2,1,0:T(8,128)(2,1)S(1)} %pad_maximum_fusion.4), channel_id=1, source_target_pairs={{0,64},{4,196},{8,72},{12,204},{16,80},{20,212},{24,88},{28,220},{... | collective-permute-start | bytes 3145736 | tf_op jit(solution)/shard_map/ppermute | solution.py:46
  63.1 25.0 %collective-permute-start.23 = (bf16[4,2,64,1024]{3,2,1,0:T(8,128)(2,1)S(1)}, bf16[4,2,64,1024]{3,2,1,0:T(8,128)(2,1)S(1)}, u32[]{:S(2)}, u32[]{:S(2)}) collective-permute-start(bf16[4,2,64,1024]{3,2,1,0:T(8,128)(2,1)S(1)} %pad_maximum_fusion.4), channel_id=1, source_target_pairs={{0,192},{4,68},{8,200},{12,76},{16,208},{20,84},{24,216},{28,92},{... | collective-permute-start | bytes 3145736 | tf_op jit(solution)/shard_map/ppermute | solution.py:46
  67.4 20.7 %collective-permute-start.24 = (bf16[4,2,64,1024]{3,2,1,0:T(8,128)(2,1)S(1)}, bf16[4,2,64,1024]{3,2,1,0:T(8,128)(2,1)S(1)}, u32[]{:S(2)}, u32[]{:S(2)}) collective-permute-start(bf16[4,2,64,1024]{3,2,1,0:T(8,128)(2,1)S(1)} %pad_maximum_fusion.5), channel_id=1, source_target_pairs={{0,48},{4,20},{8,56},{12,28},{16,32},{20,4},{24,40},{28,12},{32,16... | collective-permute-start | bytes 3145736 | tf_op jit(solution)/shard_map/ppermute | solution.py:46
  67.5 20.6 %collective-permute-start.20 = (bf16[3,128,1024]{2,1,0:T(8,128)(2,1)S(1)}, bf16[3,128,1024]{2,1,0:T(8,128)(2,1)S(1)}, u32[]{:S(2)}, u32[]{:S(2)}) collective-permute-start(bf16[3,128,1024]{2,1,0:T(8,128)(2,1)S(1)} %pad_maximum_fusion.6), channel_id=1, source_target_pairs={{0,3},{1,2},{2,1},{3,0},{4,5},{5,4},{6,7},{7,6},{8,11},{9,10},{10,... | collective-permute-start | bytes 2359304 | tf_op jit(solution)/shard_map/ppermute | solution.py:51
  88.4 15.2 %collective-permute-start.27 = (bf16[8,2,64,1024]{3,2,1,0:T(8,128)(2,1)S(1)}, bf16[8,2,64,1024]{3,2,1,0:T(8,128)(2,1)S(1)}, u32[]{:S(2)}, u32[]{:S(2)}) collective-permute-start(bf16[8,2,64,1024]{3,2,1,0:T(8,128)(2,1)S(1)} %constant_dynamic-update-slice_fusion.16.refs_2_), channel_id=1, source_target_pairs={{0,4},{4,0},{8,12},{12,8},{16,20},{20,16},{24,28},{28,24},{32,36},... | collective-permute-start | bytes 6291464 | tf_op jit(solution)/shard_map/ppermute | solution.py:46
  91.3 12.3 %collective-permute-start.26 = (bf16[8,2,64,1024]{3,2,1,0:T(8,128)(2,1)S(1)}, bf16[8,2,64,1024]{3,2,1,0:T(8,128)(2,1)S(1)}, u32[]{:S(2)}, u32[]{:S(2)}) collective-permute-start(bf16[8,2,64,1024]{3,2,1,0:T(8,128)(2,1)S(1)} %constant_dynamic-update-slice_fusion.14.refs_0_), channel_id=1, source_target_pairs={{0,4},{4,0},{8,12},{12,8},{16,20},{20,16},{24,28},{28,24},{32,36},... | collective-permute-start | bytes 6291464 | tf_op jit(solution)/shard_map/ppermute | solution.py:46
  91.4 14.0 %collective-permute-start.28 = (bf16[4,2,64,1024]{3,2,1,0:T(8,128)(2,1)S(1)}, bf16[4,2,64,1024]{3,2,1,0:T(8,128)(2,1)S(1)}, u32[]{:S(2)}, u32[]{:S(2)}) collective-permute-start(bf16[4,2,64,1024]{3,2,1,0:T(8,128)(2,1)S(1)} %collective-permute-done.21), channel_id=1, source_target_pairs={{0,192},{4,68},{8,200},{12,76},{16,208},{20,84},{24,216},{28,92},{... | collective-permute-start | bytes 3145736 | tf_op jit(solution)/shard_map/ppermute | solution.py:46
  91.5 14.0 %collective-permute-start.29 = (bf16[4,2,64,1024]{3,2,1,0:T(8,128)(2,1)S(1)}, bf16[4,2,64,1024]{3,2,1,0:T(8,128)(2,1)S(1)}, u32[]{:S(2)}, u32[]{:S(2)}) collective-permute-start(bf16[4,2,64,1024]{3,2,1,0:T(8,128)(2,1)S(1)} %collective-permute-done.22), channel_id=1, source_target_pairs={{0,48},{4,20},{8,56},{12,28},{16,32},{20,4},{24,40},{28,12},{32,16... | collective-permute-start | bytes 3145736 | tf_op jit(solution)/shard_map/ppermute | solution.py:46
  91.7 11.9 %collective-permute-start.25 = (bf16[2,128,1024]{2,1,0:T(8,128)(2,1)S(1)}, bf16[2,128,1024]{2,1,0:T(8,128)(2,1)S(1)}, u32[]{:S(2)}, u32[]{:S(2)}) collective-permute-start(bf16[2,128,1024]{2,1,0:T(8,128)(2,1)S(1)} %pad_maximum_fusion.11), channel_id=1, source_target_pairs={{0,1},{1,0},{2,3},{3,2},{4,7},{5,6},{6,5},{7,4},{8,9},{9,8},{10,11... | collective-permute-start | bytes 1572872 | tf_op jit(solution)/shard_map/ppermute | solution.py:51
  105.5 4.7 %collective-permute-start.30 = (bf16[4,2,64,1024]{3,2,1,0:T(8,128)(2,1)S(1)}, bf16[4,2,64,1024]{3,2,1,0:T(8,128)(2,1)S(1)}, u32[]{:S(2)}, u32[]{:S(2)}) collective-permute-start(bf16[4,2,64,1024]{3,2,1,0:T(8,128)(2,1)S(1)} %collective-permute-done.23), channel_id=1, source_target_pairs={{0,4},{4,0},{8,12},{12,8},{16,20},{20,16},{24,28},{28,24},{32,36},... | collective-permute-start | bytes 3145736 | tf_op jit(solution)/shard_map/ppermute | solution.py:46
  107.9 3.8 %collective-permute-start.31 = (bf16[4,2,64,1024]{3,2,1,0:T(8,128)(2,1)S(1)}, bf16[4,2,64,1024]{3,2,1,0:T(8,128)(2,1)S(1)}, u32[]{:S(2)}, u32[]{:S(2)}) collective-permute-start(bf16[4,2,64,1024]{3,2,1,0:T(8,128)(2,1)S(1)} %collective-permute-done.28), channel_id=1, source_target_pairs={{0,4},{4,0},{8,12},{12,8},{16,20},{20,16},{24,28},{28,24},{32,36},... | collective-permute-start | bytes 3145736 | tf_op jit(solution)/shard_map/ppermute | solution.py:46
  108.0 5.2 %collective-permute-start.32 = (bf16[4,2,64,1024]{3,2,1,0:T(8,128)(2,1)S(1)}, bf16[4,2,64,1024]{3,2,1,0:T(8,128)(2,1)S(1)}, u32[]{:S(2)}, u32[]{:S(2)}) collective-permute-start(bf16[4,2,64,1024]{3,2,1,0:T(8,128)(2,1)S(1)} %collective-permute-done.24), channel_id=1, source_target_pairs={{0,4},{4,0},{8,12},{12,8},{16,20},{20,16},{24,28},{28,24},{32,36},... | collective-permute-start | bytes 3145736 | tf_op jit(solution)/shard_map/ppermute | solution.py:46
  108.4 6.3 %collective-permute-start.33 = (bf16[4,2,64,1024]{3,2,1,0:T(8,128)(2,1)S(1)}, bf16[4,2,64,1024]{3,2,1,0:T(8,128)(2,1)S(1)}, u32[]{:S(2)}, u32[]{:S(2)}) collective-permute-start(bf16[4,2,64,1024]{3,2,1,0:T(8,128)(2,1)S(1)} %collective-permute-done.29), channel_id=1, source_target_pairs={{0,4},{4,0},{8,12},{12,8},{16,20},{20,16},{24,28},{28,24},{32,36},... | collective-permute-start | bytes 3145736 | tf_op jit(solution)/shard_map/ppermute | solution.py:46
  (8 other events, 38.5 us)

commit v3 on v2

--- a/solution.py
+++ b/solution.py
@@ -74,55 +74,54 @@
 
 
 def add_values(acc, h, exps, shrink, values):
-    acc[h] = acc[h] * jnp.concatenate([shrink, shrink], axis=1) + jnp.dot(
-        exps, values, preferred_element_type=jnp.float32)
+    fresh = jnp.dot(exps, values, preferred_element_type=jnp.float32)
+    if shrink is not None:
+        fresh = acc[h] * jnp.concatenate([shrink, shrink], axis=1) + fresh
+    acc[h] = fresh
 
 
 def attend_kernel(is_prompt, first, count, info, q, own_k, own_v, *refs):
     blocks, (out, top, acc) = refs[:4], refs[4:]
     me = info[0]
-    core, low_z = me & 1, (me >> 1) & 1
     row = lax.broadcasted_iota(jnp.int32, (ROWS, ROWS), 0)
-    col = lax.broadcasted_iota(jnp.int32, (ROWS, ROWS), 1)
-    keys = own_k[...]
-    values = jnp.concatenate([own_v[...], jnp.ones((ROWS, HD), jnp.bfloat16)], axis=1)
-    scores = [
-        jnp.where(row >= col, score_head(q, first + h, keys), -1e30) for h in range(count)]
-    best = [
-        jnp.broadcast_to(jnp.max(part, axis=1, keepdims=True), (ROWS, HD)) for part in scores]
-    exps = [
-        jnp.exp2((part - high) * SCALE).astype(jnp.bfloat16) for part, high in zip(scores, best)]
-    for h in range(count):
-        top[h] = best[h]
-        acc[h] = jnp.dot(exps[h], values, preferred_element_type=jnp.float32)
-
-    def absorb(pair, masked):
+    ahead_by = row - lax.broadcasted_iota(jnp.int32, (ROWS, ROWS), 1)
+
+    def absorb(pair, opening):
         begin = 8 * (me >> 5 if is_prompt else info[1]) + 2 * pair
-        keys, values, allowed = [], [], []
+        keys, values, floors = [], [], []
         for there in (begin, begin + 1):
             for rc in range(2):
                 for rz in range(2):
-                    slot = slot_of(info, rc, rz, there)
-                    both = blocks[rc * 2 + rz][slot]
+                    both = blocks[rc * 2 + rz][slot_of(info, rc, rz, there)]
                     keys.append(both[:, :HD])
                     values.append(both[:, HD:])
-                    allowed.append(there * 4 + ((me ^ (rz * 2 + rc)) & 3) < me)
+                    later = there * 4 + ((me ^ (rz * 2 + rc)) & 3) - me
+                    floors.append(later * ROWS if is_prompt and opening else None)
+        if opening and not is_prompt:
+            keys.append(own_k[...])
+            values.append(own_v[...])
+            floors.append(0)
         keys = jnp.concatenate(keys, axis=0)
         values = jnp.concatenate(values, axis=0)
         values = jnp.concatenate([values, jnp.ones(values.shape, jnp.bfloat16)], axis=1)
-        ahead = score_head(q, first, keys)
+        ready = [score_head(q, first, keys), score_head(q, first + 1, keys)]
         behind = None
         for h in range(count):
-            scores = ahead
-            if h + 1 < count:
-                ahead = score_head(q, first + h + 1, keys)
-            parts = [scores[:, i * ROWS:(i + 1) * ROWS] for i in range(8)]
-            if masked:
-                parts = [jnp.where(ok, part, -1e30) for ok, part in zip(allowed, parts)]
-            best = functools.reduce(jnp.maximum, parts)
-            old = top[h]
-            new = jnp.maximum(old, jnp.max(best, axis=1, keepdims=True))
-            shrink = jnp.exp2((old - new) * SCALE)
+            scores = ready.pop(0)
+            if h + 2 < count:
+                ready.append(score_head(q, first + h + 2, keys))
+            parts = [scores[:, i * ROWS:(i + 1) * ROWS] for i in range(len(floors))]
+            parts = [
+                part if floor is None else jnp.where(ahead_by >= floor, part, -1e30)
+                for floor, part in zip(floors, parts)]
+            new = jnp.max(functools.reduce(jnp.maximum, parts), axis=1, keepdims=True)
+            if opening:
+                new = jnp.broadcast_to(new, (ROWS, HD))
+                shrink = None
+            else:
+                old = top[h]
+                new = jnp.maximum(old, new)
+                shrink = jnp.exp2((old - new) * SCALE)
             top[h] = new
             exps = jnp.concatenate(
                 [jnp.exp2((part - new) * SCALE).astype(jnp.bfloat16) for part in parts], axis=1)
@@ -131,12 +130,14 @@
             behind = exps, shrink
         add_values(acc, count - 1, *behind, values)
 
-    whole = (me & 31) >> 3 if is_prompt else 4
-    lax.fori_loop(0, whole, lambda i, c: (absorb(i, False), c)[1], 0)
     if is_prompt:
-        @pl.when((me & 7) > 0)
-        def _():
-            absorb(whole, True)
+        last = (me & 31) >> 3
+        absorb(last, True)
+        lax.fori_loop(0, last, lambda i, c: (absorb(i, False), c)[1], 0)
+    else:
+        for i in range(4):
+            absorb(i, i == 0)
+    core, low_z = me & 1, (me >> 1) & 1
     for h in range(count):
         result = acc[h][:, :HD] / acc[h][:, HD:]
         if not is_prompt:
@@ -235,24 +236,15 @@
     w_3 = gather_step(w, 2)
     near_s = swap_tensor(a_s, (1, 3))
     a_p = attend(True, 0, 8, info, after(prompt_q, *w), prompt_k, prompt_v, blocks)
-    a_s, near_s, a_p, *w = lax.optimization_barrier((a_s, near_s, a_p, *w))
+    a_s, near_s, a_p = lax.optimization_barrier((a_s, near_s, a_p))
+    w = join(w, [after(a, a_p) for a in w_3])
 
     mixed = swap_tensor(jnp.stack([a_s, near_s, a_p]), (3, 1))
-    w_4 = gather_step(w, 3)
-    mixed, *w = lax.optimization_barrier((mixed, *w, *w_3, *w_4))
-    w, w_3, w_4 = w[:2], w[2:4], w[4:]
-
+    w_came = gather_step(w, 3)
     far_p = swap_tensor(jnp.stack([a_p, mixed[2]]), (1, 3))
-    w_5 = gather_step(w_3, 3)
-    w = join(w, w_3)
     w_mate = [swap(a, 1) for a in w]
-    far_p, *w_mate = lax.optimization_barrier((far_p, *w_mate))
-
-    *w_5, _ = lax.optimization_barrier((*w_5, far_p))
-    w_5_mate = [swap(a, 1) for a in w_5]
-    w_4_mate = [swap(after(a, *w_5), 1) for a in w_4]
-    w_came = join(w_4, w_5)
-    w_came_mate = join(w_4_mate, w_5_mate)
+    w_came = [after(a, mixed) for a in w_came]
+    w_came_mate = [swap(a, 1) for a in w_came]
     weights = [w[0], w_came[0], w[1], w_came[1],
                w_mate[0], w_came_mate[0], w_mate[1], w_came_mate[1]]
     return tuple(project(info, [a_p, a_s, near_s, mixed, far_p], weights))

time: 121 us -> 118 us (0.975); the launches traced: 121 us -> 117 us
  waiting for transfers between devices: 48.7 us -> 45.3 us
  Pallas kernels: 17.2 us -> 15.2 us
  starting transfers between devices: 48.8 us -> 50.4 us
    ppermute x3, starting transfers between devices: 10.8 us -> 13.8 us  [swap_tensor(): return lax.ppermute(x, ('sample', 'tensor'), pairs)]
    ppermute x31 -> x27, waiting for transfers between devices: 21.1 us -> 19 us  [swap(): return lax.ppermute(x, 'sample', [(s, s ^ masks[s & 1]) for s in range(64)])]
    pallas_call x2, Pallas kernels: 11 us -> 9 us  [attend(): pl.pallas_call(functools.partial(attend_kernel, is_prompt, first, count),...]
    ppermute x31 -> x27, starting transfers between devices: 38 us -> 36.6 us  [swap(): return lax.ppermute(x, 'sample', [(s, s ^ masks[s & 1]) for s in range(64)])]
    ppermute x3, waiting for transfers between devices: 27.6 us -> 26.3 us  [swap_tensor(): return lax.ppermute(x, ('sample', 'tensor'), pairs)]
  transfers between devices with their start and end apart: 34 -> 30, of which waited for: 15 -> 12; matrix products, arithmetic and copies ran while one was open for 3% -> 3% of each run, Pallas kernels for 9% -> 8%
where the time goes in v3:
time: 118 us; the launch traced here: 117 us
  starting transfers between devices  50.4 us (43%)
  waiting for transfers between devices  45.3 us (38%)
  Pallas kernels  15.2 us (13%)
  between operations  2.4 us (2%)
  other arithmetic  1.96 us (2%)
  local copies, waits for them, and re-layouts  1.43 us (1%)
    ppermute x27, starting transfers between devices, swap(): return lax.ppermute(x, 'sample', [(s, s ^ masks[s & 1]) for s in range(64)])  36.6 us
    ppermute x3, waiting for transfers between devices, swap_tensor(): return lax.ppermute(x, ('sample', 'tensor'), pairs)  26.3 us
    ppermute x27, waiting for transfers between devices, swap(): return lax.ppermute(x, 'sample', [(s, s ^ masks[s & 1]) for s in range(64)])  19 us
    ppermute x3, starting transfers between devices, swap_tensor(): return lax.ppermute(x, ('sample', 'tensor'), pairs)  13.8 us
    pallas_call x2, Pallas kernels, attend(): pl.pallas_call(functools.partial(attend_kernel, is_prompt, first, count),...  9 us
    pallas_call x1, Pallas kernels, project(): pl.pallas_call(project_kernel, out_shape=[jax.ShapeDtypeStruct((ROWS, 204...  6.19 us
  transfers between devices with their start and end apart: 30, of which 12 were waited for; matrix products, arithmetic and copies ran while one was open for 3% of the time, Pallas kernels for 8%

profile of v3, /device:TPU:1, one launch (start us, length us, event | category | flops | bytes accessed | tf_op | source)
XLA Modules:
  0.0 116.7 jit_solution(17427005429236321154)
XLA Ops:
  0.6 2.6 %collective-permute-start = (bf16[128,128]{1,0:T(8,128)(2,1)}, bf16[128,128]{1,0:T(8,128)(2,1)S(1)}, u32[]{:S(2)}, u32[]{:S(2)}) collective-permute-start(bf16[128,128]{1,0:T(8,128)(2,1)} %own_k.3), channel_id=1, source_target_pairs={{0,8},{4,12},{8,0},{12,4},{16,24},{20,28},{24,16},{28,20},{32,40},... | collective-permute-start | bytes 98312 | tf_op jit(solution)/shard_map/ppermute | solution.py:46
  4.1 2.6 %collective-permute-start.2 = (bf16[1,128,256]{2,1,0:T(8,128)(2,1)S(1)}, bf16[1,128,256]{2,1,0:T(8,128)(2,1)S(1)}, u32[]{:S(2)}, u32[]{:S(2)}) collective-permute-start(bf16[1,128,256]{2,1,0:T(8,128)(2,1)S(1)} %bitcast.27), channel_id=1, source_target_pairs={{0,16},{4,52},{8,24},{12,60},{16,0},{20,36},{24,8},{28,44},{32,48}... | collective-permute-start | bytes 196616 | tf_op jit(solution)/shard_map/ppermute | solution.py:46
  6.7 2.8 %collective-permute-start.9 = (bf16[1,128,256]{2,1,0:T(8,128)(2,1)S(1)}, bf16[1,128,256]{2,1,0:T(8,128)(2,1)S(1)}, u32[]{:S(2)}, u32[]{:S(2)}) collective-permute-start(bf16[1,128,256]{2,1,0:T(8,128)(2,1)S(1)} %maximum_bitcast_fusion.2), channel_id=1, source_target_pairs={{0,64},{4,196},{8,72},{12,204},{16,80},{20,212},{24,88},{28,220},{... | collective-permute-start | bytes 196616 | tf_op jit(solution)/shard_map/ppermute | solution.py:46
  9.5 1.4 %collective-permute-start.1 = (bf16[64,2048]{1,0:T(8,128)(2,1)}, bf16[64,2048]{1,0:T(8,128)(2,1)S(1)}, u32[]{:S(2)}, u32[]{:S(2)}) collective-permute-start(bf16[64,2048]{1,0:T(8,128)(2,1)} %param.17), channel_id=1, source_target_pairs={{0,8},{4,12},{8,0},{12,4},{16,24},{20,28},{24,16},{28,20},{32,40},... | collective-permute-start | bytes 786440 | tf_op jit(solution)/shard_map/ppermute | solution.py:46
  12.6 2.6 %collective-permute-done.3 = bf16[2,128,256]{2,1,0:T(8,128)(2,1)S(1)} collective-permute-done((bf16[2,128,256]{2,1,0:T(8,128)(2,1)S(1)}, bf16[2,128,256]{2,1,0:T(8,128)(2,1)S(1)}, u32[]{:S(2)}, u32[]{:S(2)}) %collective-permute-start.3) | collective-permute-done | bytes 131104 | tf_op jit(solution)/shard_map/ppermute | solution.py:46
  15.2 2.1 %collective-permute-done.1 = bf16[64,2048]{1,0:T(8,128)(2,1)S(1)} collective-permute-done((bf16[64,2048]{1,0:T(8,128)(2,1)}, bf16[64,2048]{1,0:T(8,128)(2,1)S(1)}, u32[]{:S(2)}, u32[]{:S(2)}) %collective-permute-start.1) | collective-permute-done | bytes 262176 | tf_op jit(solution)/shard_map/ppermute | solution.py:46
  18.4 2.7 %collective-permute-start.6 = (bf16[1,2,64,1024]{3,2,1,0:T(8,128)(2,1)S(1)}, bf16[1,2,64,1024]{3,2,1,0:T(8,128)(2,1)S(1)}, u32[]{:S(2)}, u32[]{:S(2)}) collective-permute-start(bf16[1,2,64,1024]{3,2,1,0:T(8,128)(2,1)S(1)} %maximum_bitcast_fusion.1), channel_id=1, source_target_pairs={{0,64},{4,196},{8,72},{12,204},{16,80},{20,212},{24,88},{28,220},{... | collective-permute-start | bytes 786440 | tf_op jit(solution)/shard_map/ppermute | solution.py:46
  21.2 1.3 %collective-permute-start.5 = (bf16[1,2,64,1024]{3,2,1,0:T(8,128)(2,1)S(1)}, bf16[1,2,64,1024]{3,2,1,0:T(8,128)(2,1)S(1)}, u32[]{:S(2)}, u32[]{:S(2)}) collective-permute-start(bf16[1,2,64,1024]{3,2,1,0:T(8,128)(2,1)S(1)} %maximum_bitcast_fusion), channel_id=1, source_target_pairs={{0,16},{4,52},{8,24},{12,60},{16,0},{20,36},{24,8},{28,44},{32,48}... | collective-permute-start | bytes 786440 | tf_op jit(solution)/shard_map/ppermute | solution.py:46
  22.5 1.4 %collective-permute-start.11 = (bf16[4,128,256]{2,1,0:T(8,128)(2,1)S(1)}, bf16[4,128,256]{2,1,0:T(8,128)(2,1)S(1)}, u32[]{:S(2)}, u32[]{:S(2)}) collective-permute-start(bf16[4,128,256]{2,1,0:T(8,128)(2,1)S(1)} %pad_maximum_fusion.11), channel_id=1, source_target_pairs={{0,16},{4,52},{8,24},{12,60},{16,0},{20,36},{24,8},{28,44},{32,48}... | collective-permute-start | bytes 786440 | tf_op jit(solution)/shard_map/ppermute | solution.py:46
  24.9 1.3 %collective-permute-start.13 = (bf16[8,128,256]{2,1,0:T(8,128)(2,1)S(1)}, bf16[8,128,256]{2,1,0:T(8,128)(2,1)S(1)}, u32[]{:S(2)}, u32[]{:S(2)}) collective-permute-start(bf16[8,128,256]{2,1,0:T(8,128)(2,1)S(1)} %pad_maximum_fusion.5), channel_id=1, source_target_pairs={{0,4},{4,0},{8,12},{12,8},{16,20},{20,16},{24,28},{28,24},{32,36},... | collective-permute-start | bytes 1572872 | tf_op jit(solution)/shard_map/ppermute | solution.py:46
  26.2 1.5 %collective-permute-done.6 = bf16[1,2,64,1024]{3,2,1,0:T(8,128)(2,1)S(1)} collective-permute-done((bf16[1,2,64,1024]{3,2,1,0:T(8,128)(2,1)S(1)}, bf16[1,2,64,1024]{3,2,1,0:T(8,128)(2,1)S(1)}, u32[]{:S(2)}, u32[]{:S(2)}) %collective-permute-start.6) | collective-permute-done | bytes 262176 | tf_op jit(solution)/shard_map/ppermute | solution.py:46
  27.9 2.6 %collective-permute-done.11 = bf16[4,128,256]{2,1,0:T(8,128)(2,1)S(1)} collective-permute-done((bf16[4,128,256]{2,1,0:T(8,128)(2,1)S(1)}, bf16[4,128,256]{2,1,0:T(8,128)(2,1)S(1)}, u32[]{:S(2)}, u32[]{:S(2)}) %collective-permute-start.11) | collective-permute-done | bytes 262176 | tf_op jit(solution)/shard_map/ppermute | solution.py:46
  30.6 2.7 %collective-permute-start.15 = (bf16[8,128,256]{2,1,0:T(8,128)(2,1)S(1)}, bf16[8,128,256]{2,1,0:T(8,128)(2,1)S(1)}, u32[]{:S(2)}, u32[]{:S(2)}) collective-permute-start(bf16[8,128,256]{2,1,0:T(8,128)(2,1)S(1)} %pad_maximum_fusion.8), channel_id=1, source_target_pairs={{0,4},{4,0},{8,12},{12,8},{16,20},{20,16},{24,28},{28,24},{32,36},... | collective-permute-start | bytes 1572872 | tf_op jit(solution)/shard_map/ppermute | solution.py:46
  33.5 2.7 %collective-permute-done.7 = bf16[8,128,256]{2,1,0:T(8,128)(2,1)S(1)} collective-permute-done((bf16[8,128,256]{2,1,0:T(8,128)(2,1)S(1)}, bf16[8,128,256]{2,1,0:T(8,128)(2,1)S(1)}, u32[]{:S(2)}, u32[]{:S(2)}) %collective-permute-start.7) | collective-permute-done | bytes 524320 | tf_op jit(solution)/shard_map/ppermute | solution.py:46
  36.2 3.2 %collective-permute-start.14 = (bf16[8,128,256]{2,1,0:T(8,128)(2,1)S(1)}, bf16[8,128,256]{2,1,0:T(8,128)(2,1)S(1)}, u32[]{:S(2)}, u32[]{:S(2)}) collective-permute-start(bf16[8,128,256]{2,1,0:T(8,128)(2,1)S(1)} %collective-permute-done.7), channel_id=1, source_target_pairs={{0,4},{4,0},{8,12},{12,8},{16,20},{20,16},{24,28},{28,24},{32,36},... | collective-permute-start | bytes 1572872 | tf_op jit(solution)/shard_map/ppermute | solution.py:46
  39.6 1.9 %collective-permute-start.16 = (bf16[8,128,256]{2,1,0:T(8,128)(2,1)S(1)}, bf16[8,128,256]{2,1,0:T(8,128)(2,1)S(1)}, u32[]{:S(2)}, u32[]{:S(2)}) collective-permute-start(bf16[8,128,256]{2,1,0:T(8,128)(2,1)S(1)} %collective-permute-done.12), channel_id=1, source_target_pairs={{0,4},{4,0},{8,12},{12,8},{16,20},{20,16},{24,28},{28,24},{32,36},... | collective-permute-start | bytes 1572872 | tf_op jit(solution)/shard_map/ppermute | solution.py:46
  41.8 1.3 %collective-permute-done.16 = bf16[8,128,256]{2,1,0:T(8,128)(2,1)S(1)} collective-permute-done((bf16[8,128,256]{2,1,0:T(8,128)(2,1)S(1)}, bf16[8,128,256]{2,1,0:T(8,128)(2,1)S(1)}, u32[]{:S(2)}, u32[]{:S(2)}) %collective-permute-start.16) | collective-permute-done | bytes 524320 | tf_op jit(solution)/shard_map/ppermute | solution.py:46
  43.1 6.5 %attend_suffix_0.1.a_s = bf16[128,1024]{1,0:T(8,128)(2,1)S(1)} custom-call(s32[68]{0:T(128)S(1)} %concatenate.67.info, bf16[128,1024]{1,0:T(8,128)(2,1)S(1)} %copy-done, bf16[128,128]{1,0:T(8,128)(2,1)S(1)} %copy-done.4, bf16[128,128]{1,0:T(8,128)(2,1)S(1)} %copy-done.5, bf16[16,128,256]{2,1,0:T(8,128)(2,1)S(1)} %constant_dynamic-update-slice_fusion.refs_0_, ...), custom_call_target="tpu_custom_call" | custom-call | tf_op jit(solution)/shard_map/attend_suffix_0/pallas_call | solution.py:151
  49.8 2.0 %collective-permute-start.24 = (bf16[4,2,64,1024]{3,2,1,0:T(8,128)(2,1)S(1)}, bf16[4,2,64,1024]{3,2,1,0:T(8,128)(2,1)S(1)}, u32[]{:S(2)}, u32[]{:S(2)}) collective-permute-start(bf16[4,2,64,1024]{3,2,1,0:T(8,128)(2,1)S(1)} %pad_maximum_fusion.3), channel_id=1, source_target_pairs={{0,16},{4,52},{8,24},{12,60},{16,0},{20,36},{24,8},{28,44},{32,48}... | collective-permute-start | bytes 3145736 | tf_op jit(solution)/shard_map/ppermute | solution.py:46
  53.1 5.5 %collective-permute-start.19 = (bf16[128,1024]{1,0:T(8,128)(2,1)S(1)}, bf16[128,1024]{1,0:T(8,128)(2,1)S(1)}, u32[]{:S(2)}, u32[]{:S(2)}) collective-permute-start(bf16[128,1024]{1,0:T(8,128)(2,1)S(1)} %attend_suffix_0.1.a_s), channel_id=1, source_target_pairs={{0,1},{1,0},{2,3},{3,2},{4,7},{5,6},{6,5},{7,4},{8,9},{9,8},{10,11... | collective-permute-start | bytes 786440 | tf_op jit(solution)/shard_map/ppermute | solution.py:51
  58.6 2.5 %attend_prompt_0.1.a_p = bf16[128,1024]{1,0:T(8,128)(2,1)S(1)} custom-call(s32[68]{0:T(128)S(1)} %concatenate.67.info, bf16[128,1024]{1,0:T(8,128)(2,1)S(1)} %copy-done.1, bf16[128,128]{1,0:T(8,128)(2,1)S(1)} %copy-done.2, bf16[128,128]{1,0:T(8,128)(2,1)S(1)} %copy-done.3, bf16[16,128,256]{2,1,0:T(8,128)(2,1)S(1)} %constant_dynamic-update-slice_fusion.refs_0_, ...), custom_call_target="tpu_custom_call" | custom-call | tf_op jit(solution)/shard_map/attend_prompt_0/pallas_call | solution.py:151
  61.1 3.6 %collective-permute-done.19.near_s = bf16[128,1024]{1,0:T(8,128)(2,1)S(1)} collective-permute-done((bf16[128,1024]{1,0:T(8,128)(2,1)S(1)}, bf16[128,1024]{1,0:T(8,128)(2,1)S(1)}, u32[]{:S(2)}, u32[]{:S(2)}) %collective-permute-start.19) | collective-permute-done | bytes 262176 | tf_op jit(solution)/shard_map/ppermute | solution.py:51
  64.8 2.1 %collective-permute-done.22 = bf16[4,2,64,1024]{3,2,1,0:T(8,128)(2,1)S(1)} collective-permute-done((bf16[4,2,64,1024]{3,2,1,0:T(8,128)(2,1)S(1)}, bf16[4,2,64,1024]{3,2,1,0:T(8,128)(2,1)S(1)}, u32[]{:S(2)}, u32[]{:S(2)}) %collective-permute-start.22) | collective-permute-done | bytes 1048608 | tf_op jit(solution)/shard_map/ppermute | solution.py:46
  67.8 3.1 %collective-permute-start.20 = (bf16[3,128,1024]{2,1,0:T(8,128)(2,1)S(1)}, bf16[3,128,1024]{2,1,0:T(8,128)(2,1)S(1)}, u32[]{:S(2)}, u32[]{:S(2)}) collective-permute-start(bf16[3,128,1024]{2,1,0:T(8,128)(2,1)S(1)} %pad_maximum_fusion.4), channel_id=1, source_target_pairs={{0,3},{1,2},{2,1},{3,0},{4,5},{5,4},{6,7},{7,6},{8,11},{9,10},{10,... | collective-permute-start | bytes 2359304 | tf_op jit(solution)/shard_map/ppermute | solution.py:51
  70.9 5.1 %collective-permute-start.26 = (bf16[8,2,64,1024]{3,2,1,0:T(8,128)(2,1)S(1)}, bf16[8,2,64,1024]{3,2,1,0:T(8,128)(2,1)S(1)}, u32[]{:S(2)}, u32[]{:S(2)}) collective-permute-start(bf16[8,2,64,1024]{3,2,1,0:T(8,128)(2,1)S(1)} %pad_maximum_fusion.refs_0_), channel_id=1, source_target_pairs={{0,4},{4,0},{8,12},{12,8},{16,20},{20,16},{24,28},{28,24},{32,36},... | collective-permute-start | bytes 6291464 | tf_op jit(solution)/shard_map/ppermute | solution.py:46
  76.0 13.1 %collective-permute-done.20.mixed = bf16[3,128,1024]{2,1,0:T(8,128)(2,1)S(1)} collective-permute-done((bf16[3,128,1024]{2,1,0:T(8,128)(2,1)S(1)}, bf16[3,128,1024]{2,1,0:T(8,128)(2,1)S(1)}, u32[]{:S(2)}, u32[]{:S(2)}) %collective-permute-start.20) | collective-permute-done | bytes 786464 | tf_op jit(solution)/shard_map/ppermute | solution.py:51
  89.1 3.3 %collective-permute-done.23.refs_1_ = bf16[8,2,64,1024]{3,2,1,0:T(8,128)(2,1)S(1)} collective-permute-done((bf16[8,2,64,1024]{3,2,1,0:T(8,128)(2,1)S(1)}, bf16[8,2,64,1024]{3,2,1,0:T(8,128)(2,1)S(1)}, u32[]{:S(2)}, u32[]{:S(2)}) %collective-permute-start.23) | collective-permute-done | bytes 2097184 | tf_op jit(solution)/shard_map/ppermute | solution.py:46
  92.4 1.6 %collective-permute-start.27 = (bf16[8,2,64,1024]{3,2,1,0:T(8,128)(2,1)S(1)}, bf16[8,2,64,1024]{3,2,1,0:T(8,128)(2,1)S(1)}, u32[]{:S(2)}, u32[]{:S(2)}) collective-permute-start(bf16[8,2,64,1024]{3,2,1,0:T(8,128)(2,1)S(1)} %collective-permute-done.23.refs_1_), channel_id=1, source_target_pairs={{0,4},{4,0},{8,12},{12,8},{16,20},{20,16},{24,28},{28,24},{32,36},... | collective-permute-start | bytes 6291464 | tf_op jit(solution)/shard_map/ppermute | solution.py:46
  93.9 1.6 %collective-permute-start.29 = (bf16[8,2,64,1024]{3,2,1,0:T(8,128)(2,1)S(1)}, bf16[8,2,64,1024]{3,2,1,0:T(8,128)(2,1)S(1)}, u32[]{:S(2)}, u32[]{:S(2)}) collective-permute-start(bf16[8,2,64,1024]{3,2,1,0:T(8,128)(2,1)S(1)} %collective-permute-done.25.refs_3_), channel_id=1, source_target_pairs={{0,4},{4,0},{8,12},{12,8},{16,20},{20,16},{24,28},{28,24},{32,36},... | collective-permute-start | bytes 6291464 | tf_op jit(solution)/shard_map/ppermute | solution.py:46
  95.7 5.2 %collective-permute-start.21 = (bf16[2,128,1024]{2,1,0:T(8,128)(2,1)S(1)}, bf16[2,128,1024]{2,1,0:T(8,128)(2,1)S(1)}, u32[]{:S(2)}, u32[]{:S(2)}) collective-permute-start(bf16[2,128,1024]{2,1,0:T(8,128)(2,1)S(1)} %pad_maximum_fusion.9), channel_id=1, source_target_pairs={{0,1},{1,0},{2,3},{3,2},{4,7},{5,6},{6,5},{7,4},{8,9},{9,8},{10,11... | collective-permute-start | bytes 1572872 | tf_op jit(solution)/shard_map/ppermute | solution.py:51
  100.9 9.6 %collective-permute-done.21.far_p = bf16[2,128,1024]{2,1,0:T(8,128)(2,1)S(1)} collective-permute-done((bf16[2,128,1024]{2,1,0:T(8,128)(2,1)S(1)}, bf16[2,128,1024]{2,1,0:T(8,128)(2,1)S(1)}, u32[]{:S(2)}, u32[]{:S(2)}) %collective-permute-start.21) | collective-permute-done | bytes 524320 | tf_op jit(solution)/shard_map/ppermute | solution.py:51
  110.5 6.2 %project.1 = (bf16[128,2048]{1,0:T(8,128)(2,1)}, bf16[128,2048]{1,0:T(8,128)(2,1)}) custom-call(s32[68]{0:T(128)S(1)} %concatenate.67.info, bf16[128,1024]{1,0:T(8,128)(2,1)S(1)} %attend_prompt_0.1.a_p, bf16[128,1024]{1,0:T(8,128)(2,1)S(1)} %attend_suffix_0.1.a_s, bf16[128,1024]{1,0:T(8,128)(2,1)S(1)} %collective-permute-done.19.near_s, ...), custom_call_target="tpu_custom_call" | custom-call | tf_op jit(solution)/shard_map/project/pallas_call | solution.py:196
  (81 shorter events, 6.6 us)
Async XLA Ops:
  0.6 6.0 %collective-permute-start = (bf16[128,128]{1,0:T(8,128)(2,1)}, bf16[128,128]{1,0:T(8,128)(2,1)S(1)}, u32[]{:S(2)}, u32[]{:S(2)}) collective-permute-start(bf16[128,128]{1,0:T(8,128)(2,1)} %own_k.3), channel_id=1, source_target_pairs={{0,8},{4,12},{8,0},{12,4},{16,24},{20,28},{24,16},{28,20},{32,40},... | collective-permute-start | bytes 98312 | tf_op jit(solution)/shard_map/ppermute | solution.py:46
  3.2 3.5 %collective-permute-start.8 = (bf16[128,128]{1,0:T(8,128)(2,1)}, bf16[128,128]{1,0:T(8,128)(2,1)S(1)}, u32[]{:S(2)}, u32[]{:S(2)}) collective-permute-start(bf16[128,128]{1,0:T(8,128)(2,1)} %own_v.3), channel_id=1, source_target_pairs={{0,8},{4,12},{8,0},{12,4},{16,24},{20,28},{24,16},{28,20},{32,40},... | collective-permute-start | bytes 98312 | tf_op jit(solution)/shard_map/ppermute | solution.py:46
  4.1 6.8 %collective-permute-start.2 = (bf16[1,128,256]{2,1,0:T(8,128)(2,1)S(1)}, bf16[1,128,256]{2,1,0:T(8,128)(2,1)S(1)}, u32[]{:S(2)}, u32[]{:S(2)}) collective-permute-start(bf16[1,128,256]{2,1,0:T(8,128)(2,1)S(1)} %bitcast.27), channel_id=1, source_target_pairs={{0,16},{4,52},{8,24},{12,60},{16,0},{20,36},{24,8},{28,44},{32,48}... | collective-permute-start | bytes 196616 | tf_op jit(solution)/shard_map/ppermute | solution.py:46
  6.7 5.7 %collective-permute-start.9 = (bf16[1,128,256]{2,1,0:T(8,128)(2,1)S(1)}, bf16[1,128,256]{2,1,0:T(8,128)(2,1)S(1)}, u32[]{:S(2)}, u32[]{:S(2)}) collective-permute-start(bf16[1,128,256]{2,1,0:T(8,128)(2,1)S(1)} %maximum_bitcast_fusion.2), channel_id=1, source_target_pairs={{0,64},{4,196},{8,72},{12,204},{16,80},{20,212},{24,88},{28,220},{... | collective-permute-start | bytes 196616 | tf_op jit(solution)/shard_map/ppermute | solution.py:46
  9.5 7.7 %collective-permute-start.1 = (bf16[64,2048]{1,0:T(8,128)(2,1)}, bf16[64,2048]{1,0:T(8,128)(2,1)S(1)}, u32[]{:S(2)}, u32[]{:S(2)}) collective-permute-start(bf16[64,2048]{1,0:T(8,128)(2,1)} %param.17), channel_id=1, source_target_pairs={{0,8},{4,12},{8,0},{12,4},{16,24},{20,28},{24,16},{28,20},{32,40},... | collective-permute-start | bytes 786440 | tf_op jit(solution)/shard_map/ppermute | solution.py:46
  10.9 4.2 %collective-permute-start.3 = (bf16[2,128,256]{2,1,0:T(8,128)(2,1)S(1)}, bf16[2,128,256]{2,1,0:T(8,128)(2,1)S(1)}, u32[]{:S(2)}, u32[]{:S(2)}) collective-permute-start(bf16[2,128,256]{2,1,0:T(8,128)(2,1)S(1)} %pad_maximum_fusion.12), channel_id=1, source_target_pairs={{0,48},{4,20},{8,56},{12,28},{16,32},{20,4},{24,40},{28,12},{32,16... | collective-permute-start | bytes 393224 | tf_op jit(solution)/shard_map/ppermute | solution.py:46
  12.5 10.0 %collective-permute-start.10 = (bf16[2,128,256]{2,1,0:T(8,128)(2,1)S(1)}, bf16[2,128,256]{2,1,0:T(8,128)(2,1)S(1)}, u32[]{:S(2)}, u32[]{:S(2)}) collective-permute-start(bf16[2,128,256]{2,1,0:T(8,128)(2,1)S(1)} %pad_maximum_fusion.13), channel_id=1, source_target_pairs={{0,192},{4,68},{8,200},{12,76},{16,208},{20,84},{24,216},{28,92},{... | collective-permute-start | bytes 393224 | tf_op jit(solution)/shard_map/ppermute | solution.py:46
  18.3 6.5 %collective-permute-start.4 = (bf16[4,128,256]{2,1,0:T(8,128)(2,1)S(1)}, bf16[4,128,256]{2,1,0:T(8,128)(2,1)S(1)}, u32[]{:S(2)}, u32[]{:S(2)}) collective-permute-start(bf16[4,128,256]{2,1,0:T(8,128)(2,1)S(1)} %pad_maximum_fusion.10), channel_id=1, source_target_pairs={{0,64},{4,196},{8,72},{12,204},{16,80},{20,212},{24,88},{28,220},{... | collective-permute-start | bytes 786440 | tf_op jit(solution)/shard_map/ppermute | solution.py:46
  18.4 9.2 %collective-permute-start.6 = (bf16[1,2,64,1024]{3,2,1,0:T(8,128)(2,1)S(1)}, bf16[1,2,64,1024]{3,2,1,0:T(8,128)(2,1)S(1)}, u32[]{:S(2)}, u32[]{:S(2)}) collective-permute-start(bf16[1,2,64,1024]{3,2,1,0:T(8,128)(2,1)S(1)} %maximum_bitcast_fusion.1), channel_id=1, source_target_pairs={{0,64},{4,196},{8,72},{12,204},{16,80},{20,212},{24,88},{28,220},{... | collective-permute-start | bytes 786440 | tf_op jit(solution)/shard_map/ppermute | solution.py:46
  21.2 6.5 %collective-permute-start.5 = (bf16[1,2,64,1024]{3,2,1,0:T(8,128)(2,1)S(1)}, bf16[1,2,64,1024]{3,2,1,0:T(8,128)(2,1)S(1)}, u32[]{:S(2)}, u32[]{:S(2)}) collective-permute-start(bf16[1,2,64,1024]{3,2,1,0:T(8,128)(2,1)S(1)} %maximum_bitcast_fusion), channel_id=1, source_target_pairs={{0,16},{4,52},{8,24},{12,60},{16,0},{20,36},{24,8},{28,44},{32,48}... | collective-permute-start | bytes 786440 | tf_op jit(solution)/shard_map/ppermute | solution.py:46
  22.5 7.9 %collective-permute-start.11 = (bf16[4,128,256]{2,1,0:T(8,128)(2,1)S(1)}, bf16[4,128,256]{2,1,0:T(8,128)(2,1)S(1)}, u32[]{:S(2)}, u32[]{:S(2)}) collective-permute-start(bf16[4,128,256]{2,1,0:T(8,128)(2,1)S(1)} %pad_maximum_fusion.11), channel_id=1, source_target_pairs={{0,16},{4,52},{8,24},{12,60},{16,0},{20,36},{24,8},{28,44},{32,48}... | collective-permute-start | bytes 786440 | tf_op jit(solution)/shard_map/ppermute | solution.py:46
  24.9 14.6 %collective-permute-start.13 = (bf16[8,128,256]{2,1,0:T(8,128)(2,1)S(1)}, bf16[8,128,256]{2,1,0:T(8,128)(2,1)S(1)}, u32[]{:S(2)}, u32[]{:S(2)}) collective-permute-start(bf16[8,128,256]{2,1,0:T(8,128)(2,1)S(1)} %pad_maximum_fusion.5), channel_id=1, source_target_pairs={{0,4},{4,0},{8,12},{12,8},{16,20},{20,16},{24,28},{28,24},{32,36},... | collective-permute-start | bytes 1572872 | tf_op jit(solution)/shard_map/ppermute | solution.py:46
  27.8 8.4 %collective-permute-start.7 = (bf16[8,128,256]{2,1,0:T(8,128)(2,1)S(1)}, bf16[8,128,256]{2,1,0:T(8,128)(2,1)S(1)}, u32[]{:S(2)}, u32[]{:S(2)}) collective-permute-start(bf16[8,128,256]{2,1,0:T(8,128)(2,1)S(1)} %pad_maximum_fusion.5), channel_id=1, source_target_pairs={{0,192},{4,68},{8,200},{12,76},{16,208},{20,84},{24,216},{28,92},{... | collective-permute-start | bytes 1572872 | tf_op jit(solution)/shard_map/ppermute | solution.py:46
  30.5 9.1 %collective-permute-start.12 = (bf16[8,128,256]{2,1,0:T(8,128)(2,1)S(1)}, bf16[8,128,256]{2,1,0:T(8,128)(2,1)S(1)}, u32[]{:S(2)}, u32[]{:S(2)}) collective-permute-start(bf16[8,128,256]{2,1,0:T(8,128)(2,1)S(1)} %pad_maximum_fusion.8), channel_id=1, source_target_pairs={{0,48},{4,20},{8,56},{12,28},{16,32},{20,4},{24,40},{28,12},{32,16... | collective-permute-start | bytes 1572872 | tf_op jit(solution)/shard_map/ppermute | solution.py:46
  30.6 10.9 %collective-permute-start.15 = (bf16[8,128,256]{2,1,0:T(8,128)(2,1)S(1)}, bf16[8,128,256]{2,1,0:T(8,128)(2,1)S(1)}, u32[]{:S(2)}, u32[]{:S(2)}) collective-permute-start(bf16[8,128,256]{2,1,0:T(8,128)(2,1)S(1)} %pad_maximum_fusion.8), channel_id=1, source_target_pairs={{0,4},{4,0},{8,12},{12,8},{16,20},{20,16},{24,28},{28,24},{32,36},... | collective-permute-start | bytes 1572872 | tf_op jit(solution)/shard_map/ppermute | solution.py:46
  33.4 16.3 %collective-permute-start.17 = (bf16[2,2,64,1024]{3,2,1,0:T(8,128)(2,1)S(1)}, bf16[2,2,64,1024]{3,2,1,0:T(8,128)(2,1)S(1)}, u32[]{:S(2)}, u32[]{:S(2)}) collective-permute-start(bf16[2,2,64,1024]{3,2,1,0:T(8,128)(2,1)S(1)} %pad_maximum_fusion.6), channel_id=1, source_target_pairs={{0,48},{4,20},{8,56},{12,28},{16,32},{20,4},{24,40},{28,12},{32,16... | collective-permute-start | bytes 1572872 | tf_op jit(solution)/shard_map/ppermute | solution.py:46
  36.2 5.5 %collective-permute-start.14 = (bf16[8,128,256]{2,1,0:T(8,128)(2,1)S(1)}, bf16[8,128,256]{2,1,0:T(8,128)(2,1)S(1)}, u32[]{:S(2)}, u32[]{:S(2)}) collective-permute-start(bf16[8,128,256]{2,1,0:T(8,128)(2,1)S(1)} %collective-permute-done.7), channel_id=1, source_target_pairs={{0,4},{4,0},{8,12},{12,8},{16,20},{20,16},{24,28},{28,24},{32,36},... | collective-permute-start | bytes 1572872 | tf_op jit(solution)/shard_map/ppermute | solution.py:46
  39.5 10.2 %collective-permute-start.18 = (bf16[2,2,64,1024]{3,2,1,0:T(8,128)(2,1)S(1)}, bf16[2,2,64,1024]{3,2,1,0:T(8,128)(2,1)S(1)}, u32[]{:S(2)}, u32[]{:S(2)}) collective-permute-start(bf16[2,2,64,1024]{3,2,1,0:T(8,128)(2,1)S(1)} %pad_maximum_fusion.7), channel_id=1, source_target_pairs={{0,192},{4,68},{8,200},{12,76},{16,208},{20,84},{24,216},{28,92},{... | collective-permute-start | bytes 1572872 | tf_op jit(solution)/shard_map/ppermute | solution.py:46
  39.6 3.5 %collective-permute-start.16 = (bf16[8,128,256]{2,1,0:T(8,128)(2,1)S(1)}, bf16[8,128,256]{2,1,0:T(8,128)(2,1)S(1)}, u32[]{:S(2)}, u32[]{:S(2)}) collective-permute-start(bf16[8,128,256]{2,1,0:T(8,128)(2,1)S(1)} %collective-permute-done.12), channel_id=1, source_target_pairs={{0,4},{4,0},{8,12},{12,8},{16,20},{20,16},{24,28},{28,24},{32,36},... | collective-permute-start | bytes 1572872 | tf_op jit(solution)/shard_map/ppermute | solution.py:46
  49.6 9.0 %copy-start.1 = (bf16[128,1024]{1,0:T(8,128)(2,1)S(1)}, bf16[128,1024]{1,0:T(8,128)(2,1)}, u32[]{:S(2)}) copy-start(bf16[128,1024]{1,0:T(8,128)(2,1)} %q.2) | copy-start | bytes 786436
  49.7 8.9 %copy-start.2 = (bf16[128,128]{1,0:T(8,128)(2,1)S(1)}, bf16[128,128]{1,0:T(8,128)(2,1)}, u32[]{:S(2)}) copy-start(bf16[128,128]{1,0:T(8,128)(2,1)} %own_k.3) | copy-start | bytes 98308
  49.8 14.9 %collective-permute-start.24 = (bf16[4,2,64,1024]{3,2,1,0:T(8,128)(2,1)S(1)}, bf16[4,2,64,1024]{3,2,1,0:T(8,128)(2,1)S(1)}, u32[]{:S(2)}, u32[]{:S(2)}) collective-permute-start(bf16[4,2,64,1024]{3,2,1,0:T(8,128)(2,1)S(1)} %pad_maximum_fusion.3), channel_id=1, source_target_pairs={{0,16},{4,52},{8,24},{12,60},{16,0},{20,36},{24,8},{28,44},{32,48}... | collective-permute-start | bytes 3145736 | tf_op jit(solution)/shard_map/ppermute | solution.py:46
  51.9 14.9 %collective-permute-start.22 = (bf16[4,2,64,1024]{3,2,1,0:T(8,128)(2,1)S(1)}, bf16[4,2,64,1024]{3,2,1,0:T(8,128)(2,1)S(1)}, u32[]{:S(2)}, u32[]{:S(2)}) collective-permute-start(bf16[4,2,64,1024]{3,2,1,0:T(8,128)(2,1)S(1)} %pad_maximum_fusion.2), channel_id=1, source_target_pairs={{0,64},{4,196},{8,72},{12,204},{16,80},{20,212},{24,88},{28,220},{... | collective-permute-start | bytes 3145736 | tf_op jit(solution)/shard_map/ppermute | solution.py:46
  53.1 11.7 %collective-permute-start.19 = (bf16[128,1024]{1,0:T(8,128)(2,1)S(1)}, bf16[128,1024]{1,0:T(8,128)(2,1)S(1)}, u32[]{:S(2)}, u32[]{:S(2)}) collective-permute-start(bf16[128,1024]{1,0:T(8,128)(2,1)S(1)} %attend_suffix_0.1.a_s), channel_id=1, source_target_pairs={{0,1},{1,0},{2,3},{3,2},{4,7},{5,6},{6,5},{7,4},{8,9},{9,8},{10,11... | collective-permute-start | bytes 786440 | tf_op jit(solution)/shard_map/ppermute | solution.py:51
  67.1 25.3 %collective-permute-start.23 = (bf16[8,2,64,1024]{3,2,1,0:T(8,128)(2,1)S(1)}, bf16[8,2,64,1024]{3,2,1,0:T(8,128)(2,1)S(1)}, u32[]{:S(2)}, u32[]{:S(2)}) collective-permute-start(bf16[8,2,64,1024]{3,2,1,0:T(8,128)(2,1)S(1)} %pad_maximum_fusion.refs_0_), channel_id=1, source_target_pairs={{0,192},{4,68},{8,200},{12,76},{16,208},{20,84},{24,216},{28,92},{... | collective-permute-start | bytes 6291464 | tf_op jit(solution)/shard_map/ppermute | solution.py:46
  67.4 26.5 %collective-permute-start.25 = (bf16[8,2,64,1024]{3,2,1,0:T(8,128)(2,1)S(1)}, bf16[8,2,64,1024]{3,2,1,0:T(8,128)(2,1)S(1)}, u32[]{:S(2)}, u32[]{:S(2)}) collective-permute-start(bf16[8,2,64,1024]{3,2,1,0:T(8,128)(2,1)S(1)} %pad_maximum_fusion.1.refs_2_), channel_id=1, source_target_pairs={{0,48},{4,20},{8,56},{12,28},{16,32},{20,4},{24,40},{28,12},{32,16... | collective-permute-start | bytes 6291464 | tf_op jit(solution)/shard_map/ppermute | solution.py:46
  67.8 21.2 %collective-permute-start.20 = (bf16[3,128,1024]{2,1,0:T(8,128)(2,1)S(1)}, bf16[3,128,1024]{2,1,0:T(8,128)(2,1)S(1)}, u32[]{:S(2)}, u32[]{:S(2)}) collective-permute-start(bf16[3,128,1024]{2,1,0:T(8,128)(2,1)S(1)} %pad_maximum_fusion.4), channel_id=1, source_target_pairs={{0,3},{1,2},{2,1},{3,0},{4,5},{5,4},{6,7},{7,6},{8,11},{9,10},{10,... | collective-permute-start | bytes 2359304 | tf_op jit(solution)/shard_map/ppermute | solution.py:51
  70.9 39.6 %collective-permute-start.26 = (bf16[8,2,64,1024]{3,2,1,0:T(8,128)(2,1)S(1)}, bf16[8,2,64,1024]{3,2,1,0:T(8,128)(2,1)S(1)}, u32[]{:S(2)}, u32[]{:S(2)}) collective-permute-start(bf16[8,2,64,1024]{3,2,1,0:T(8,128)(2,1)S(1)} %pad_maximum_fusion.refs_0_), channel_id=1, source_target_pairs={{0,4},{4,0},{8,12},{12,8},{16,20},{20,16},{24,28},{28,24},{32,36},... | collective-permute-start | bytes 6291464 | tf_op jit(solution)/shard_map/ppermute | solution.py:46
  76.0 34.5 %collective-permute-start.28 = (bf16[8,2,64,1024]{3,2,1,0:T(8,128)(2,1)S(1)}, bf16[8,2,64,1024]{3,2,1,0:T(8,128)(2,1)S(1)}, u32[]{:S(2)}, u32[]{:S(2)}) collective-permute-start(bf16[8,2,64,1024]{3,2,1,0:T(8,128)(2,1)S(1)} %pad_maximum_fusion.1.refs_2_), channel_id=1, source_target_pairs={{0,4},{4,0},{8,12},{12,8},{16,20},{20,16},{24,28},{28,24},{32,36},... | collective-permute-start | bytes 6291464 | tf_op jit(solution)/shard_map/ppermute | solution.py:46
  92.4 18.1 %collective-permute-start.27 = (bf16[8,2,64,1024]{3,2,1,0:T(8,128)(2,1)S(1)}, bf16[8,2,64,1024]{3,2,1,0:T(8,128)(2,1)S(1)}, u32[]{:S(2)}, u32[]{:S(2)}) collective-permute-start(bf16[8,2,64,1024]{3,2,1,0:T(8,128)(2,1)S(1)} %collective-permute-done.23.refs_1_), channel_id=1, source_target_pairs={{0,4},{4,0},{8,12},{12,8},{16,20},{20,16},{24,28},{28,24},{32,36},... | collective-permute-start | bytes 6291464 | tf_op jit(solution)/shard_map/ppermute | solution.py:46
  93.9 16.6 %collective-permute-start.29 = (bf16[8,2,64,1024]{3,2,1,0:T(8,128)(2,1)S(1)}, bf16[8,2,64,1024]{3,2,1,0:T(8,128)(2,1)S(1)}, u32[]{:S(2)}, u32[]{:S(2)}) collective-permute-start(bf16[8,2,64,1024]{3,2,1,0:T(8,128)(2,1)S(1)} %collective-permute-done.25.refs_3_), channel_id=1, source_target_pairs={{0,4},{4,0},{8,12},{12,8},{16,20},{20,16},{24,28},{28,24},{32,36},... | collective-permute-start | bytes 6291464 | tf_op jit(solution)/shard_map/ppermute | solution.py:46
  95.7 14.8 %collective-permute-start.21 = (bf16[2,128,1024]{2,1,0:T(8,128)(2,1)S(1)}, bf16[2,128,1024]{2,1,0:T(8,128)(2,1)S(1)}, u32[]{:S(2)}, u32[]{:S(2)}) collective-permute-start(bf16[2,128,1024]{2,1,0:T(8,128)(2,1)S(1)} %pad_maximum_fusion.9), channel_id=1, source_target_pairs={{0,1},{1,0},{2,3},{3,2},{4,7},{5,6},{6,5},{7,4},{8,9},{9,8},{10,11... | collective-permute-start | bytes 1572872 | tf_op jit(solution)/shard_map/ppermute | solution.py:51
  (4 other events, 13.4 us)

commit v4 on v3

--- a/solution.py
+++ b/solution.py
@@ -224,7 +224,7 @@
     kv = join(kv, gather_step([after(a, *w) for a in kv], 2))
     w = join(w, w_came)
     w_came = gather_step(w, 1)
-    came = gather_step([after(a, *w) for a in kv], 3)
+    came = gather_step(kv, 3)
     kv_mate = [swap(a, 1) for a in kv]
     came_mate = [swap(a, 1) for a in came]
     blocks = [*join(kv, came), *join(kv_mate, came_mate)]
@@ -237,14 +237,13 @@
     near_s = swap_tensor(a_s, (1, 3))
     a_p = attend(True, 0, 8, info, after(prompt_q, *w), prompt_k, prompt_v, blocks)
     a_s, near_s, a_p = lax.optimization_barrier((a_s, near_s, a_p))
+    mixed = swap_tensor(jnp.stack([a_s, near_s, a_p]), (3, 1))
     w = join(w, [after(a, a_p) for a in w_3])
-
-    mixed = swap_tensor(jnp.stack([a_s, near_s, a_p]), (3, 1))
     w_came = gather_step(w, 3)
     far_p = swap_tensor(jnp.stack([a_p, mixed[2]]), (1, 3))
     w_mate = [swap(a, 1) for a in w]
     w_came = [after(a, mixed) for a in w_came]
-    w_came_mate = [swap(a, 1) for a in w_came]
+    w_came_mate = [swap(w_came[0], 1), swap(after(w_came[1], far_p), 1)]
     weights = [w[0], w_came[0], w[1], w_came[1],
                w_mate[0], w_came_mate[0], w_mate[1], w_came_mate[1]]
     return tuple(project(info, [a_p, a_s, near_s, mixed, far_p], weights))

time: 118 us -> 117 us (level); the launches traced: 117 us -> 117 us
  waiting for transfers between devices: 45.3 us -> 51.2 us
  starting transfers between devices: 50.4 us -> 45 us
    ppermute x3, waiting for transfers between devices: 26.3 us -> 31 us  [swap_tensor(): return lax.ppermute(x, ('sample', 'tensor'), pairs)]
    ppermute x3, starting transfers between devices: 13.8 us -> 10.6 us  [swap_tensor(): return lax.ppermute(x, ('sample', 'tensor'), pairs)]
    ppermute x27, starting transfers between devices: 36.6 us -> 34.4 us  [swap(): return lax.ppermute(x, 'sample', [(s, s ^ masks[s & 1]) for s in range(64)])]
    ppermute x27, waiting for transfers between devices: 19 us -> 20.3 us  [swap(): return lax.ppermute(x, 'sample', [(s, s ^ masks[s & 1]) for s in range(64)])]
  transfers between devices with their start and end apart: 30 -> 30, of which waited for: 12 -> 14; matrix products, arithmetic and copies ran while one was open for 3% -> 3% of each run, Pallas kernels for 8% -> 8%
where the time goes in v4:
time: 117 us
  waiting for transfers between devices  51.2 us (44%)
  starting transfers between devices  45 us (38%)
  Pallas kernels  15.2 us (13%)
  between operations  2.37 us (2%)
  other arithmetic  1.96 us (2%)
  local copies, waits for them, and re-layouts  1.43 us (1%)
    ppermute x27, starting transfers between devices, swap(): return lax.ppermute(x, 'sample', [(s, s ^ masks[s & 1]) for s in range(64)])  34.4 us
    ppermute x3, waiting for transfers between devices, swap_tensor(): return lax.ppermute(x, ('sample', 'tensor'), pairs)  31 us
    ppermute x27, waiting for transfers between devices, swap(): return lax.ppermute(x, 'sample', [(s, s ^ masks[s & 1]) for s in range(64)])  20.3 us
    ppermute x3, starting transfers between devices, swap_tensor(): return lax.ppermute(x, ('sample', 'tensor'), pairs)  10.6 us
    pallas_call x2, Pallas kernels, attend(): pl.pallas_call(functools.partial(attend_kernel, is_prompt, first, count),...  9 us
    pallas_call x1, Pallas kernels, project(): pl.pallas_call(project_kernel, out_shape=[jax.ShapeDtypeStruct((ROWS, 204...  6.18 us
  transfers between devices with their start and end apart: 30, of which 14 were waited for; matrix products, arithmetic and copies ran while one was open for 3% of the time, Pallas kernels for 8%

profile of v4, /device:TPU:1, one launch (start us, length us, event | category | flops | bytes accessed | tf_op | source)
XLA Modules:
  0.0 117.2 jit_solution(469923384214802533)
XLA Ops:
  0.6 2.6 %collective-permute-start = (bf16[128,128]{1,0:T(8,128)(2,1)}, bf16[128,128]{1,0:T(8,128)(2,1)S(1)}, u32[]{:S(2)}, u32[]{:S(2)}) collective-permute-start(bf16[128,128]{1,0:T(8,128)(2,1)} %own_k.3), channel_id=1, source_target_pairs={{0,8},{4,12},{8,0},{12,4},{16,24},{20,28},{24,16},{28,20},{32,40},... | collective-permute-start | bytes 98312 | tf_op jit(solution)/shard_map/ppermute | solution.py:46
  3.3 0.8 pad_maximum_fusion.14
  4.1 2.6 %collective-permute-start.2 = (bf16[1,128,256]{2,1,0:T(8,128)(2,1)S(1)}, bf16[1,128,256]{2,1,0:T(8,128)(2,1)S(1)}, u32[]{:S(2)}, u32[]{:S(2)}) collective-permute-start(bf16[1,128,256]{2,1,0:T(8,128)(2,1)S(1)} %bitcast.27), channel_id=1, source_target_pairs={{0,16},{4,52},{8,24},{12,60},{16,0},{20,36},{24,8},{28,44},{32,48}... | collective-permute-start | bytes 196616 | tf_op jit(solution)/shard_map/ppermute | solution.py:46
  8.1 2.8 %collective-permute-start.7 = (bf16[1,128,256]{2,1,0:T(8,128)(2,1)S(1)}, bf16[1,128,256]{2,1,0:T(8,128)(2,1)S(1)}, u32[]{:S(2)}, u32[]{:S(2)}) collective-permute-start(bf16[1,128,256]{2,1,0:T(8,128)(2,1)S(1)} %maximum_bitcast_fusion.2), channel_id=1, source_target_pairs={{0,64},{4,196},{8,72},{12,204},{16,80},{20,212},{24,88},{28,220},{... | collective-permute-start | bytes 196616 | tf_op jit(solution)/shard_map/ppermute | solution.py:46
  10.9 1.4 %collective-permute-start.1 = (bf16[64,2048]{1,0:T(8,128)(2,1)}, bf16[64,2048]{1,0:T(8,128)(2,1)S(1)}, u32[]{:S(2)}, u32[]{:S(2)}) collective-permute-start(bf16[64,2048]{1,0:T(8,128)(2,1)} %param.17), channel_id=1, source_target_pairs={{0,8},{4,12},{8,0},{12,4},{16,24},{20,28},{24,16},{28,20},{32,40},... | collective-permute-start | bytes 786440 | tf_op jit(solution)/shard_map/ppermute | solution.py:46
  13.0 3.5 %collective-permute-done.3 = bf16[2,128,256]{2,1,0:T(8,128)(2,1)S(1)} collective-permute-done((bf16[2,128,256]{2,1,0:T(8,128)(2,1)S(1)}, bf16[2,128,256]{2,1,0:T(8,128)(2,1)S(1)}, u32[]{:S(2)}, u32[]{:S(2)}) %collective-permute-start.3) | collective-permute-done | bytes 131104 | tf_op jit(solution)/shard_map/ppermute | solution.py:46
  16.6 2.4 %collective-permute-done.1 = bf16[64,2048]{1,0:T(8,128)(2,1)S(1)} collective-permute-done((bf16[64,2048]{1,0:T(8,128)(2,1)}, bf16[64,2048]{1,0:T(8,128)(2,1)S(1)}, u32[]{:S(2)}, u32[]{:S(2)}) %collective-permute-start.1) | collective-permute-done | bytes 262176 | tf_op jit(solution)/shard_map/ppermute | solution.py:46
  18.9 1.0 slice_bitcast_fusion.1
  20.3 2.7 %collective-permute-start.15 = (bf16[1,2,64,1024]{3,2,1,0:T(8,128)(2,1)S(1)}, bf16[1,2,64,1024]{3,2,1,0:T(8,128)(2,1)S(1)}, u32[]{:S(2)}, u32[]{:S(2)}) collective-permute-start(bf16[1,2,64,1024]{3,2,1,0:T(8,128)(2,1)S(1)} %maximum_bitcast_fusion), channel_id=1, source_target_pairs={{0,16},{4,52},{8,24},{12,60},{16,0},{20,36},{24,8},{28,44},{32,48}... | collective-permute-start | bytes 786440 | tf_op jit(solution)/shard_map/ppermute | solution.py:46
  23.0 2.7 %collective-permute-start.17 = (bf16[1,2,64,1024]{3,2,1,0:T(8,128)(2,1)S(1)}, bf16[1,2,64,1024]{3,2,1,0:T(8,128)(2,1)S(1)}, u32[]{:S(2)}, u32[]{:S(2)}) collective-permute-start(bf16[1,2,64,1024]{3,2,1,0:T(8,128)(2,1)S(1)} %maximum_bitcast_fusion.1), channel_id=1, source_target_pairs={{0,64},{4,196},{8,72},{12,204},{16,80},{20,212},{24,88},{28,220},{... | collective-permute-start | bytes 786440 | tf_op jit(solution)/shard_map/ppermute | solution.py:46
  25.7 0.9 collective-permute-done.4
  27.7 1.8 %collective-permute-done.15 = bf16[1,2,64,1024]{3,2,1,0:T(8,128)(2,1)S(1)} collective-permute-done((bf16[1,2,64,1024]{3,2,1,0:T(8,128)(2,1)S(1)}, bf16[1,2,64,1024]{3,2,1,0:T(8,128)(2,1)S(1)}, u32[]{:S(2)}, u32[]{:S(2)}) %collective-permute-start.15) | collective-permute-done | bytes 262176 | tf_op jit(solution)/shard_map/ppermute | solution.py:46
  29.5 0.9 collective-permute-start.13
  30.7 4.5 %collective-permute-done.5 = bf16[8,128,256]{2,1,0:T(8,128)(2,1)S(1)} collective-permute-done((bf16[8,128,256]{2,1,0:T(8,128)(2,1)S(1)}, bf16[8,128,256]{2,1,0:T(8,128)(2,1)S(1)}, u32[]{:S(2)}, u32[]{:S(2)}) %collective-permute-start.5) | collective-permute-done | bytes 524320 | tf_op jit(solution)/shard_map/ppermute | solution.py:46
  35.1 2.5 %collective-permute-start.12 = (bf16[8,128,256]{2,1,0:T(8,128)(2,1)S(1)}, bf16[8,128,256]{2,1,0:T(8,128)(2,1)S(1)}, u32[]{:S(2)}, u32[]{:S(2)}) collective-permute-start(bf16[8,128,256]{2,1,0:T(8,128)(2,1)S(1)} %collective-permute-done.5), channel_id=1, source_target_pairs={{0,4},{4,0},{8,12},{12,8},{16,20},{20,16},{24,28},{28,24},{32,36},... | collective-permute-start | bytes 1572872 | tf_op jit(solution)/shard_map/ppermute | solution.py:46
  37.7 1.1 collective-permute-start.14
  39.2 1.2 %collective-permute-done.14 = bf16[8,128,256]{2,1,0:T(8,128)(2,1)S(1)} collective-permute-done((bf16[8,128,256]{2,1,0:T(8,128)(2,1)S(1)}, bf16[8,128,256]{2,1,0:T(8,128)(2,1)S(1)}, u32[]{:S(2)}, u32[]{:S(2)}) %collective-permute-start.14) | collective-permute-done | bytes 524320 | tf_op jit(solution)/shard_map/ppermute | solution.py:46
  40.4 6.5 %attend_suffix_0.1.a_s = bf16[128,1024]{1,0:T(8,128)(2,1)S(1)} custom-call(s32[68]{0:T(128)S(1)} %concatenate.67.info, bf16[128,1024]{1,0:T(8,128)(2,1)S(1)} %copy-done, bf16[128,128]{1,0:T(8,128)(2,1)S(1)} %copy-done.4, bf16[128,128]{1,0:T(8,128)(2,1)S(1)} %copy-done.5, bf16[16,128,256]{2,1,0:T(8,128)(2,1)S(1)} %constant_dynamic-update-slice_fusion.refs_0_, ...), custom_call_target="tpu_custom_call" | custom-call | tf_op jit(solution)/shard_map/attend_suffix_0/pallas_call | solution.py:151
  47.2 1.6 %collective-permute-start.24 = (bf16[4,2,64,1024]{3,2,1,0:T(8,128)(2,1)S(1)}, bf16[4,2,64,1024]{3,2,1,0:T(8,128)(2,1)S(1)}, u32[]{:S(2)}, u32[]{:S(2)}) collective-permute-start(bf16[4,2,64,1024]{3,2,1,0:T(8,128)(2,1)S(1)} %pad_maximum_fusion.3), channel_id=1, source_target_pairs={{0,16},{4,52},{8,24},{12,60},{16,0},{20,36},{24,8},{28,44},{32,48}... | collective-permute-start | bytes 3145736 | tf_op jit(solution)/shard_map/ppermute | solution.py:46
  48.9 1.4 %collective-permute-start.22 = (bf16[4,2,64,1024]{3,2,1,0:T(8,128)(2,1)S(1)}, bf16[4,2,64,1024]{3,2,1,0:T(8,128)(2,1)S(1)}, u32[]{:S(2)}, u32[]{:S(2)}) collective-permute-start(bf16[4,2,64,1024]{3,2,1,0:T(8,128)(2,1)S(1)} %pad_maximum_fusion.2), channel_id=1, source_target_pairs={{0,64},{4,196},{8,72},{12,204},{16,80},{20,212},{24,88},{28,220},{... | collective-permute-start | bytes 3145736 | tf_op jit(solution)/shard_map/ppermute | solution.py:46
  50.3 5.4 %collective-permute-start.19 = (bf16[128,1024]{1,0:T(8,128)(2,1)S(1)}, bf16[128,1024]{1,0:T(8,128)(2,1)S(1)}, u32[]{:S(2)}, u32[]{:S(2)}) collective-permute-start(bf16[128,1024]{1,0:T(8,128)(2,1)S(1)} %attend_suffix_0.1.a_s), channel_id=1, source_target_pairs={{0,1},{1,0},{2,3},{3,2},{4,7},{5,6},{6,5},{7,4},{8,9},{9,8},{10,11... | collective-permute-start | bytes 786440 | tf_op jit(solution)/shard_map/ppermute | solution.py:51
  55.7 2.5 %attend_prompt_0.1.a_p = bf16[128,1024]{1,0:T(8,128)(2,1)S(1)} custom-call(s32[68]{0:T(128)S(1)} %concatenate.67.info, bf16[128,1024]{1,0:T(8,128)(2,1)S(1)} %copy-done.1, bf16[128,128]{1,0:T(8,128)(2,1)S(1)} %copy-done.2, bf16[128,128]{1,0:T(8,128)(2,1)S(1)} %copy-done.3, bf16[16,128,256]{2,1,0:T(8,128)(2,1)S(1)} %constant_dynamic-update-slice_fusion.refs_0_, ...), custom_call_target="tpu_custom_call" | custom-call | tf_op jit(solution)/shard_map/attend_prompt_0/pallas_call | solution.py:151
  58.2 3.6 %collective-permute-done.19.near_s = bf16[128,1024]{1,0:T(8,128)(2,1)S(1)} collective-permute-done((bf16[128,1024]{1,0:T(8,128)(2,1)S(1)}, bf16[128,1024]{1,0:T(8,128)(2,1)S(1)}, u32[]{:S(2)}, u32[]{:S(2)}) %collective-permute-start.19) | collective-permute-done | bytes 262176 | tf_op jit(solution)/shard_map/ppermute | solution.py:51
  62.1 1.7 %collective-permute-done.22 = bf16[4,2,64,1024]{3,2,1,0:T(8,128)(2,1)S(1)} collective-permute-done((bf16[4,2,64,1024]{3,2,1,0:T(8,128)(2,1)S(1)}, bf16[4,2,64,1024]{3,2,1,0:T(8,128)(2,1)S(1)}, u32[]{:S(2)}, u32[]{:S(2)}) %collective-permute-start.22) | collective-permute-done | bytes 1048608 | tf_op jit(solution)/shard_map/ppermute | solution.py:46
  64.8 3.1 %collective-permute-start.20 = (bf16[3,128,1024]{2,1,0:T(8,128)(2,1)S(1)}, bf16[3,128,1024]{2,1,0:T(8,128)(2,1)S(1)}, u32[]{:S(2)}, u32[]{:S(2)}) collective-permute-start(bf16[3,128,1024]{2,1,0:T(8,128)(2,1)S(1)} %pad_maximum_fusion.4), channel_id=1, source_target_pairs={{0,3},{1,2},{2,1},{3,0},{4,5},{5,4},{6,7},{7,6},{8,11},{9,10},{10,... | collective-permute-start | bytes 2359304 | tf_op jit(solution)/shard_map/ppermute | solution.py:51
  67.8 18.1 %collective-permute-done.20.mixed = bf16[3,128,1024]{2,1,0:T(8,128)(2,1)S(1)} collective-permute-done((bf16[3,128,1024]{2,1,0:T(8,128)(2,1)S(1)}, bf16[3,128,1024]{2,1,0:T(8,128)(2,1)S(1)}, u32[]{:S(2)}, u32[]{:S(2)}) %collective-permute-start.20) | collective-permute-done | bytes 786464 | tf_op jit(solution)/shard_map/ppermute | solution.py:51
  86.1 2.1 %collective-permute-start.21 = (bf16[2,128,1024]{2,1,0:T(8,128)(2,1)S(1)}, bf16[2,128,1024]{2,1,0:T(8,128)(2,1)S(1)}, u32[]{:S(2)}, u32[]{:S(2)}) collective-permute-start(bf16[2,128,1024]{2,1,0:T(8,128)(2,1)S(1)} %pad_maximum_fusion.9), channel_id=1, source_target_pairs={{0,1},{1,0},{2,3},{3,2},{4,7},{5,6},{6,5},{7,4},{8,9},{9,8},{10,11... | collective-permute-start | bytes 1572872 | tf_op jit(solution)/shard_map/ppermute | solution.py:51
  88.2 4.5 %collective-permute-start.26 = (bf16[8,2,64,1024]{3,2,1,0:T(8,128)(2,1)S(1)}, bf16[8,2,64,1024]{3,2,1,0:T(8,128)(2,1)S(1)}, u32[]{:S(2)}, u32[]{:S(2)}) collective-permute-start(bf16[8,2,64,1024]{3,2,1,0:T(8,128)(2,1)S(1)} %pad_maximum_fusion.refs_0_), channel_id=1, source_target_pairs={{0,4},{4,0},{8,12},{12,8},{16,20},{20,16},{24,28},{28,24},{32,36},... | collective-permute-start | bytes 6291464 | tf_op jit(solution)/shard_map/ppermute | solution.py:46
  93.2 9.2 %collective-permute-done.21.far_p = bf16[2,128,1024]{2,1,0:T(8,128)(2,1)S(1)} collective-permute-done((bf16[2,128,1024]{2,1,0:T(8,128)(2,1)S(1)}, bf16[2,128,1024]{2,1,0:T(8,128)(2,1)S(1)}, u32[]{:S(2)}, u32[]{:S(2)}) %collective-permute-start.21) | collective-permute-done | bytes 524320 | tf_op jit(solution)/shard_map/ppermute | solution.py:51
  102.4 4.8 %collective-permute-start.29 = (bf16[8,2,64,1024]{3,2,1,0:T(8,128)(2,1)S(1)}, bf16[8,2,64,1024]{3,2,1,0:T(8,128)(2,1)S(1)}, u32[]{:S(2)}, u32[]{:S(2)}) collective-permute-start(bf16[8,2,64,1024]{3,2,1,0:T(8,128)(2,1)S(1)} %collective-permute-done.25.refs_3_), channel_id=1, source_target_pairs={{0,4},{4,0},{8,12},{12,8},{16,20},{20,16},{24,28},{28,24},{32,36},... | collective-permute-start | bytes 6291464 | tf_op jit(solution)/shard_map/ppermute | solution.py:46
  107.2 3.8 %collective-permute-done.29.refs_7_ = bf16[8,2,64,1024]{3,2,1,0:T(8,128)(2,1)S(1)} collective-permute-done((bf16[8,2,64,1024]{3,2,1,0:T(8,128)(2,1)S(1)}, bf16[8,2,64,1024]{3,2,1,0:T(8,128)(2,1)S(1)}, u32[]{:S(2)}, u32[]{:S(2)}) %collective-permute-start.29) | collective-permute-done | bytes 2097184 | tf_op jit(solution)/shard_map/ppermute | solution.py:46
  111.0 6.2 %project.1 = (bf16[128,2048]{1,0:T(8,128)(2,1)}, bf16[128,2048]{1,0:T(8,128)(2,1)}) custom-call(s32[68]{0:T(128)S(1)} %concatenate.67.info, bf16[128,1024]{1,0:T(8,128)(2,1)S(1)} %attend_prompt_0.1.a_p, bf16[128,1024]{1,0:T(8,128)(2,1)S(1)} %attend_suffix_0.1.a_s, bf16[128,1024]{1,0:T(8,128)(2,1)S(1)} %collective-permute-done.19.near_s, ...), custom_call_target="tpu_custom_call" | custom-call | tf_op jit(solution)/shard_map/project/pallas_call | solution.py:196
  (81 shorter events, 5.0 us)
Async XLA Ops:
  0.6 7.4 %collective-permute-start = (bf16[128,128]{1,0:T(8,128)(2,1)}, bf16[128,128]{1,0:T(8,128)(2,1)S(1)}, u32[]{:S(2)}, u32[]{:S(2)}) collective-permute-start(bf16[128,128]{1,0:T(8,128)(2,1)} %own_k.3), channel_id=1, source_target_pairs={{0,8},{4,12},{8,0},{12,4},{16,24},{20,28},{24,16},{28,20},{32,40},... | collective-permute-start | bytes 98312 | tf_op jit(solution)/shard_map/ppermute | solution.py:46
  3.2 4.9 %collective-permute-start.6 = (bf16[128,128]{1,0:T(8,128)(2,1)}, bf16[128,128]{1,0:T(8,128)(2,1)S(1)}, u32[]{:S(2)}, u32[]{:S(2)}) collective-permute-start(bf16[128,128]{1,0:T(8,128)(2,1)} %own_v.3), channel_id=1, source_target_pairs={{0,8},{4,12},{8,0},{12,4},{16,24},{20,28},{24,16},{28,20},{32,40},... | collective-permute-start | bytes 98312 | tf_op jit(solution)/shard_map/ppermute | solution.py:46
  4.1 8.2 %collective-permute-start.2 = (bf16[1,128,256]{2,1,0:T(8,128)(2,1)S(1)}, bf16[1,128,256]{2,1,0:T(8,128)(2,1)S(1)}, u32[]{:S(2)}, u32[]{:S(2)}) collective-permute-start(bf16[1,128,256]{2,1,0:T(8,128)(2,1)S(1)} %bitcast.27), channel_id=1, source_target_pairs={{0,16},{4,52},{8,24},{12,60},{16,0},{20,36},{24,8},{28,44},{32,48}... | collective-permute-start | bytes 196616 | tf_op jit(solution)/shard_map/ppermute | solution.py:46
  8.1 4.5 %collective-permute-start.7 = (bf16[1,128,256]{2,1,0:T(8,128)(2,1)S(1)}, bf16[1,128,256]{2,1,0:T(8,128)(2,1)S(1)}, u32[]{:S(2)}, u32[]{:S(2)}) collective-permute-start(bf16[1,128,256]{2,1,0:T(8,128)(2,1)S(1)} %maximum_bitcast_fusion.2), channel_id=1, source_target_pairs={{0,64},{4,196},{8,72},{12,204},{16,80},{20,212},{24,88},{28,220},{... | collective-permute-start | bytes 196616 | tf_op jit(solution)/shard_map/ppermute | solution.py:46
  10.9 8.0 %collective-permute-start.1 = (bf16[64,2048]{1,0:T(8,128)(2,1)}, bf16[64,2048]{1,0:T(8,128)(2,1)S(1)}, u32[]{:S(2)}, u32[]{:S(2)}) collective-permute-start(bf16[64,2048]{1,0:T(8,128)(2,1)} %param.17), channel_id=1, source_target_pairs={{0,8},{4,12},{8,0},{12,4},{16,24},{20,28},{24,16},{28,20},{32,40},... | collective-permute-start | bytes 786440 | tf_op jit(solution)/shard_map/ppermute | solution.py:46
  12.3 4.2 %collective-permute-start.3 = (bf16[2,128,256]{2,1,0:T(8,128)(2,1)S(1)}, bf16[2,128,256]{2,1,0:T(8,128)(2,1)S(1)}, u32[]{:S(2)}, u32[]{:S(2)}) collective-permute-start(bf16[2,128,256]{2,1,0:T(8,128)(2,1)S(1)} %pad_maximum_fusion.12), channel_id=1, source_target_pairs={{0,48},{4,20},{8,56},{12,28},{16,32},{20,4},{24,40},{28,12},{32,16... | collective-permute-start | bytes 393224 | tf_op jit(solution)/shard_map/ppermute | solution.py:46
  12.6 7.5 %collective-permute-start.8 = (bf16[2,128,256]{2,1,0:T(8,128)(2,1)S(1)}, bf16[2,128,256]{2,1,0:T(8,128)(2,1)S(1)}, u32[]{:S(2)}, u32[]{:S(2)}) collective-permute-start(bf16[2,128,256]{2,1,0:T(8,128)(2,1)S(1)} %pad_maximum_fusion.13), channel_id=1, source_target_pairs={{0,192},{4,68},{8,200},{12,76},{16,208},{20,84},{24,216},{28,92},{... | collective-permute-start | bytes 393224 | tf_op jit(solution)/shard_map/ppermute | solution.py:46
  20.0 6.5 %collective-permute-start.4 = (bf16[4,128,256]{2,1,0:T(8,128)(2,1)S(1)}, bf16[4,128,256]{2,1,0:T(8,128)(2,1)S(1)}, u32[]{:S(2)}, u32[]{:S(2)}) collective-permute-start(bf16[4,128,256]{2,1,0:T(8,128)(2,1)S(1)} %pad_maximum_fusion.10), channel_id=1, source_target_pairs={{0,64},{4,196},{8,72},{12,204},{16,80},{20,212},{24,88},{28,220},{... | collective-permute-start | bytes 786440 | tf_op jit(solution)/shard_map/ppermute | solution.py:46
  20.2 7.1 %collective-permute-start.9 = (bf16[4,128,256]{2,1,0:T(8,128)(2,1)S(1)}, bf16[4,128,256]{2,1,0:T(8,128)(2,1)S(1)}, u32[]{:S(2)}, u32[]{:S(2)}) collective-permute-start(bf16[4,128,256]{2,1,0:T(8,128)(2,1)S(1)} %pad_maximum_fusion.11), channel_id=1, source_target_pairs={{0,16},{4,52},{8,24},{12,60},{16,0},{20,36},{24,8},{28,44},{32,48}... | collective-permute-start | bytes 786440 | tf_op jit(solution)/shard_map/ppermute | solution.py:46
  20.3 9.2 %collective-permute-start.15 = (bf16[1,2,64,1024]{3,2,1,0:T(8,128)(2,1)S(1)}, bf16[1,2,64,1024]{3,2,1,0:T(8,128)(2,1)S(1)}, u32[]{:S(2)}, u32[]{:S(2)}) collective-permute-start(bf16[1,2,64,1024]{3,2,1,0:T(8,128)(2,1)S(1)} %maximum_bitcast_fusion), channel_id=1, source_target_pairs={{0,16},{4,52},{8,24},{12,60},{16,0},{20,36},{24,8},{28,44},{32,48}... | collective-permute-start | bytes 786440 | tf_op jit(solution)/shard_map/ppermute | solution.py:46
  23.0 7.4 %collective-permute-start.17 = (bf16[1,2,64,1024]{3,2,1,0:T(8,128)(2,1)S(1)}, bf16[1,2,64,1024]{3,2,1,0:T(8,128)(2,1)S(1)}, u32[]{:S(2)}, u32[]{:S(2)}) collective-permute-start(bf16[1,2,64,1024]{3,2,1,0:T(8,128)(2,1)S(1)} %maximum_bitcast_fusion.1), channel_id=1, source_target_pairs={{0,64},{4,196},{8,72},{12,204},{16,80},{20,212},{24,88},{28,220},{... | collective-permute-start | bytes 786440 | tf_op jit(solution)/shard_map/ppermute | solution.py:46
  26.6 11.0 %collective-permute-start.11 = (bf16[8,128,256]{2,1,0:T(8,128)(2,1)S(1)}, bf16[8,128,256]{2,1,0:T(8,128)(2,1)S(1)}, u32[]{:S(2)}, u32[]{:S(2)}) collective-permute-start(bf16[8,128,256]{2,1,0:T(8,128)(2,1)S(1)} %pad_maximum_fusion.5), channel_id=1, source_target_pairs={{0,4},{4,0},{8,12},{12,8},{16,20},{20,16},{24,28},{28,24},{32,36},... | collective-permute-start | bytes 1572872 | tf_op jit(solution)/shard_map/ppermute | solution.py:46
  26.7 8.4 %collective-permute-start.5 = (bf16[8,128,256]{2,1,0:T(8,128)(2,1)S(1)}, bf16[8,128,256]{2,1,0:T(8,128)(2,1)S(1)}, u32[]{:S(2)}, u32[]{:S(2)}) collective-permute-start(bf16[8,128,256]{2,1,0:T(8,128)(2,1)S(1)} %pad_maximum_fusion.5), channel_id=1, source_target_pairs={{0,192},{4,68},{8,200},{12,76},{16,208},{20,84},{24,216},{28,92},{... | collective-permute-start | bytes 1572872 | tf_op jit(solution)/shard_map/ppermute | solution.py:46
  27.4 10.4 %collective-permute-start.10 = (bf16[8,128,256]{2,1,0:T(8,128)(2,1)S(1)}, bf16[8,128,256]{2,1,0:T(8,128)(2,1)S(1)}, u32[]{:S(2)}, u32[]{:S(2)}) collective-permute-start(bf16[8,128,256]{2,1,0:T(8,128)(2,1)S(1)} %pad_maximum_fusion.6), channel_id=1, source_target_pairs={{0,48},{4,20},{8,56},{12,28},{16,32},{20,4},{24,40},{28,12},{32,16... | collective-permute-start | bytes 1572872 | tf_op jit(solution)/shard_map/ppermute | solution.py:46
  29.5 9.4 %collective-permute-start.13 = (bf16[8,128,256]{2,1,0:T(8,128)(2,1)S(1)}, bf16[8,128,256]{2,1,0:T(8,128)(2,1)S(1)}, u32[]{:S(2)}, u32[]{:S(2)}) collective-permute-start(bf16[8,128,256]{2,1,0:T(8,128)(2,1)S(1)} %pad_maximum_fusion.6), channel_id=1, source_target_pairs={{0,4},{4,0},{8,12},{12,8},{16,20},{20,16},{24,28},{28,24},{32,36},... | collective-permute-start | bytes 1572872 | tf_op jit(solution)/shard_map/ppermute | solution.py:46
  30.5 16.6 %collective-permute-start.16 = (bf16[2,2,64,1024]{3,2,1,0:T(8,128)(2,1)S(1)}, bf16[2,2,64,1024]{3,2,1,0:T(8,128)(2,1)S(1)}, u32[]{:S(2)}, u32[]{:S(2)}) collective-permute-start(bf16[2,2,64,1024]{3,2,1,0:T(8,128)(2,1)S(1)} %pad_maximum_fusion.7), channel_id=1, source_target_pairs={{0,48},{4,20},{8,56},{12,28},{16,32},{20,4},{24,40},{28,12},{32,16... | collective-permute-start | bytes 1572872 | tf_op jit(solution)/shard_map/ppermute | solution.py:46
  35.1 4.0 %collective-permute-start.12 = (bf16[8,128,256]{2,1,0:T(8,128)(2,1)S(1)}, bf16[8,128,256]{2,1,0:T(8,128)(2,1)S(1)}, u32[]{:S(2)}, u32[]{:S(2)}) collective-permute-start(bf16[8,128,256]{2,1,0:T(8,128)(2,1)S(1)} %collective-permute-done.5), channel_id=1, source_target_pairs={{0,4},{4,0},{8,12},{12,8},{16,20},{20,16},{24,28},{28,24},{32,36},... | collective-permute-start | bytes 1572872 | tf_op jit(solution)/shard_map/ppermute | solution.py:46
  37.6 9.4 %collective-permute-start.18 = (bf16[2,2,64,1024]{3,2,1,0:T(8,128)(2,1)S(1)}, bf16[2,2,64,1024]{3,2,1,0:T(8,128)(2,1)S(1)}, u32[]{:S(2)}, u32[]{:S(2)}) collective-permute-start(bf16[2,2,64,1024]{3,2,1,0:T(8,128)(2,1)S(1)} %pad_maximum_fusion.8), channel_id=1, source_target_pairs={{0,192},{4,68},{8,200},{12,76},{16,208},{20,84},{24,216},{28,92},{... | collective-permute-start | bytes 1572872 | tf_op jit(solution)/shard_map/ppermute | solution.py:46
  37.7 2.6 %collective-permute-start.14 = (bf16[8,128,256]{2,1,0:T(8,128)(2,1)S(1)}, bf16[8,128,256]{2,1,0:T(8,128)(2,1)S(1)}, u32[]{:S(2)}, u32[]{:S(2)}) collective-permute-start(bf16[8,128,256]{2,1,0:T(8,128)(2,1)S(1)} %collective-permute-done.10), channel_id=1, source_target_pairs={{0,4},{4,0},{8,12},{12,8},{16,20},{20,16},{24,28},{28,24},{32,36},... | collective-permute-start | bytes 1572872 | tf_op jit(solution)/shard_map/ppermute | solution.py:46
  47.0 8.7 %copy-start.1 = (bf16[128,1024]{1,0:T(8,128)(2,1)S(1)}, bf16[128,1024]{1,0:T(8,128)(2,1)}, u32[]{:S(2)}) copy-start(bf16[128,1024]{1,0:T(8,128)(2,1)} %q.2) | copy-start | bytes 786436
  47.0 8.7 %copy-start.2 = (bf16[128,128]{1,0:T(8,128)(2,1)S(1)}, bf16[128,128]{1,0:T(8,128)(2,1)}, u32[]{:S(2)}) copy-start(bf16[128,128]{1,0:T(8,128)(2,1)} %own_k.3) | copy-start | bytes 98308
  47.2 14.9 %collective-permute-start.24 = (bf16[4,2,64,1024]{3,2,1,0:T(8,128)(2,1)S(1)}, bf16[4,2,64,1024]{3,2,1,0:T(8,128)(2,1)S(1)}, u32[]{:S(2)}, u32[]{:S(2)}) collective-permute-start(bf16[4,2,64,1024]{3,2,1,0:T(8,128)(2,1)S(1)} %pad_maximum_fusion.3), channel_id=1, source_target_pairs={{0,16},{4,52},{8,24},{12,60},{16,0},{20,36},{24,8},{28,44},{32,48}... | collective-permute-start | bytes 3145736 | tf_op jit(solution)/shard_map/ppermute | solution.py:46
  48.9 14.9 %collective-permute-start.22 = (bf16[4,2,64,1024]{3,2,1,0:T(8,128)(2,1)S(1)}, bf16[4,2,64,1024]{3,2,1,0:T(8,128)(2,1)S(1)}, u32[]{:S(2)}, u32[]{:S(2)}) collective-permute-start(bf16[4,2,64,1024]{3,2,1,0:T(8,128)(2,1)S(1)} %pad_maximum_fusion.2), channel_id=1, source_target_pairs={{0,64},{4,196},{8,72},{12,204},{16,80},{20,212},{24,88},{28,220},{... | collective-permute-start | bytes 3145736 | tf_op jit(solution)/shard_map/ppermute | solution.py:46
  50.3 11.5 %collective-permute-start.19 = (bf16[128,1024]{1,0:T(8,128)(2,1)S(1)}, bf16[128,1024]{1,0:T(8,128)(2,1)S(1)}, u32[]{:S(2)}, u32[]{:S(2)}) collective-permute-start(bf16[128,1024]{1,0:T(8,128)(2,1)S(1)} %attend_suffix_0.1.a_s), channel_id=1, source_target_pairs={{0,1},{1,0},{2,3},{3,2},{4,7},{5,6},{6,5},{7,4},{8,9},{9,8},{10,11... | collective-permute-start | bytes 786440 | tf_op jit(solution)/shard_map/ppermute | solution.py:51
  64.0 28.7 %collective-permute-start.23 = (bf16[8,2,64,1024]{3,2,1,0:T(8,128)(2,1)S(1)}, bf16[8,2,64,1024]{3,2,1,0:T(8,128)(2,1)S(1)}, u32[]{:S(2)}, u32[]{:S(2)}) collective-permute-start(bf16[8,2,64,1024]{3,2,1,0:T(8,128)(2,1)S(1)} %pad_maximum_fusion.refs_0_), channel_id=1, source_target_pairs={{0,192},{4,68},{8,200},{12,76},{16,208},{20,84},{24,216},{28,92},{... | collective-permute-start | bytes 6291464 | tf_op jit(solution)/shard_map/ppermute | solution.py:46
  64.3 28.9 %collective-permute-start.25 = (bf16[8,2,64,1024]{3,2,1,0:T(8,128)(2,1)S(1)}, bf16[8,2,64,1024]{3,2,1,0:T(8,128)(2,1)S(1)}, u32[]{:S(2)}, u32[]{:S(2)}) collective-permute-start(bf16[8,2,64,1024]{3,2,1,0:T(8,128)(2,1)S(1)} %pad_maximum_fusion.1.refs_2_), channel_id=1, source_target_pairs={{0,48},{4,20},{8,56},{12,28},{16,32},{20,4},{24,40},{28,12},{32,16... | collective-permute-start | bytes 6291464 | tf_op jit(solution)/shard_map/ppermute | solution.py:46
  64.8 21.2 %collective-permute-start.20 = (bf16[3,128,1024]{2,1,0:T(8,128)(2,1)S(1)}, bf16[3,128,1024]{2,1,0:T(8,128)(2,1)S(1)}, u32[]{:S(2)}, u32[]{:S(2)}) collective-permute-start(bf16[3,128,1024]{2,1,0:T(8,128)(2,1)S(1)} %pad_maximum_fusion.4), channel_id=1, source_target_pairs={{0,3},{1,2},{2,1},{3,0},{4,5},{5,4},{6,7},{7,6},{8,11},{9,10},{10,... | collective-permute-start | bytes 2359304 | tf_op jit(solution)/shard_map/ppermute | solution.py:51
  86.1 16.3 %collective-permute-start.21 = (bf16[2,128,1024]{2,1,0:T(8,128)(2,1)S(1)}, bf16[2,128,1024]{2,1,0:T(8,128)(2,1)S(1)}, u32[]{:S(2)}, u32[]{:S(2)}) collective-permute-start(bf16[2,128,1024]{2,1,0:T(8,128)(2,1)S(1)} %pad_maximum_fusion.9), channel_id=1, source_target_pairs={{0,1},{1,0},{2,3},{3,2},{4,7},{5,6},{6,5},{7,4},{8,9},{9,8},{10,11... | collective-permute-start | bytes 1572872 | tf_op jit(solution)/shard_map/ppermute | solution.py:51
  88.2 19.0 %collective-permute-start.26 = (bf16[8,2,64,1024]{3,2,1,0:T(8,128)(2,1)S(1)}, bf16[8,2,64,1024]{3,2,1,0:T(8,128)(2,1)S(1)}, u32[]{:S(2)}, u32[]{:S(2)}) collective-permute-start(bf16[8,2,64,1024]{3,2,1,0:T(8,128)(2,1)S(1)} %pad_maximum_fusion.refs_0_), channel_id=1, source_target_pairs={{0,4},{4,0},{8,12},{12,8},{16,20},{20,16},{24,28},{28,24},{32,36},... | collective-permute-start | bytes 6291464 | tf_op jit(solution)/shard_map/ppermute | solution.py:46
  92.7 14.5 %collective-permute-start.28 = (bf16[8,2,64,1024]{3,2,1,0:T(8,128)(2,1)S(1)}, bf16[8,2,64,1024]{3,2,1,0:T(8,128)(2,1)S(1)}, u32[]{:S(2)}, u32[]{:S(2)}) collective-permute-start(bf16[8,2,64,1024]{3,2,1,0:T(8,128)(2,1)S(1)} %pad_maximum_fusion.1.refs_2_), channel_id=1, source_target_pairs={{0,4},{4,0},{8,12},{12,8},{16,20},{20,16},{24,28},{28,24},{32,36},... | collective-permute-start | bytes 6291464 | tf_op jit(solution)/shard_map/ppermute | solution.py:46
  92.7 14.5 %collective-permute-start.27 = (bf16[8,2,64,1024]{3,2,1,0:T(8,128)(2,1)S(1)}, bf16[8,2,64,1024]{3,2,1,0:T(8,128)(2,1)S(1)}, u32[]{:S(2)}, u32[]{:S(2)}) collective-permute-start(bf16[8,2,64,1024]{3,2,1,0:T(8,128)(2,1)S(1)} %collective-permute-done.23.refs_1_), channel_id=1, source_target_pairs={{0,4},{4,0},{8,12},{12,8},{16,20},{20,16},{24,28},{28,24},{32,36},... | collective-permute-start | bytes 6291464 | tf_op jit(solution)/shard_map/ppermute | solution.py:46
  102.4 8.6 %collective-permute-start.29 = (bf16[8,2,64,1024]{3,2,1,0:T(8,128)(2,1)S(1)}, bf16[8,2,64,1024]{3,2,1,0:T(8,128)(2,1)S(1)}, u32[]{:S(2)}, u32[]{:S(2)}) collective-permute-start(bf16[8,2,64,1024]{3,2,1,0:T(8,128)(2,1)S(1)} %collective-permute-done.25.refs_3_), channel_id=1, source_target_pairs={{0,4},{4,0},{8,12},{12,8},{16,20},{20,16},{24,28},{28,24},{32,36},... | collective-permute-start | bytes 6291464 | tf_op jit(solution)/shard_map/ppermute | solution.py:46
  (4 other events, 13.1 us)

commit v5 on v4

--- a/solution.py
+++ b/solution.py
@@ -229,9 +229,11 @@
     came_mate = [swap(a, 1) for a in came]
     blocks = [*join(kv, came), *join(kv_mate, came_mate)]
 
-    a_s = attend(False, 0, 8, info, suffix_q, suffix_k, suffix_v, blocks)
-    a_s, prompt_q, *w_came = lax.optimization_barrier((a_s, prompt_q, *w_came))
-
+    a_s = attend(False, 0, 4, info, suffix_q, suffix_k, suffix_v, blocks)
+    a_s, suffix_q, prompt_q, *w_came = lax.optimization_barrier(
+        (a_s, suffix_q, prompt_q, *w_came))
+    more = attend(False, 4, 4, info, suffix_q, suffix_k, suffix_v, blocks)
+    a_s = jnp.concatenate([a_s, more], axis=1)
     w = join(w, w_came)
     w_3 = gather_step(w, 2)
     near_s = swap_tensor(a_s, (1, 3))

time: 117 us -> 121 us (1.034); the launches traced: 117 us -> 119 us
  starting transfers between devices: 45 us -> 50.8 us
  waiting for transfers between devices: 51.2 us -> 46.9 us
    ppermute x27, starting transfers between devices: 34.4 us -> 41.4 us  [swap(): return lax.ppermute(x, 'sample', [(s, s ^ masks[s & 1]) for s in range(64)])]
    ppermute x3, waiting for transfers between devices: 31 us -> 26.6 us  [swap_tensor(): return lax.ppermute(x, ('sample', 'tensor'), pairs)]
    ppermute x3, starting transfers between devices: 10.6 us -> 9.38 us  [swap_tensor(): return lax.ppermute(x, ('sample', 'tensor'), pairs)]
    pallas_call x2 -> x3, Pallas kernels: 9 us -> 9.52 us  [attend(): pl.pallas_call(functools.partial(attend_kernel, is_prompt, first, count),...]
  transfers between devices with their start and end apart: 30 -> 30, of which waited for: 14 -> 13; matrix products, arithmetic and copies ran while one was open for 3% -> 3% of each run, Pallas kernels for 8% -> 8%
where the time goes in v5:
time: 121 us; the launch traced here: 119 us
  starting transfers between devices  50.8 us (42%)
  waiting for transfers between devices  46.9 us (39%)
  Pallas kernels  15.7 us (13%)
  between operations  2.38 us (2%)
  other arithmetic  1.98 us (2%)
  local copies, waits for them, and re-layouts  1.43 us (1%)
    ppermute x27, starting transfers between devices, swap(): return lax.ppermute(x, 'sample', [(s, s ^ masks[s & 1]) for s in range(64)])  41.4 us
    ppermute x3, waiting for transfers between devices, swap_tensor(): return lax.ppermute(x, ('sample', 'tensor'), pairs)  26.6 us
    ppermute x27, waiting for transfers between devices, swap(): return lax.ppermute(x, 'sample', [(s, s ^ masks[s & 1]) for s in range(64)])  20.3 us
    pallas_call x3, Pallas kernels, attend(): pl.pallas_call(functools.partial(attend_kernel, is_prompt, first, count),...  9.52 us
    ppermute x3, starting transfers between devices, swap_tensor(): return lax.ppermute(x, ('sample', 'tensor'), pairs)  9.38 us
    pallas_call x1, Pallas kernels, project(): pl.pallas_call(project_kernel, out_shape=[jax.ShapeDtypeStruct((ROWS, 204...  6.18 us
  transfers between devices with their start and end apart: 30, of which 13 were waited for; matrix products, arithmetic and copies ran while one was open for 3% of the time, Pallas kernels for 8%

profile of v5, /device:TPU:1, one launch (start us, length us, event | category | flops | bytes accessed | tf_op | source)
XLA Modules:
  0.0 119.2 jit_solution(8680953110316856594)
XLA Ops:
  0.6 2.6 %collective-permute-start = (bf16[128,128]{1,0:T(8,128)(2,1)}, bf16[128,128]{1,0:T(8,128)(2,1)S(1)}, u32[]{:S(2)}, u32[]{:S(2)}) collective-permute-start(bf16[128,128]{1,0:T(8,128)(2,1)} %own_k.5), channel_id=1, source_target_pairs={{0,8},{4,12},{8,0},{12,4},{16,24},{20,28},{24,16},{28,20},{32,40},... | collective-permute-start | bytes 98312 | tf_op jit(solution)/shard_map/ppermute | solution.py:46
  4.1 2.6 %collective-permute-start.2 = (bf16[1,128,256]{2,1,0:T(8,128)(2,1)S(1)}, bf16[1,128,256]{2,1,0:T(8,128)(2,1)S(1)}, u32[]{:S(2)}, u32[]{:S(2)}) collective-permute-start(bf16[1,128,256]{2,1,0:T(8,128)(2,1)S(1)} %bitcast.27), channel_id=1, source_target_pairs={{0,16},{4,52},{8,24},{12,60},{16,0},{20,36},{24,8},{28,44},{32,48}... | collective-permute-start | bytes 196616 | tf_op jit(solution)/shard_map/ppermute | solution.py:46
  8.1 2.8 %collective-permute-start.7 = (bf16[1,128,256]{2,1,0:T(8,128)(2,1)S(1)}, bf16[1,128,256]{2,1,0:T(8,128)(2,1)S(1)}, u32[]{:S(2)}, u32[]{:S(2)}) collective-permute-start(bf16[1,128,256]{2,1,0:T(8,128)(2,1)S(1)} %maximum_bitcast_fusion.2), channel_id=1, source_target_pairs={{0,64},{4,196},{8,72},{12,204},{16,80},{20,212},{24,88},{28,220},{... | collective-permute-start | bytes 196616 | tf_op jit(solution)/shard_map/ppermute | solution.py:46
  10.9 1.4 %collective-permute-start.1 = (bf16[64,2048]{1,0:T(8,128)(2,1)}, bf16[64,2048]{1,0:T(8,128)(2,1)S(1)}, u32[]{:S(2)}, u32[]{:S(2)}) collective-permute-start(bf16[64,2048]{1,0:T(8,128)(2,1)} %param.17), channel_id=1, source_target_pairs={{0,8},{4,12},{8,0},{12,4},{16,24},{20,28},{24,16},{28,20},{32,40},... | collective-permute-start | bytes 786440 | tf_op jit(solution)/shard_map/ppermute | solution.py:46
  13.0 3.5 %collective-permute-done.3 = bf16[2,128,256]{2,1,0:T(8,128)(2,1)S(1)} collective-permute-done((bf16[2,128,256]{2,1,0:T(8,128)(2,1)S(1)}, bf16[2,128,256]{2,1,0:T(8,128)(2,1)S(1)}, u32[]{:S(2)}, u32[]{:S(2)}) %collective-permute-start.3) | collective-permute-done | bytes 131104 | tf_op jit(solution)/shard_map/ppermute | solution.py:46
  16.6 2.4 %collective-permute-done.1 = bf16[64,2048]{1,0:T(8,128)(2,1)S(1)} collective-permute-done((bf16[64,2048]{1,0:T(8,128)(2,1)}, bf16[64,2048]{1,0:T(8,128)(2,1)S(1)}, u32[]{:S(2)}, u32[]{:S(2)}) %collective-permute-start.1) | collective-permute-done | bytes 262176 | tf_op jit(solution)/shard_map/ppermute | solution.py:46
  18.9 1.0 slice_bitcast_fusion.1
  20.3 2.7 %collective-permute-start.15 = (bf16[1,2,64,1024]{3,2,1,0:T(8,128)(2,1)S(1)}, bf16[1,2,64,1024]{3,2,1,0:T(8,128)(2,1)S(1)}, u32[]{:S(2)}, u32[]{:S(2)}) collective-permute-start(bf16[1,2,64,1024]{3,2,1,0:T(8,128)(2,1)S(1)} %maximum_bitcast_fusion), channel_id=1, source_target_pairs={{0,16},{4,52},{8,24},{12,60},{16,0},{20,36},{24,8},{28,44},{32,48}... | collective-permute-start | bytes 786440 | tf_op jit(solution)/shard_map/ppermute | solution.py:46
  23.0 2.7 %collective-permute-start.17 = (bf16[1,2,64,1024]{3,2,1,0:T(8,128)(2,1)S(1)}, bf16[1,2,64,1024]{3,2,1,0:T(8,128)(2,1)S(1)}, u32[]{:S(2)}, u32[]{:S(2)}) collective-permute-start(bf16[1,2,64,1024]{3,2,1,0:T(8,128)(2,1)S(1)} %maximum_bitcast_fusion.1), channel_id=1, source_target_pairs={{0,64},{4,196},{8,72},{12,204},{16,80},{20,212},{24,88},{28,220},{... | collective-permute-start | bytes 786440 | tf_op jit(solution)/shard_map/ppermute | solution.py:46
  25.7 0.9 collective-permute-done.4
  27.7 1.8 %collective-permute-done.15 = bf16[1,2,64,1024]{3,2,1,0:T(8,128)(2,1)S(1)} collective-permute-done((bf16[1,2,64,1024]{3,2,1,0:T(8,128)(2,1)S(1)}, bf16[1,2,64,1024]{3,2,1,0:T(8,128)(2,1)S(1)}, u32[]{:S(2)}, u32[]{:S(2)}) %collective-permute-start.15) | collective-permute-done | bytes 262176 | tf_op jit(solution)/shard_map/ppermute | solution.py:46
  29.5 0.9 collective-permute-start.13
  30.7 4.5 %collective-permute-done.5 = bf16[8,128,256]{2,1,0:T(8,128)(2,1)S(1)} collective-permute-done((bf16[8,128,256]{2,1,0:T(8,128)(2,1)S(1)}, bf16[8,128,256]{2,1,0:T(8,128)(2,1)S(1)}, u32[]{:S(2)}, u32[]{:S(2)}) %collective-permute-start.5) | collective-permute-done | bytes 524320 | tf_op jit(solution)/shard_map/ppermute | solution.py:46
  35.1 2.5 %collective-permute-start.12 = (bf16[8,128,256]{2,1,0:T(8,128)(2,1)S(1)}, bf16[8,128,256]{2,1,0:T(8,128)(2,1)S(1)}, u32[]{:S(2)}, u32[]{:S(2)}) collective-permute-start(bf16[8,128,256]{2,1,0:T(8,128)(2,1)S(1)} %collective-permute-done.5), channel_id=1, source_target_pairs={{0,4},{4,0},{8,12},{12,8},{16,20},{20,16},{24,28},{28,24},{32,36},... | collective-permute-start | bytes 1572872 | tf_op jit(solution)/shard_map/ppermute | solution.py:46
  37.7 1.1 collective-permute-start.14
  39.2 1.2 %collective-permute-done.14 = bf16[8,128,256]{2,1,0:T(8,128)(2,1)S(1)} collective-permute-done((bf16[8,128,256]{2,1,0:T(8,128)(2,1)S(1)}, bf16[8,128,256]{2,1,0:T(8,128)(2,1)S(1)}, u32[]{:S(2)}, u32[]{:S(2)}) %collective-permute-start.14) | collective-permute-done | bytes 524320 | tf_op jit(solution)/shard_map/ppermute | solution.py:46
  40.4 3.5 %attend_suffix_0.1 = bf16[128,512]{1,0:T(8,128)(2,1)S(1)} custom-call(s32[68]{0:T(128)S(1)} %concatenate.70.info, bf16[128,1024]{1,0:T(8,128)(2,1)S(1)} %copy-done, bf16[128,128]{1,0:T(8,128)(2,1)S(1)} %copy-done.2, bf16[128,128]{1,0:T(8,128)(2,1)S(1)} %copy-done.3, bf16[16,128,256]{2,1,0:T(8,128)(2,1)S(1)} %constant_dynamic-update-slice_fusion.refs_0_, ...), custom_call_target="tpu_custom_call" | custom-call | tf_op jit(solution)/shard_map/attend_suffix_0/pallas_call | solution.py:151
  44.0 2.0 %collective-permute-done.18 = bf16[2,2,64,1024]{3,2,1,0:T(8,128)(2,1)S(1)} collective-permute-done((bf16[2,2,64,1024]{3,2,1,0:T(8,128)(2,1)S(1)}, bf16[2,2,64,1024]{3,2,1,0:T(8,128)(2,1)S(1)}, u32[]{:S(2)}, u32[]{:S(2)}) %collective-permute-start.18) | collective-permute-done | bytes 524320 | tf_op jit(solution)/shard_map/ppermute | solution.py:46
  46.1 1.1 collective-permute-start.24
  47.4 1.4 %collective-permute-start.22 = (bf16[4,2,64,1024]{3,2,1,0:T(8,128)(2,1)S(1)}, bf16[4,2,64,1024]{3,2,1,0:T(8,128)(2,1)S(1)}, u32[]{:S(2)}, u32[]{:S(2)}) collective-permute-start(bf16[4,2,64,1024]{3,2,1,0:T(8,128)(2,1)S(1)} %pad_maximum_fusion.2), channel_id=1, source_target_pairs={{0,64},{4,196},{8,72},{12,204},{16,80},{20,212},{24,88},{28,220},{... | collective-permute-start | bytes 3145736 | tf_op jit(solution)/shard_map/ppermute | solution.py:46
  48.8 3.5 %attend_suffix_4.1 = bf16[128,512]{1,0:T(8,128)(2,1)S(1)} custom-call(s32[68]{0:T(128)S(1)} %concatenate.70.info, bf16[128,1024]{1,0:T(8,128)(2,1)S(1)} %copy-done, bf16[128,128]{1,0:T(8,128)(2,1)S(1)} %copy-done.2, bf16[128,128]{1,0:T(8,128)(2,1)S(1)} %copy-done.3, bf16[16,128,256]{2,1,0:T(8,128)(2,1)S(1)} %constant_dynamic-update-slice_fusion.refs_0_, ...), custom_call_target="tpu_custom_call" | custom-call | tf_op jit(solution)/shard_map/attend_suffix_4/pallas_call | solution.py:151
  52.4 5.3 %collective-permute-start.19 = (bf16[128,1024]{1,0:T(8,128)(2,1)S(1)}, bf16[128,1024]{1,0:T(8,128)(2,1)S(1)}, u32[]{:S(2)}, u32[]{:S(2)}) collective-permute-start(bf16[128,1024]{1,0:T(8,128)(2,1)S(1)} %pad_maximum_fusion.12.a_s), channel_id=1, source_target_pairs={{0,1},{1,0},{2,3},{3,2},{4,7},{5,6},{6,5},{7,4},{8,9},{9,8},{10,11... | collective-permute-start | bytes 786440 | tf_op jit(solution)/shard_map/ppermute | solution.py:51
  57.7 2.5 %attend_prompt_0.1.a_p = bf16[128,1024]{1,0:T(8,128)(2,1)S(1)} custom-call(s32[68]{0:T(128)S(1)} %concatenate.70.info, bf16[128,1024]{1,0:T(8,128)(2,1)S(1)} %copy-done.1, bf16[128,128]{1,0:T(8,128)(2,1)S(1)} %copy-done.4, bf16[128,128]{1,0:T(8,128)(2,1)S(1)} %copy-done.5, bf16[16,128,256]{2,1,0:T(8,128)(2,1)S(1)} %constant_dynamic-update-slice_fusion.refs_0_, ...), custom_call_target="tpu_custom_call" | custom-call | tf_op jit(solution)/shard_map/attend_prompt_0/pallas_call | solution.py:151
  60.1 3.7 %collective-permute-done.19.near_s = bf16[128,1024]{1,0:T(8,128)(2,1)S(1)} collective-permute-done((bf16[128,1024]{1,0:T(8,128)(2,1)S(1)}, bf16[128,1024]{1,0:T(8,128)(2,1)S(1)}, u32[]{:S(2)}, u32[]{:S(2)}) %collective-permute-start.19) | collective-permute-done | bytes 262176 | tf_op jit(solution)/shard_map/ppermute | solution.py:51
  64.8 1.9 %collective-permute-start.20 = (bf16[3,128,1024]{2,1,0:T(8,128)(2,1)S(1)}, bf16[3,128,1024]{2,1,0:T(8,128)(2,1)S(1)}, u32[]{:S(2)}, u32[]{:S(2)}) collective-permute-start(bf16[3,128,1024]{2,1,0:T(8,128)(2,1)S(1)} %pad_maximum_fusion.4), channel_id=1, source_target_pairs={{0,3},{1,2},{2,1},{3,0},{4,5},{5,4},{6,7},{7,6},{8,11},{9,10},{10,... | collective-permute-start | bytes 2359304 | tf_op jit(solution)/shard_map/ppermute | solution.py:51
  66.6 18.7 %collective-permute-done.20.mixed = bf16[3,128,1024]{2,1,0:T(8,128)(2,1)S(1)} collective-permute-done((bf16[3,128,1024]{2,1,0:T(8,128)(2,1)S(1)}, bf16[3,128,1024]{2,1,0:T(8,128)(2,1)S(1)}, u32[]{:S(2)}, u32[]{:S(2)}) %collective-permute-start.20) | collective-permute-done | bytes 786464 | tf_op jit(solution)/shard_map/ppermute | solution.py:51
  85.4 2.2 %collective-permute-start.21 = (bf16[2,128,1024]{2,1,0:T(8,128)(2,1)S(1)}, bf16[2,128,1024]{2,1,0:T(8,128)(2,1)S(1)}, u32[]{:S(2)}, u32[]{:S(2)}) collective-permute-start(bf16[2,128,1024]{2,1,0:T(8,128)(2,1)S(1)} %pad_maximum_fusion.9), channel_id=1, source_target_pairs={{0,1},{1,0},{2,3},{3,2},{4,7},{5,6},{6,5},{7,4},{8,9},{9,8},{10,11... | collective-permute-start | bytes 1572872 | tf_op jit(solution)/shard_map/ppermute | solution.py:51
  87.6 9.5 %collective-permute-start.26 = (bf16[8,2,64,1024]{3,2,1,0:T(8,128)(2,1)S(1)}, bf16[8,2,64,1024]{3,2,1,0:T(8,128)(2,1)S(1)}, u32[]{:S(2)}, u32[]{:S(2)}) collective-permute-start(bf16[8,2,64,1024]{3,2,1,0:T(8,128)(2,1)S(1)} %pad_maximum_fusion.refs_0_), channel_id=1, source_target_pairs={{0,4},{4,0},{8,12},{12,8},{16,20},{20,16},{24,28},{28,24},{32,36},... | collective-permute-start | bytes 6291464 | tf_op jit(solution)/shard_map/ppermute | solution.py:46
  97.6 4.2 %collective-permute-done.21.far_p = bf16[2,128,1024]{2,1,0:T(8,128)(2,1)S(1)} collective-permute-done((bf16[2,128,1024]{2,1,0:T(8,128)(2,1)S(1)}, bf16[2,128,1024]{2,1,0:T(8,128)(2,1)S(1)}, u32[]{:S(2)}, u32[]{:S(2)}) %collective-permute-start.21) | collective-permute-done | bytes 524320 | tf_op jit(solution)/shard_map/ppermute | solution.py:51
  101.8 7.4 %collective-permute-start.29 = (bf16[8,2,64,1024]{3,2,1,0:T(8,128)(2,1)S(1)}, bf16[8,2,64,1024]{3,2,1,0:T(8,128)(2,1)S(1)}, u32[]{:S(2)}, u32[]{:S(2)}) collective-permute-start(bf16[8,2,64,1024]{3,2,1,0:T(8,128)(2,1)S(1)} %collective-permute-done.25.refs_3_), channel_id=1, source_target_pairs={{0,4},{4,0},{8,12},{12,8},{16,20},{20,16},{24,28},{28,24},{32,36},... | collective-permute-start | bytes 6291464 | tf_op jit(solution)/shard_map/ppermute | solution.py:46
  109.2 3.8 %collective-permute-done.29.refs_7_ = bf16[8,2,64,1024]{3,2,1,0:T(8,128)(2,1)S(1)} collective-permute-done((bf16[8,2,64,1024]{3,2,1,0:T(8,128)(2,1)S(1)}, bf16[8,2,64,1024]{3,2,1,0:T(8,128)(2,1)S(1)}, u32[]{:S(2)}, u32[]{:S(2)}) %collective-permute-start.29) | collective-permute-done | bytes 2097184 | tf_op jit(solution)/shard_map/ppermute | solution.py:46
  113.0 6.2 %project.1 = (bf16[128,2048]{1,0:T(8,128)(2,1)}, bf16[128,2048]{1,0:T(8,128)(2,1)}) custom-call(s32[68]{0:T(128)S(1)} %concatenate.70.info, bf16[128,1024]{1,0:T(8,128)(2,1)S(1)} %attend_prompt_0.1.a_p, bf16[128,1024]{1,0:T(8,128)(2,1)S(1)} %pad_maximum_fusion.12.a_s, bf16[128,1024]{1,0:T(8,128)(2,1)S(1)} %collective-permute-done.19.near_s, ...), custom_call_target="tpu_custom_call" | custom-call | tf_op jit(solution)/shard_map/project/pallas_call | solution.py:196
  (83 shorter events, 5.6 us)
Async XLA Ops:
  0.6 7.4 %collective-permute-start = (bf16[128,128]{1,0:T(8,128)(2,1)}, bf16[128,128]{1,0:T(8,128)(2,1)S(1)}, u32[]{:S(2)}, u32[]{:S(2)}) collective-permute-start(bf16[128,128]{1,0:T(8,128)(2,1)} %own_k.5), channel_id=1, source_target_pairs={{0,8},{4,12},{8,0},{12,4},{16,24},{20,28},{24,16},{28,20},{32,40},... | collective-permute-start | bytes 98312 | tf_op jit(solution)/shard_map/ppermute | solution.py:46
  3.2 4.9 %collective-permute-start.6 = (bf16[128,128]{1,0:T(8,128)(2,1)}, bf16[128,128]{1,0:T(8,128)(2,1)S(1)}, u32[]{:S(2)}, u32[]{:S(2)}) collective-permute-start(bf16[128,128]{1,0:T(8,128)(2,1)} %own_v.5), channel_id=1, source_target_pairs={{0,8},{4,12},{8,0},{12,4},{16,24},{20,28},{24,16},{28,20},{32,40},... | collective-permute-start | bytes 98312 | tf_op jit(solution)/shard_map/ppermute | solution.py:46
  4.1 8.2 %collective-permute-start.2 = (bf16[1,128,256]{2,1,0:T(8,128)(2,1)S(1)}, bf16[1,128,256]{2,1,0:T(8,128)(2,1)S(1)}, u32[]{:S(2)}, u32[]{:S(2)}) collective-permute-start(bf16[1,128,256]{2,1,0:T(8,128)(2,1)S(1)} %bitcast.27), channel_id=1, source_target_pairs={{0,16},{4,52},{8,24},{12,60},{16,0},{20,36},{24,8},{28,44},{32,48}... | collective-permute-start | bytes 196616 | tf_op jit(solution)/shard_map/ppermute | solution.py:46
  8.1 4.5 %collective-permute-start.7 = (bf16[1,128,256]{2,1,0:T(8,128)(2,1)S(1)}, bf16[1,128,256]{2,1,0:T(8,128)(2,1)S(1)}, u32[]{:S(2)}, u32[]{:S(2)}) collective-permute-start(bf16[1,128,256]{2,1,0:T(8,128)(2,1)S(1)} %maximum_bitcast_fusion.2), channel_id=1, source_target_pairs={{0,64},{4,196},{8,72},{12,204},{16,80},{20,212},{24,88},{28,220},{... | collective-permute-start | bytes 196616 | tf_op jit(solution)/shard_map/ppermute | solution.py:46
  10.9 8.0 %collective-permute-start.1 = (bf16[64,2048]{1,0:T(8,128)(2,1)}, bf16[64,2048]{1,0:T(8,128)(2,1)S(1)}, u32[]{:S(2)}, u32[]{:S(2)}) collective-permute-start(bf16[64,2048]{1,0:T(8,128)(2,1)} %param.17), channel_id=1, source_target_pairs={{0,8},{4,12},{8,0},{12,4},{16,24},{20,28},{24,16},{28,20},{32,40},... | collective-permute-start | bytes 786440 | tf_op jit(solution)/shard_map/ppermute | solution.py:46
  12.3 4.2 %collective-permute-start.3 = (bf16[2,128,256]{2,1,0:T(8,128)(2,1)S(1)}, bf16[2,128,256]{2,1,0:T(8,128)(2,1)S(1)}, u32[]{:S(2)}, u32[]{:S(2)}) collective-permute-start(bf16[2,128,256]{2,1,0:T(8,128)(2,1)S(1)} %pad_maximum_fusion.13), channel_id=1, source_target_pairs={{0,48},{4,20},{8,56},{12,28},{16,32},{20,4},{24,40},{28,12},{32,16... | collective-permute-start | bytes 393224 | tf_op jit(solution)/shard_map/ppermute | solution.py:46
  12.6 7.5 %collective-permute-start.8 = (bf16[2,128,256]{2,1,0:T(8,128)(2,1)S(1)}, bf16[2,128,256]{2,1,0:T(8,128)(2,1)S(1)}, u32[]{:S(2)}, u32[]{:S(2)}) collective-permute-start(bf16[2,128,256]{2,1,0:T(8,128)(2,1)S(1)} %pad_maximum_fusion.14), channel_id=1, source_target_pairs={{0,192},{4,68},{8,200},{12,76},{16,208},{20,84},{24,216},{28,92},{... | collective-permute-start | bytes 393224 | tf_op jit(solution)/shard_map/ppermute | solution.py:46
  20.0 6.5 %collective-permute-start.4 = (bf16[4,128,256]{2,1,0:T(8,128)(2,1)S(1)}, bf16[4,128,256]{2,1,0:T(8,128)(2,1)S(1)}, u32[]{:S(2)}, u32[]{:S(2)}) collective-permute-start(bf16[4,128,256]{2,1,0:T(8,128)(2,1)S(1)} %pad_maximum_fusion.10), channel_id=1, source_target_pairs={{0,64},{4,196},{8,72},{12,204},{16,80},{20,212},{24,88},{28,220},{... | collective-permute-start | bytes 786440 | tf_op jit(solution)/shard_map/ppermute | solution.py:46
  20.2 7.1 %collective-permute-start.9 = (bf16[4,128,256]{2,1,0:T(8,128)(2,1)S(1)}, bf16[4,128,256]{2,1,0:T(8,128)(2,1)S(1)}, u32[]{:S(2)}, u32[]{:S(2)}) collective-permute-start(bf16[4,128,256]{2,1,0:T(8,128)(2,1)S(1)} %pad_maximum_fusion.11), channel_id=1, source_target_pairs={{0,16},{4,52},{8,24},{12,60},{16,0},{20,36},{24,8},{28,44},{32,48}... | collective-permute-start | bytes 786440 | tf_op jit(solution)/shard_map/ppermute | solution.py:46
  20.3 9.2 %collective-permute-start.15 = (bf16[1,2,64,1024]{3,2,1,0:T(8,128)(2,1)S(1)}, bf16[1,2,64,1024]{3,2,1,0:T(8,128)(2,1)S(1)}, u32[]{:S(2)}, u32[]{:S(2)}) collective-permute-start(bf16[1,2,64,1024]{3,2,1,0:T(8,128)(2,1)S(1)} %maximum_bitcast_fusion), channel_id=1, source_target_pairs={{0,16},{4,52},{8,24},{12,60},{16,0},{20,36},{24,8},{28,44},{32,48}... | collective-permute-start | bytes 786440 | tf_op jit(solution)/shard_map/ppermute | solution.py:46
  23.0 7.4 %collective-permute-start.17 = (bf16[1,2,64,1024]{3,2,1,0:T(8,128)(2,1)S(1)}, bf16[1,2,64,1024]{3,2,1,0:T(8,128)(2,1)S(1)}, u32[]{:S(2)}, u32[]{:S(2)}) collective-permute-start(bf16[1,2,64,1024]{3,2,1,0:T(8,128)(2,1)S(1)} %maximum_bitcast_fusion.1), channel_id=1, source_target_pairs={{0,64},{4,196},{8,72},{12,204},{16,80},{20,212},{24,88},{28,220},{... | collective-permute-start | bytes 786440 | tf_op jit(solution)/shard_map/ppermute | solution.py:46
  26.6 11.0 %collective-permute-start.11 = (bf16[8,128,256]{2,1,0:T(8,128)(2,1)S(1)}, bf16[8,128,256]{2,1,0:T(8,128)(2,1)S(1)}, u32[]{:S(2)}, u32[]{:S(2)}) collective-permute-start(bf16[8,128,256]{2,1,0:T(8,128)(2,1)S(1)} %pad_maximum_fusion.5), channel_id=1, source_target_pairs={{0,4},{4,0},{8,12},{12,8},{16,20},{20,16},{24,28},{28,24},{32,36},... | collective-permute-start | bytes 1572872 | tf_op jit(solution)/shard_map/ppermute | solution.py:46
  26.7 8.4 %collective-permute-start.5 = (bf16[8,128,256]{2,1,0:T(8,128)(2,1)S(1)}, bf16[8,128,256]{2,1,0:T(8,128)(2,1)S(1)}, u32[]{:S(2)}, u32[]{:S(2)}) collective-permute-start(bf16[8,128,256]{2,1,0:T(8,128)(2,1)S(1)} %pad_maximum_fusion.5), channel_id=1, source_target_pairs={{0,192},{4,68},{8,200},{12,76},{16,208},{20,84},{24,216},{28,92},{... | collective-permute-start | bytes 1572872 | tf_op jit(solution)/shard_map/ppermute | solution.py:46
  27.4 10.4 %collective-permute-start.10 = (bf16[8,128,256]{2,1,0:T(8,128)(2,1)S(1)}, bf16[8,128,256]{2,1,0:T(8,128)(2,1)S(1)}, u32[]{:S(2)}, u32[]{:S(2)}) collective-permute-start(bf16[8,128,256]{2,1,0:T(8,128)(2,1)S(1)} %pad_maximum_fusion.6), channel_id=1, source_target_pairs={{0,48},{4,20},{8,56},{12,28},{16,32},{20,4},{24,40},{28,12},{32,16... | collective-permute-start | bytes 1572872 | tf_op jit(solution)/shard_map/ppermute | solution.py:46
  29.5 9.4 %collective-permute-start.13 = (bf16[8,128,256]{2,1,0:T(8,128)(2,1)S(1)}, bf16[8,128,256]{2,1,0:T(8,128)(2,1)S(1)}, u32[]{:S(2)}, u32[]{:S(2)}) collective-permute-start(bf16[8,128,256]{2,1,0:T(8,128)(2,1)S(1)} %pad_maximum_fusion.6), channel_id=1, source_target_pairs={{0,4},{4,0},{8,12},{12,8},{16,20},{20,16},{24,28},{28,24},{32,36},... | collective-permute-start | bytes 1572872 | tf_op jit(solution)/shard_map/ppermute | solution.py:46
  30.5 13.5 %collective-permute-start.16 = (bf16[2,2,64,1024]{3,2,1,0:T(8,128)(2,1)S(1)}, bf16[2,2,64,1024]{3,2,1,0:T(8,128)(2,1)S(1)}, u32[]{:S(2)}, u32[]{:S(2)}) collective-permute-start(bf16[2,2,64,1024]{3,2,1,0:T(8,128)(2,1)S(1)} %pad_maximum_fusion.7), channel_id=1, source_target_pairs={{0,48},{4,20},{8,56},{12,28},{16,32},{20,4},{24,40},{28,12},{32,16... | collective-permute-start | bytes 1572872 | tf_op jit(solution)/shard_map/ppermute | solution.py:46
  35.1 4.0 %collective-permute-start.12 = (bf16[8,128,256]{2,1,0:T(8,128)(2,1)S(1)}, bf16[8,128,256]{2,1,0:T(8,128)(2,1)S(1)}, u32[]{:S(2)}, u32[]{:S(2)}) collective-permute-start(bf16[8,128,256]{2,1,0:T(8,128)(2,1)S(1)} %collective-permute-done.5), channel_id=1, source_target_pairs={{0,4},{4,0},{8,12},{12,8},{16,20},{20,16},{24,28},{28,24},{32,36},... | collective-permute-start | bytes 1572872 | tf_op jit(solution)/shard_map/ppermute | solution.py:46
  37.6 8.4 %collective-permute-start.18 = (bf16[2,2,64,1024]{3,2,1,0:T(8,128)(2,1)S(1)}, bf16[2,2,64,1024]{3,2,1,0:T(8,128)(2,1)S(1)}, u32[]{:S(2)}, u32[]{:S(2)}) collective-permute-start(bf16[2,2,64,1024]{3,2,1,0:T(8,128)(2,1)S(1)} %pad_maximum_fusion.8), channel_id=1, source_target_pairs={{0,192},{4,68},{8,200},{12,76},{16,208},{20,84},{24,216},{28,92},{... | collective-permute-start | bytes 1572872 | tf_op jit(solution)/shard_map/ppermute | solution.py:46
  37.7 2.6 %collective-permute-start.14 = (bf16[8,128,256]{2,1,0:T(8,128)(2,1)S(1)}, bf16[8,128,256]{2,1,0:T(8,128)(2,1)S(1)}, u32[]{:S(2)}, u32[]{:S(2)}) collective-permute-start(bf16[8,128,256]{2,1,0:T(8,128)(2,1)S(1)} %collective-permute-done.10), channel_id=1, source_target_pairs={{0,4},{4,0},{8,12},{12,8},{16,20},{20,16},{24,28},{28,24},{32,36},... | collective-permute-start | bytes 1572872 | tf_op jit(solution)/shard_map/ppermute | solution.py:46
  46.1 17.7 %collective-permute-start.24 = (bf16[4,2,64,1024]{3,2,1,0:T(8,128)(2,1)S(1)}, bf16[4,2,64,1024]{3,2,1,0:T(8,128)(2,1)S(1)}, u32[]{:S(2)}, u32[]{:S(2)}) collective-permute-start(bf16[4,2,64,1024]{3,2,1,0:T(8,128)(2,1)S(1)} %pad_maximum_fusion.3), channel_id=1, source_target_pairs={{0,16},{4,52},{8,24},{12,60},{16,0},{20,36},{24,8},{28,44},{32,48}... | collective-permute-start | bytes 3145736 | tf_op jit(solution)/shard_map/ppermute | solution.py:46
  47.3 10.3 %copy-start.1 = (bf16[128,1024]{1,0:T(8,128)(2,1)S(1)}, bf16[128,1024]{1,0:T(8,128)(2,1)}, u32[]{:S(2)}) copy-start(bf16[128,1024]{1,0:T(8,128)(2,1)} %q.3) | copy-start | bytes 786436
  47.3 10.3 %copy-start.4 = (bf16[128,128]{1,0:T(8,128)(2,1)S(1)}, bf16[128,128]{1,0:T(8,128)(2,1)}, u32[]{:S(2)}) copy-start(bf16[128,128]{1,0:T(8,128)(2,1)} %own_k.5) | copy-start | bytes 98308
  47.4 16.4 %collective-permute-start.22 = (bf16[4,2,64,1024]{3,2,1,0:T(8,128)(2,1)S(1)}, bf16[4,2,64,1024]{3,2,1,0:T(8,128)(2,1)S(1)}, u32[]{:S(2)}, u32[]{:S(2)}) collective-permute-start(bf16[4,2,64,1024]{3,2,1,0:T(8,128)(2,1)S(1)} %pad_maximum_fusion.2), channel_id=1, source_target_pairs={{0,64},{4,196},{8,72},{12,204},{16,80},{20,212},{24,88},{28,220},{... | collective-permute-start | bytes 3145736 | tf_op jit(solution)/shard_map/ppermute | solution.py:46
  52.4 11.4 %collective-permute-start.19 = (bf16[128,1024]{1,0:T(8,128)(2,1)S(1)}, bf16[128,1024]{1,0:T(8,128)(2,1)S(1)}, u32[]{:S(2)}, u32[]{:S(2)}) collective-permute-start(bf16[128,1024]{1,0:T(8,128)(2,1)S(1)} %pad_maximum_fusion.12.a_s), channel_id=1, source_target_pairs={{0,1},{1,0},{2,3},{3,2},{4,7},{5,6},{6,5},{7,4},{8,9},{9,8},{10,11... | collective-permute-start | bytes 786440 | tf_op jit(solution)/shard_map/ppermute | solution.py:51
  64.0 33.2 %collective-permute-start.23 = (bf16[8,2,64,1024]{3,2,1,0:T(8,128)(2,1)S(1)}, bf16[8,2,64,1024]{3,2,1,0:T(8,128)(2,1)S(1)}, u32[]{:S(2)}, u32[]{:S(2)}) collective-permute-start(bf16[8,2,64,1024]{3,2,1,0:T(8,128)(2,1)S(1)} %pad_maximum_fusion.refs_0_), channel_id=1, source_target_pairs={{0,192},{4,68},{8,200},{12,76},{16,208},{20,84},{24,216},{28,92},{... | collective-permute-start | bytes 6291464 | tf_op jit(solution)/shard_map/ppermute | solution.py:46
  64.3 33.3 %collective-permute-start.25 = (bf16[8,2,64,1024]{3,2,1,0:T(8,128)(2,1)S(1)}, bf16[8,2,64,1024]{3,2,1,0:T(8,128)(2,1)S(1)}, u32[]{:S(2)}, u32[]{:S(2)}) collective-permute-start(bf16[8,2,64,1024]{3,2,1,0:T(8,128)(2,1)S(1)} %pad_maximum_fusion.1.refs_2_), channel_id=1, source_target_pairs={{0,48},{4,20},{8,56},{12,28},{16,32},{20,4},{24,40},{28,12},{32,16... | collective-permute-start | bytes 6291464 | tf_op jit(solution)/shard_map/ppermute | solution.py:46
  64.8 20.6 %collective-permute-start.20 = (bf16[3,128,1024]{2,1,0:T(8,128)(2,1)S(1)}, bf16[3,128,1024]{2,1,0:T(8,128)(2,1)S(1)}, u32[]{:S(2)}, u32[]{:S(2)}) collective-permute-start(bf16[3,128,1024]{2,1,0:T(8,128)(2,1)S(1)} %pad_maximum_fusion.4), channel_id=1, source_target_pairs={{0,3},{1,2},{2,1},{3,0},{4,5},{5,4},{6,7},{7,6},{8,11},{9,10},{10,... | collective-permute-start | bytes 2359304 | tf_op jit(solution)/shard_map/ppermute | solution.py:51
  85.4 16.4 %collective-permute-start.21 = (bf16[2,128,1024]{2,1,0:T(8,128)(2,1)S(1)}, bf16[2,128,1024]{2,1,0:T(8,128)(2,1)S(1)}, u32[]{:S(2)}, u32[]{:S(2)}) collective-permute-start(bf16[2,128,1024]{2,1,0:T(8,128)(2,1)S(1)} %pad_maximum_fusion.9), channel_id=1, source_target_pairs={{0,1},{1,0},{2,3},{3,2},{4,7},{5,6},{6,5},{7,4},{8,9},{9,8},{10,11... | collective-permute-start | bytes 1572872 | tf_op jit(solution)/shard_map/ppermute | solution.py:51
  87.6 21.6 %collective-permute-start.26 = (bf16[8,2,64,1024]{3,2,1,0:T(8,128)(2,1)S(1)}, bf16[8,2,64,1024]{3,2,1,0:T(8,128)(2,1)S(1)}, u32[]{:S(2)}, u32[]{:S(2)}) collective-permute-start(bf16[8,2,64,1024]{3,2,1,0:T(8,128)(2,1)S(1)} %pad_maximum_fusion.refs_0_), channel_id=1, source_target_pairs={{0,4},{4,0},{8,12},{12,8},{16,20},{20,16},{24,28},{28,24},{32,36},... | collective-permute-start | bytes 6291464 | tf_op jit(solution)/shard_map/ppermute | solution.py:46
  97.1 12.1 %collective-permute-start.28 = (bf16[8,2,64,1024]{3,2,1,0:T(8,128)(2,1)S(1)}, bf16[8,2,64,1024]{3,2,1,0:T(8,128)(2,1)S(1)}, u32[]{:S(2)}, u32[]{:S(2)}) collective-permute-start(bf16[8,2,64,1024]{3,2,1,0:T(8,128)(2,1)S(1)} %pad_maximum_fusion.1.refs_2_), channel_id=1, source_target_pairs={{0,4},{4,0},{8,12},{12,8},{16,20},{20,16},{24,28},{28,24},{32,36},... | collective-permute-start | bytes 6291464 | tf_op jit(solution)/shard_map/ppermute | solution.py:46
  97.2 12.0 %collective-permute-start.27 = (bf16[8,2,64,1024]{3,2,1,0:T(8,128)(2,1)S(1)}, bf16[8,2,64,1024]{3,2,1,0:T(8,128)(2,1)S(1)}, u32[]{:S(2)}, u32[]{:S(2)}) collective-permute-start(bf16[8,2,64,1024]{3,2,1,0:T(8,128)(2,1)S(1)} %collective-permute-done.23.refs_1_), channel_id=1, source_target_pairs={{0,4},{4,0},{8,12},{12,8},{16,20},{20,16},{24,28},{28,24},{32,36},... | collective-permute-start | bytes 6291464 | tf_op jit(solution)/shard_map/ppermute | solution.py:46
  101.8 11.2 %collective-permute-start.29 = (bf16[8,2,64,1024]{3,2,1,0:T(8,128)(2,1)S(1)}, bf16[8,2,64,1024]{3,2,1,0:T(8,128)(2,1)S(1)}, u32[]{:S(2)}, u32[]{:S(2)}) collective-permute-start(bf16[8,2,64,1024]{3,2,1,0:T(8,128)(2,1)S(1)} %collective-permute-done.25.refs_3_), channel_id=1, source_target_pairs={{0,4},{4,0},{8,12},{12,8},{16,20},{20,16},{24,28},{28,24},{32,36},... | collective-permute-start | bytes 6291464 | tf_op jit(solution)/shard_map/ppermute | solution.py:46
  (4 other events, 14.8 us)
